TPU v7x, 32 devices: a whole 2x2x4 slice. The times are simulated.
32 devices in a mesh: dp: 2 (over y), pipe: 2 (over x), tensor: 8 (over z, core).
Axes of the slice: x: 2, y: 2, z: 4, core: 2. Of those that a mesh axis runs over, the one named last changes fastest.
Arguments:
- queries: bfloat16 [2, 2, 256, 4096], P('pipe', 'dp', None, 'tensor'), may hold values from -120 to 120
- grad_out: bfloat16 [2, 2, 256, 4096], P('pipe', 'dp', None, 'tensor'), may hold values from -6 to 6
- past_keys: bfloat16 [2, 2, 512, 256], P('pipe', 'dp', 'tensor'), may hold values from -6 to 6
- past_values: bfloat16 [2, 2, 512, 256], P('pipe', 'dp', 'tensor'), may hold values from -6 to 6
- span_keys: bfloat16 [2, 2, 256, 256], P('pipe', 'dp', 'tensor'), may hold values from -6 to 6
- span_values: bfloat16 [2, 2, 256, 256], P('pipe', 'dp', 'tensor'), may hold values from -6 to 6
- normed: bfloat16 [2, 2, 256, 16384], P('pipe', 'dp', None, 'tensor'), may hold values from -6 to 6
- key_weight: bfloat16 [2, 16384, 256], P('pipe', 'tensor'), may hold values from -0.046875 to 0.046875
- value_weight: bfloat16 [2, 16384, 256], P('pipe', 'tensor'), may hold values from -0.046875 to 0.046875
- offsets: int32 [2, 2], P('pipe', 'dp'), may hold values from 256 to 512, as said below
Outputs:
- queries_grad: bfloat16 [2, 2, 256, 4096], P('pipe', 'dp', None, 'tensor')
- past_key_grad: float32 [2, 2, 512, 256], P('pipe', 'dp', 'tensor')
- past_value_grad: float32 [2, 2, 512, 256], P('pipe', 'dp', 'tensor')
- key_weight_grad: float32 [2, 16384, 256], P('pipe', 'tensor', 'dp')
- value_weight_grad: float32 [2, 16384, 256], P('pipe', 'tensor', 'dp')
- section_grad: bfloat16 [2, 2, 256, 16384], P('pipe', 'dp', None, 'tensor')
Inputs may be any that keep to these rules, and one draw needn't show every extreme that they name: `offsets`: the number of earlier tokens of that section's sequence that the block's queries see; 256 and 512 are each reached by some section and sequence.
All inputs are finite; a program needn't handle non-finite values.
Results may differ from a plain program's by a relative error of at most 0.014.
The roundings to bfloat16 on the way count: a program that leaves them out, or rounds other values in their place, can miss the bound.
Values may be sent and summed in bfloat16 or wider, within the bound.
No kernel may reach another device: no remote copies, remote signals or barrier semaphores. Data moves between devices by JAX's collectives and lax.ppermute only.
A program may use at most 64 MiB of HBM per device.

v0:
```python
import jax
import jax.numpy as jnp
from jax import lax
from jax.sharding import PartitionSpec as P

HD = 128
GROUP = 16
QH_DEV = 4
SPAN = 256
PAST = 512


rope_base = 500000.0
neg_large = -1e30


def from_behind(block, axis, distance):
    devices = range(lax.axis_size(axis))
    route = [(i - distance, i) for i in devices if i - distance in devices]
    return lax.ppermute(block, axis, route)


def rotary_tables(positions):
    half_dim = HD // 2
    freq_index = jnp.arange(half_dim, dtype=jnp.float32)
    inverse_freq = rope_base ** (-2.0 * freq_index / HD)
    angles = positions.astype(jnp.float32)[:, None] * inverse_freq[None, :]
    return (jnp.cos(angles), jnp.sin(angles))


def rotate_rows(values, cosine_table, sine_table):
    half_dim = values.shape[1] // 2
    first_half = values[:, :half_dim]
    second_half = values[:, half_dim:]
    return jnp.concatenate(
        [
            first_half * cosine_table - second_half * sine_table,
            second_half * cosine_table + first_half * sine_table,
        ],
        axis=1,
    )


def unrotate_rows(gradient, cosine_table, sine_table):
    half_dim = gradient.shape[1] // 2
    first_grad = gradient[:, :half_dim]
    second_grad = gradient[:, half_dim:]
    return jnp.concatenate(
        [
            first_grad * cosine_table + second_grad * sine_table,
            second_grad * cosine_table - first_grad * sine_table,
        ],
        axis=1,
    )


def visible_keys(offset):
    row_index = lax.broadcasted_iota(jnp.int32, (SPAN, PAST + SPAN), 0)
    column_index = lax.broadcasted_iota(jnp.int32, (SPAN, PAST + SPAN), 1)
    return jnp.where(column_index < PAST, column_index < offset, column_index - PAST <= row_index)


def attend_backward(query_rows, grad_rows, key_rows, value_rows, offset):
    positions = jnp.concatenate(
        [jnp.arange(PAST, dtype=jnp.int32), offset + jnp.arange(SPAN, dtype=jnp.int32)]
    )
    cosine_table, sine_table = rotary_tables(positions)
    key_turned = rotate_rows(key_rows.astype(jnp.float32), cosine_table, sine_table).astype(
        jnp.bfloat16
    )
    scale_factor = HD ** (-0.5)
    scores = (
        jnp.einsum("thd,kd->htk", query_rows, key_turned, preferred_element_type=jnp.float32)
        * scale_factor
    )
    visible = visible_keys(offset)[None]
    masked = jnp.where(visible, scores, neg_large)
    row_max = jnp.max(masked, axis=-1, keepdims=True)
    exponent = jnp.where(visible, jnp.exp(masked - row_max), 0.0)
    attention = exponent / jnp.sum(exponent, axis=-1, keepdims=True)
    attention_bf = attention.astype(jnp.bfloat16)
    attended = jnp.einsum(
        "htk,kd->thd", attention_bf, value_rows, preferred_element_type=jnp.float32
    )
    row_delta = jnp.sum(grad_rows.astype(jnp.float32) * attended, axis=-1)
    grad_attention = jnp.einsum(
        "thd,kd->htk", grad_rows, value_rows, preferred_element_type=jnp.float32
    )
    grad_scores = (attention * (grad_attention - row_delta.T[:, :, None])).astype(jnp.bfloat16)
    query_grad = (
        jnp.einsum("htk,kd->thd", grad_scores, key_turned, preferred_element_type=jnp.float32)
        * scale_factor
    ).astype(jnp.bfloat16)
    key_grad = (
        jnp.einsum("htk,thd->kd", grad_scores, query_rows, preferred_element_type=jnp.float32)
        * scale_factor
    )
    value_grad = jnp.einsum(
        "htk,thd->kd", attention_bf, grad_rows, preferred_element_type=jnp.float32
    )
    key_grad = unrotate_rows(key_grad, cosine_table, sine_table)
    return (query_grad, key_grad, value_grad)


def spread_heads(rows_in, copies):
    row_count = rows_in.shape[0]
    head_count = rows_in.shape[1] // HD
    expanded = jnp.broadcast_to(
        rows_in.reshape(row_count, head_count, 1, HD), (row_count, head_count, copies, HD)
    )
    return expanded.reshape(row_count, head_count * copies * HD)


def merge_copies(received, copies):
    row_count = received.shape[0]
    head_count = received.shape[1] // (copies * HD)
    return (
        received.reshape(row_count, head_count, copies, HD)
        .sum(axis=2)
        .reshape(row_count, head_count * HD)
    )


def on_device(
    queries,
    grad_out,
    past_keys,
    past_values,
    span_keys,
    span_values,
    normed,
    key_weight,
    value_weight,
    offsets,
):
    copies = GROUP // QH_DEV
    past_key_rows = past_keys[0, 0]
    past_value_rows = past_values[0, 0]
    span_key_rows = span_keys[0, 0]
    span_value_rows = span_values[0, 0]
    heads_only = (
        lax.all_to_all(
            spread_heads(past_key_rows, copies), "tensor", split_axis=1, concat_axis=0, tiled=True
        ),
        lax.all_to_all(
            spread_heads(past_value_rows, copies), "tensor", split_axis=1, concat_axis=0, tiled=True
        ),
        lax.all_to_all(
            spread_heads(span_key_rows, copies), "tensor", split_axis=1, concat_axis=0, tiled=True
        ),
        lax.all_to_all(
            spread_heads(span_value_rows, copies), "tensor", split_axis=1, concat_axis=0, tiled=True
        ),
    )
    key_rows = jnp.concatenate([heads_only[0], heads_only[2]], axis=0)
    value_rows = jnp.concatenate([heads_only[1], heads_only[3]], axis=0)
    query_rows = queries[0, 0].reshape(SPAN, QH_DEV, HD)
    grad_rows = grad_out[0, 0].reshape(SPAN, QH_DEV, HD)
    offset = offsets[0, 0]
    query_grad, key_grad, value_grad = attend_backward(
        query_rows, grad_rows, key_rows, value_rows, offset
    )
    returned = (
        lax.all_to_all(key_grad[:PAST], "tensor", split_axis=0, concat_axis=1, tiled=True),
        lax.all_to_all(value_grad[:PAST], "tensor", split_axis=0, concat_axis=1, tiled=True),
        lax.all_to_all(key_grad[PAST:], "tensor", split_axis=0, concat_axis=1, tiled=True),
        lax.all_to_all(value_grad[PAST:], "tensor", split_axis=0, concat_axis=1, tiled=True),
    )
    past_key_grad, past_value_grad, span_key_sum, span_value_sum = [
        merge_copies(received, copies) for received in returned
    ]
    span_key_bf = span_key_sum.astype(jnp.bfloat16)
    span_value_bf = span_value_sum.astype(jnp.bfloat16)
    normed_rows = normed[0, 0]
    key_local = key_weight[0]
    value_local = value_weight[0]
    key_piece = lax.all_gather(span_key_bf, "tensor", axis=0, tiled=True)
    value_piece = lax.all_gather(span_value_bf, "tensor", axis=0, tiled=True)
    key_total = jnp.einsum("rf,rc->fc", normed_rows, key_piece, preferred_element_type=jnp.float32)
    value_total = jnp.einsum(
        "rf,rc->fc", normed_rows, value_piece, preferred_element_type=jnp.float32
    )
    piece_grad = jnp.einsum("rc,fc->rf", key_piece, key_local, preferred_element_type=jnp.float32)
    piece_grad = piece_grad + jnp.einsum(
        "rc,fc->rf", value_piece, value_local, preferred_element_type=jnp.float32
    )
    input_grad = piece_grad
    key_total, value_total, input_grad = (key_total, value_total, input_grad)
    key_share, value_share = (
        lax.psum_scatter(
            key_total.astype(jnp.bfloat16), "dp", scatter_dimension=1, tiled=True
        ).astype(jnp.float32),
        lax.psum_scatter(
            value_total.astype(jnp.bfloat16), "dp", scatter_dimension=1, tiled=True
        ).astype(jnp.float32),
    )
    passed = from_behind(input_grad.astype(jnp.bfloat16), "pipe", -1)
    return (
        query_grad.reshape(1, 1, SPAN, QH_DEV * HD),
        past_key_grad[None, None],
        past_value_grad[None, None],
        key_share[None],
        value_share[None],
        passed[None, None],
    )


def solution(mesh):
    return jax.shard_map(
        on_device,
        mesh=mesh,
        in_specs=(
            P("pipe", "dp", None, "tensor"),
            P("pipe", "dp", None, "tensor"),
            P("pipe", "dp", "tensor", None),
            P("pipe", "dp", "tensor", None),
            P("pipe", "dp", "tensor", None),
            P("pipe", "dp", "tensor", None),
            P("pipe", "dp", None, "tensor"),
            P("pipe", "tensor", None),
            P("pipe", "tensor", None),
            P("pipe", "dp"),
        ),
        out_specs=(
            P("pipe", "dp", None, "tensor"),
            P("pipe", "dp", "tensor", None),
            P("pipe", "dp", "tensor", None),
            P("pipe", "tensor", "dp"),
            P("pipe", "tensor", "dp"),
            P("pipe", "dp", None, "tensor"),
        ),
        check_vma=False,
    )
```

profile of v0, /device:TPU:0, one launch (start us, length us, event | category | flops | bytes accessed | tf_op | source)
XLA Modules:
  0.0 157.0 jit_solution(5637116586846061793)
XLA Ops:
  8.6 6.3 %all-to-all-start.1 = ((bf16[32,8,128]{2,0,1:T(8,128)(2,1)}), bf16[32,8,128]{2,0,1:T(8,128)(2,1)S(1)}, u32[]{:S(2)}, u32[]{:S(2)}) async-start(bf16[32,8,128]{2,0,1:T(8,128)(2,1)} %bitcast.3), calls=%async_computation.1 | async-start | bytes 131072 | tf_op jit(solution)/shard_map/all_to_all | solution.py:148
  19.1 1.8 %all-to-all-done.1 = bf16[32,8,128]{2,0,1:T(8,128)(2,1)S(1)} async-done(((bf16[32,8,128]{2,0,1:T(8,128)(2,1)}), bf16[32,8,128]{2,0,1:T(8,128)(2,1)S(1)}, u32[]{:S(2)}, u32[]{:S(2)}) %all-to-all-start.1) | async-done | bytes 65568 | tf_op jit(solution)/shard_map/all_to_all | solution.py:148
  21.6 3.4 %all-to-all-start = ((bf16[64,8,128]{2,0,1:T(8,128)(2,1)}), bf16[64,8,128]{2,0,1:T(8,128)(2,1)S(1)}, u32[]{:S(2)}, u32[]{:S(2)}) async-start(bf16[64,8,128]{2,0,1:T(8,128)(2,1)} %bitcast), calls=%async_computation | async-start | bytes 262144 | tf_op jit(solution)/shard_map/all_to_all | solution.py:142
  26.8 4.9 %all-to-all-done = bf16[64,8,128]{2,0,1:T(8,128)(2,1)S(1)} async-done(((bf16[64,8,128]{2,0,1:T(8,128)(2,1)}), bf16[64,8,128]{2,0,1:T(8,128)(2,1)S(1)}, u32[]{:S(2)}, u32[]{:S(2)}) %all-to-all-start) | async-done | bytes 131104 | tf_op jit(solution)/shard_map/all_to_all | solution.py:142
  32.3 3.4 %all-to-all-start.3 = ((bf16[32,8,128]{2,0,1:T(8,128)(2,1)}), bf16[32,8,128]{2,0,1:T(8,128)(2,1)S(1)}, u32[]{:S(2)}, u32[]{:S(2)}) async-start(bf16[32,8,128]{2,0,1:T(8,128)(2,1)} %bitcast.13), calls=%async_computation.3 | async-start | bytes 131072 | tf_op jit(solution)/shard_map/all_to_all | solution.py:151
  35.7 1.8 %fusion.30 = (bf16[768,64]{1,0:T(8,128)(2,1)S(1)}, bf16[768,64]{1,0:T(8,128)(2,1)S(1)}) fusion(f32[768,128]{1,0:T(8,128)S(1)} %maximum_convert_fusion, f32[64]{0:T(128)S(1)} %multiply_power_fusion, f32[768]{0:T(1024)S(1)} %add_convert_fusion), kind=kLoop, calls=%fused_computation.46 | loop fusion | flops 442368 | bytes 593152 | tf_op jit(solution)/shard_map/convert.2
  37.6 3.2 %fusion.42 = (f32[4,256]{1,0:T(4,128)S(1)}, f32[4,256,768]{1,2,0:T(8,128)}) fusion(pred[256,768]{0,1:T(8,128)(4,1)S(1)} %fusion.20, bf16[256,4,128]{0,2,1:T(8,128)(2,1)S(1)} %bitcast.151, bf16[768,64]{1,0:T(8,128)(2,1)S(1)} %get-tuple-element.27, bf16[768,64]{1,0:T(8,128)(2,1)S(1)} %get-tuple-element.26), kind=kOutput, calls=%fused_computation.77 | convolution fusion | flops 205652736 | bytes 3805184 | tf_op jit(solution)/shard_map/sub | solution.py:79
  42.2 4.2 %all-to-all-start.2 = ((bf16[64,8,128]{2,0,1:T(8,128)(2,1)}), bf16[64,8,128]{2,0,1:T(8,128)(2,1)S(1)}, u32[]{:S(2)}, u32[]{:S(2)}) async-start(bf16[64,8,128]{2,0,1:T(8,128)(2,1)} %bitcast.10), calls=%async_computation.2 | async-start | bytes 262144 | tf_op jit(solution)/shard_map/all_to_all | solution.py:145
  46.5 2.1 %fusion.10 = bf16[4,256,768]{1,2,0:T(8,128)(2,1)S(1)} fusion(f32[4,256,768]{1,2,0:T(8,128)} %get-tuple-element.29, f32[4,256]{1,0:T(4,128)S(1)} %get-tuple-element.28), kind=kLoop, calls=%fused_computation.17 | loop fusion | flops 1572864 | bytes 4722688 | tf_op jit(solution)/shard_map/convert_element_type | solution.py:81
  48.6 4.6 %all-to-all-done.2 = bf16[64,8,128]{2,0,1:T(8,128)(2,1)S(1)} async-done(((bf16[64,8,128]{2,0,1:T(8,128)(2,1)}), bf16[64,8,128]{2,0,1:T(8,128)(2,1)S(1)}, u32[]{:S(2)}, u32[]{:S(2)}) %all-to-all-start.2) | async-done | bytes 131104 | tf_op jit(solution)/shard_map/all_to_all | solution.py:145
  53.6 2.4 %fusion.2 = bf16[4,256,768]{1,2,0:T(8,128)(2,1)S(1)} fusion(bf16[256,4,128]{0,2,1:T(8,128)(2,1)S(1)} %bitcast.149, f32[4,256]{1,0:T(4,128)S(1)} %bitcast.164, f32[4,256,768]{1,2,0:T(8,128)} %get-tuple-element.29, f32[4,256]{1,0:T(4,128)S(1)} %get-tuple-element.28, bf16[256,128]{1,0:T(8,128)(2,1)S(1)} %bitcast.163, bf16[512,128]{1,0:T(8,128)(2,1)S(1)} %bitcast.157), kind=kOutput, calls=%fused_computation.3 | convolution fusion | flops 204865536 | bytes 5185536 | tf_op jit(solution)/shard_map/thd,kd->htk/dot_general | solution.py:86
  56.7 1.7 %fusion.34 = (f32[768,64]{1,0:T(8,128)S(1)}, f32[768,64]{1,0:T(8,128)S(1)}) fusion(f32[768,128]{1,0:T(8,128)S(1)} %fusion.13, f32[64]{0:T(128)S(1)} %multiply_power_fusion, f32[768]{0:T(1024)S(1)} %add_convert_fusion), kind=kLoop, calls=%fused_computation.50 | loop fusion | flops 344064 | bytes 789760 | tf_op jit(solution)/shard_map/sub | solution.py:51
  58.5 9.3 %all_to_all.140 = f32[8,32,128]{2,1,0:T(8,128)S(1)} all-to-all(f32[8,32,128]{2,1,0:T(8,128)S(1)} %bitcast.158), channel_id=1, replica_groups=mesh['dp'=2,'pipe'=2,'tensor'=8] {'tensor'}, dimensions={0} | all-to-all | bytes 262144 | tf_op jit(solution)/shard_map/all_to_all | solution.py:166
  67.8 14.0 %all_gather.6 = bf16[256,256]{1,0:T(8,128)(2,1)S(1)} all-gather(bf16[32,256]{1,0:T(8,128)(2,1)S(1)} %copy_bitcast_fusion.1), channel_id=1, replica_groups=mesh['dp'=2,'pipe'=2,'tensor'=8] {'tensor'}, dimensions={0}, use_global_device_ids=true | all-gather | bytes 147456 | tf_op jit(solution)/shard_map/all_gather | solution.py:177
  83.3 1.5 convolution_bitcast_fusion.1
  85.6 9.4 %all_to_all.141 = f32[8,32,128]{2,1,0:T(8,128)S(1)} all-to-all(f32[8,32,128]{2,1,0:T(8,128)S(1)} %bitcast.159), channel_id=1, replica_groups=mesh['dp'=2,'pipe'=2,'tensor'=8] {'tensor'}, dimensions={0} | all-to-all | bytes 262144 | tf_op jit(solution)/shard_map/all_to_all | solution.py:167
  95.1 14.0 %all_gather.7 = bf16[256,256]{1,0:T(8,128)(2,1)S(1)} all-gather(bf16[32,256]{1,0:T(8,128)(2,1)S(1)} %copy_bitcast_fusion), channel_id=1, replica_groups=mesh['dp'=2,'pipe'=2,'tensor'=8] {'tensor'}, dimensions={0}, use_global_device_ids=true | all-gather | bytes 147456 | tf_op jit(solution)/shard_map/all_gather | solution.py:178
  111.7 1.5 fusion.3
  115.3 4.1 %all-to-all-start.5 = ((f32[8,64,128]{2,1,0:T(8,128)}), f32[8,64,128]{2,1,0:T(8,128)}, u32[]{:S(2)}, u32[]{:S(2)}) async-start(f32[8,64,128]{2,1,0:T(8,128)} %bitcast.154), calls=%async_computation.5 | async-start | bytes 524288 | tf_op jit(solution)/shard_map/all_to_all | solution.py:165
  120.2 8.9 %all-to-all-done.5 = f32[8,64,128]{2,1,0:T(8,128)} async-done(((f32[8,64,128]{2,1,0:T(8,128)}), f32[8,64,128]{2,1,0:T(8,128)}, u32[]{:S(2)}, u32[]{:S(2)}) %all-to-all-start.5) | async-done | bytes 262176 | tf_op jit(solution)/shard_map/all_to_all | solution.py:165
  129.1 3.4 %all-to-all-start.4 = ((f32[8,64,128]{2,1,0:T(8,128)}), f32[8,64,128]{2,1,0:T(8,128)S(1)}, u32[]{:S(2)}, u32[]{:S(2)}) async-start(f32[8,64,128]{2,1,0:T(8,128)} %bitcast.155), calls=%async_computation.4 | async-start | bytes 524288 | tf_op jit(solution)/shard_map/all_to_all | solution.py:164
  132.6 1.6 fusion.12
  136.7 5.5 %all-to-all-done.4 = f32[8,64,128]{2,1,0:T(8,128)S(1)} async-done(((f32[8,64,128]{2,1,0:T(8,128)}), f32[8,64,128]{2,1,0:T(8,128)S(1)}, u32[]{:S(2)}, u32[]{:S(2)}) %all-to-all-start.4) | async-done | bytes 262176 | tf_op jit(solution)/shard_map/all_to_all | solution.py:164
  147.9 2.3 %copy.92 = bf16[1,1,256,2048]{3,2,1,0:T(8,128)(2,1)} copy(bf16[1,1,256,2048]{3,2,1,0:T(8,128)(2,1)} %bitcast.45) | data formatting | bytes 2097152
  (75 shorter events, 26.8 us)
Async XLA Ops:
  7.2 74.6 %copy-start = (bf16[1,1,256,2048]{3,2,1,0:T(8,128)(2,1)S(1)}, bf16[1,1,256,2048]{3,2,1,0:T(8,128)(2,1)}, u32[]{:S(2)}) copy-start(bf16[1,1,256,2048]{3,2,1,0:T(8,128)(2,1)} %param.16) | copy-start | bytes 3145732
  8.6 12.2 %all-to-all-start.1 = ((bf16[32,8,128]{2,0,1:T(8,128)(2,1)}), bf16[32,8,128]{2,0,1:T(8,128)(2,1)S(1)}, u32[]{:S(2)}, u32[]{:S(2)}) async-start(bf16[32,8,128]{2,0,1:T(8,128)(2,1)} %bitcast.3), calls=%async_computation.1 | async-start | bytes 131072 | tf_op jit(solution)/shard_map/all_to_all | solution.py:148
  21.6 10.1 %all-to-all-start = ((bf16[64,8,128]{2,0,1:T(8,128)(2,1)}), bf16[64,8,128]{2,0,1:T(8,128)(2,1)S(1)}, u32[]{:S(2)}, u32[]{:S(2)}) async-start(bf16[64,8,128]{2,0,1:T(8,128)(2,1)} %bitcast), calls=%async_computation | async-start | bytes 262144 | tf_op jit(solution)/shard_map/all_to_all | solution.py:142
  26.0 27.6 %copy-start.3 = (bf16[1,1,256,512]{2,3,1,0:T(8,128)(2,1)}, bf16[1,1,256,512]{2,3,1,0:T(8,128)(2,1)S(1)}, u32[]{:S(2)}) copy-start(bf16[1,1,256,512]{2,3,1,0:T(8,128)(2,1)S(1)} %copy.57) | copy-start | bytes 786436
  32.3 9.2 %all-to-all-start.3 = ((bf16[32,8,128]{2,0,1:T(8,128)(2,1)}), bf16[32,8,128]{2,0,1:T(8,128)(2,1)S(1)}, u32[]{:S(2)}, u32[]{:S(2)}) async-start(bf16[32,8,128]{2,0,1:T(8,128)(2,1)} %bitcast.13), calls=%async_computation.3 | async-start | bytes 131072 | tf_op jit(solution)/shard_map/all_to_all | solution.py:151
  37.5 3.2 %copy-start.8 = (bf16[768,64]{1,0:T(8,128)(2,1)}, bf16[768,64]{1,0:T(8,128)(2,1)S(1)}, u32[]{:S(2)}) copy-start(bf16[768,64]{1,0:T(8,128)(2,1)S(1)} %get-tuple-element.26) | copy-start | bytes 294916
  37.5 3.2 %copy-start.9 = (bf16[768,64]{1,0:T(8,128)(2,1)}, bf16[768,64]{1,0:T(8,128)(2,1)S(1)}, u32[]{:S(2)}) copy-start(bf16[768,64]{1,0:T(8,128)(2,1)S(1)} %get-tuple-element.27) | copy-start | bytes 294916
  42.2 11.0 %all-to-all-start.2 = ((bf16[64,8,128]{2,0,1:T(8,128)(2,1)}), bf16[64,8,128]{2,0,1:T(8,128)(2,1)S(1)}, u32[]{:S(2)}, u32[]{:S(2)}) async-start(bf16[64,8,128]{2,0,1:T(8,128)(2,1)} %bitcast.10), calls=%async_computation.2 | async-start | bytes 262144 | tf_op jit(solution)/shard_map/all_to_all | solution.py:145
  46.4 96.5 %reduce-scatter.3.cloned.1.call-start = ((), (), s32[]{:S(2)}) async-start(), calls=%async_computation.10 | async-start | bytes 1572864 | tf_op jit(solution)/shard_map/reduce_scatter | solution.py:190
  56.1 2.4 %copy-start.1 = (bf16[4,256,768]{1,2,0:T(8,128)(2,1)}, bf16[4,256,768]{1,2,0:T(8,128)(2,1)S(1)}, u32[]{:S(2)}) copy-start(bf16[4,256,768]{1,2,0:T(8,128)(2,1)S(1)} %fusion.2) | copy-start | bytes 4718596
  83.2 62.2 %reduce-scatter.5.cloned.1.call-start = ((), (), s32[]{:S(2)}) async-start(), calls=%async_computation.11 | async-start | bytes 1572864 | tf_op jit(solution)/shard_map/reduce_scatter | solution.py:193
  84.8 0.8 copy-start.4
  85.6 24.9 %copy-start.6 = (bf16[1,2048,256]{2,1,0:T(8,128)(2,1)S(1)}, bf16[1,2048,256]{2,1,0:T(8,128)(2,1)}, u32[]{:S(2)}) copy-start(bf16[1,2048,256]{2,1,0:T(8,128)(2,1)} %param.17) | copy-start | bytes 3145732
  110.5 1.2 copy-start.7
  111.7 2.9 %copy-start.5 = (f32[768,128]{1,0:T(8,128)S(1)}, f32[768,128]{1,0:T(8,128)}, u32[]{:S(2)}) copy-start(f32[768,128]{1,0:T(8,128)} %copy-done.4) | copy-start | bytes 1179652
  113.2 19.4 %copy-start.2 = (bf16[4,256,768]{1,2,0:T(8,128)(2,1)S(1)}, bf16[4,256,768]{1,2,0:T(8,128)(2,1)}, u32[]{:S(2)}) copy-start(bf16[4,256,768]{1,2,0:T(8,128)(2,1)} %copy-done.1) | copy-start | bytes 4718596
  113.2 29.8 %collective-permute-start = (bf16[256,2048]{1,0:T(8,128)(2,1)}, bf16[256,2048]{1,0:T(8,128)(2,1)}, u32[]{:S(2)}, u32[]{:S(2)}) collective-permute-start(bf16[256,2048]{1,0:T(8,128)(2,1)} %fusion.3), channel_id=1, source_target_pairs={{8,0},{9,1},{10,2},{11,3},{12,4},{13,5},{14,6},{15,7},{24,16},{25,... | collective-permute-start | bytes 3145736 | tf_op jit(solution)/shard_map/ppermute | solution.py:20
  115.3 13.8 %all-to-all-start.5 = ((f32[8,64,128]{2,1,0:T(8,128)}), f32[8,64,128]{2,1,0:T(8,128)}, u32[]{:S(2)}, u32[]{:S(2)}) async-start(f32[8,64,128]{2,1,0:T(8,128)} %bitcast.154), calls=%async_computation.5 | async-start | bytes 524288 | tf_op jit(solution)/shard_map/all_to_all | solution.py:165
  129.1 13.1 %all-to-all-start.4 = ((f32[8,64,128]{2,1,0:T(8,128)}), f32[8,64,128]{2,1,0:T(8,128)S(1)}, u32[]{:S(2)}, u32[]{:S(2)}) async-start(f32[8,64,128]{2,1,0:T(8,128)} %bitcast.155), calls=%async_computation.4 | async-start | bytes 524288 | tf_op jit(solution)/shard_map/all_to_all | solution.py:164
Sparse Core Ops, SparseCore 0:
  83.4 19.4 reduce-scatter.2
  110.6 19.4 reduce-scatter.4
where the time goes:
time: 159 us; the launch traced here: 157 us
  blocking collectives  46.6 us (29%)
  waiting for transfers between devices  26.5 us (17%)
  starting transfers between devices  26.2 us (16%)
  local copies, waits for them, and re-layouts  17.4 us (11%)
  between operations  15 us (9%)
  matrix products  14.5 us (9%)
  other arithmetic  10.7 us (7%)
    all_gather x1, blocking collectives, on_device(): key_piece = lax.all_gather(span_key_bf, 'tensor', axis=0, tiled=True)  14 us
    all_gather x1, blocking collectives, on_device(): value_piece = lax.all_gather(span_value_bf, 'tensor', axis=0, tiled=True)  14 us
    all_to_all x1, blocking collectives, on_device(): lax.all_to_all(value_grad[PAST:], 'tensor', split_axis=0, concat_axis=1,...  9.44 us
    all_to_all x1, blocking collectives, on_device(): lax.all_to_all(key_grad[PAST:], 'tensor', split_axis=0, concat_axis=1, ti...  9.26 us
    all_to_all x1, waiting for transfers between devices, on_device(): lax.all_to_all(value_grad[:PAST], 'tensor', split_axis=0, concat_axis=1,...  8.91 us
    unnamed x25, local copies, waits for them, and re-layouts  8.39 us
    all_to_all x1, starting transfers between devices, on_device(): lax.all_to_all(spread_heads(span_key_rows, copies), 'tensor', split_axis=...  6.33 us
    broadcast_in_dim x12, local copies, waits for them, and re-layouts, spread_heads(): jnp.broadcast_to(rows_in.reshape(row_count, head_count, 1, HD), (row_coun...  5.75 us
  transfers between devices with their start and end apart: 9, of which 6 were waited for; matrix products, arithmetic and copies ran while one was open for 17% of the time, Pallas kernels for 0%

commit v1 on v0

v1 whole, which is shorter than its diff:
```python
import functools

import jax
import jax.numpy as jnp
from jax import lax
from jax.experimental import pallas as pl
from jax.experimental.pallas import tpu as pltpu
from jax.sharding import PartitionSpec as P

HD = 128
rope_base = 500000.0
neg_large = -1e30
BF = jnp.bfloat16
F32 = jnp.float32
VMEM = pltpu.VMEM

AHEAD = 8


def call(body, out_shape, args, scratch=(), flops=0, nbytes=0):
    return pl.pallas_call(
        body,
        out_shape=out_shape,
        in_specs=[pl.BlockSpec(memory_space=VMEM)] * len(args),
        out_specs=jax.tree.map(lambda _: pl.BlockSpec(memory_space=VMEM), out_shape),
        scratch_shapes=list(scratch),
        compiler_params=pltpu.CompilerParams(vmem_limit_bytes=40 * 1024 * 1024),
        cost_estimate=pl.CostEstimate(flops=flops, bytes_accessed=nbytes, transcendentals=0),
    )(*args)


def shape(rows, columns, dtype):
    return jax.ShapeDtypeStruct((rows, columns), dtype)


def swap(block, axis, distance):
    size = lax.axis_size(axis)
    return lax.ppermute(block, axis, [(i, i ^ distance) for i in range(size)])


def from_next_section(block):
    size = lax.axis_size("pipe")
    return lax.ppermute(block, "pipe", [(i, i - 1) for i in range(1, size)])


def head_columns(head):
    return pl.ds(pl.multiple_of(head * HD, HD), HD)


def my_place(copies):
    me = lax.axis_index("tensor")
    return me // 2, me % 2, me // copies


def pack_body(heads, copies, pk, pv, sk, sv, *outs):
    z, core, own = my_place(copies)
    rows = pk.shape[0]
    for apart in range(heads):
        columns = head_columns(own ^ apart)
        outs[apart][:rows, :HD] = pk[:, columns]
        outs[apart][:rows, HD:] = pv[:, columns]
        outs[apart][rows:, :HD] = sk[:, columns]
        outs[apart][rows:, HD:] = sv[:, columns]


def attend_body(chips, past_rows, span_rows, q, do, cos, sin, first, *refs):
    pieces = refs[: 2 * chips]
    dq, keep, send, kr, krt, v, at, dst, qs, ds = refs[2 * chips :]
    span = q.shape[0]
    heads = q.shape[1] // HD
    past = 2 * chips * past_rows
    keys = past + 2 * chips * span_rows
    scale = HD**-0.5
    for place in range(2 * chips):
        piece = pieces[place]
        for start, count, lower in (
            (place * past_rows, past_rows, 0),
            (past + place * span_rows, span_rows, past_rows),
        ):
            rows = slice(start, start + count)
            k = piece[lower : lower + count, :HD].astype(F32)
            turned = k * cos[rows, :] + pltpu.roll(k, HD // 2, 1) * sin[rows, :]
            kr[rows, :] = turned.astype(BF)
            v[rows, :] = piece[lower : lower + count, HD:]
    krt[...] = kr[...].T
    for h in range(heads):
        qs[h * span : (h + 1) * span, :] = q[:, h * HD : (h + 1) * HD]
        ds[h * span : (h + 1) * span, :] = do[:, h * HD : (h + 1) * HD]
    row = lax.broadcasted_iota(jnp.int32, (keys, span), 1)
    start_key = jnp.concatenate([first[...]] * (span // HD), axis=1)
    visible = start_key <= row
    contract_last = (((1,), (1,)), ((), ()))
    for h in range(heads):
        columns = slice(h * span, (h + 1) * span)
        s = lax.dot_general(kr[...], qs[columns, :], contract_last, preferred_element_type=F32)
        s = jnp.where(visible, s * scale, neg_large)
        e = jnp.exp(s - jnp.max(s, axis=0, keepdims=True))
        a = e * (1.0 / jnp.sum(e, axis=0, keepdims=True))
        a_bf = a.astype(BF)
        at[:, columns] = a_bf
        dp = lax.dot_general(v[...], ds[columns, :], contract_last, preferred_element_type=F32)
        delta = jnp.sum(a_bf.astype(F32) * dp, axis=0, keepdims=True)
        d = (a * (dp - delta)).astype(BF)
        dst[:, columns] = d
        dqt = jnp.dot(krt[...], d, preferred_element_type=F32) * scale
        dq[:, h * HD : (h + 1) * HD] = dqt.T.astype(BF)
    dk = jnp.dot(dst[...], qs[...], preferred_element_type=F32) * scale
    dk = dk * cos[...] - pltpu.roll(dk, HD // 2, 1) * sin[...]
    dv = jnp.dot(at[...], ds[...], preferred_element_type=F32)
    half = chips * past_rows
    quarter = chips * span_rows
    for columns, grad in ((slice(0, HD), dk), (slice(HD, 2 * HD), dv)):
        keep[:half, columns] = grad[:half]
        keep[half:, columns] = grad[past : past + quarter]
        send[:half, columns] = grad[half:past].astype(BF)
        send[half:, columns] = grad[past + quarter :].astype(BF)


def chip_sum_body(chips, past_rows, keep, received, *outs):
    own, sends = outs[0], outs[1:]
    half = chips * past_rows
    total = keep[...] + received[...].astype(F32)
    own[:past_rows, :] = total[:past_rows]
    own[past_rows:, :] = total[half:]
    span_part = total[half:].astype(BF)
    for j in range(1, chips):
        sends[j - 1][:past_rows, :] = total[j * past_rows : (j + 1) * past_rows].astype(BF)
        sends[j - 1][past_rows:, :] = span_part


def group_sum_body(heads, copies, chips, past_rows, span_rows, peers, *refs):
    own, received = refs[0], refs[1:chips]
    dk_past, dv_past, span_grad = refs[chips : chips + 3]
    sends = refs[chips + 3 : chips + 2 + peers]
    mine, ordered = refs[chips + 2 + peers :]
    z, core, head = my_place(copies)
    replica = lax.axis_index("dp")
    per_head = copies // 2
    width = heads * HD
    share = width // peers
    for apart in range(heads):
        past_total = None
        span_total = [None] * chips
        for j in range(apart * per_head, (apart + 1) * per_head):
            block = own if j == 0 else received[j - 1]
            part = block[:past_rows, :].astype(F32)
            past_total = part if past_total is None else past_total + part
            for i in range(chips):
                lower = past_rows + i * span_rows
                part = block[lower : lower + span_rows, :].astype(F32)
                span_total[i ^ j] = part if span_total[i ^ j] is None else span_total[i ^ j] + part
        columns = head_columns(head ^ apart)
        dk_past[:, columns] = past_total[:, :HD]
        dv_past[:, columns] = past_total[:, HD:]
        value_columns = pl.ds(pl.multiple_of(width + (head ^ apart) * HD, HD), HD)
        for i in range(chips):
            rows = pl.ds(pl.multiple_of((z ^ i) * span_rows, span_rows), span_rows)
            rounded = span_total[i].astype(ordered.dtype)
            ordered[rows, columns] = rounded[:, :HD]
            ordered[rows, value_columns] = rounded[:, HD:]
    span_grad[...] = ordered[...].astype(BF)
    for k in range(peers):
        target = mine if k == 0 else sends[k - 1]
        lower = pl.multiple_of((replica ^ k) * share, HD)
        target[:, :share] = span_grad[:, pl.ds(lower, share)]
        target[:, share:] = span_grad[:, pl.ds(pl.multiple_of(width + lower, HD), share)]


def row_type(span_rows):
    return BF if span_rows % 16 == 0 else F32


def weave(chips, span_rows, target, own, other):
    core = lax.axis_index("tensor") % 2
    for z in range(chips):
        part = slice(z * span_rows, (z + 1) * span_rows)
        lower = pl.multiple_of((2 * z + core) * span_rows, span_rows)
        target[pl.ds(lower, span_rows), :] = own[part, :].astype(target.dtype)
        lower = pl.multiple_of((2 * z + 1 - core) * span_rows, span_rows)
        target[pl.ds(lower, span_rows), :] = other[part, :].astype(target.dtype)


def input_grad_body(chips, span_rows, own, other, kw, vw, out, rows):
    weave(chips, span_rows, rows, own, other)
    width = kw.shape[1]
    contract_last = (((1,), (1,)), ((), ()))
    total = lax.dot_general(rows[:, :width].astype(BF), kw[...], contract_last, preferred_element_type=F32)
    total = total + lax.dot_general(
        rows[:, width:].astype(BF), vw[...], contract_last, preferred_element_type=F32
    )
    out[...] = total.astype(BF)


def weight_grad_body(chips, span_rows, replicas, *refs):
    normed = refs[:replicas]
    own = refs[replicas : 2 * replicas]
    other = refs[2 * replicas : 3 * replicas]
    dkw, dvw, rows = refs[3 * replicas :]
    share = dkw.shape[1]
    contract_first = (((0,), (0,)), ((), ()))
    total = None
    for k in range(replicas):
        weave(chips, span_rows, rows.at[k], own[k], other[k])
        product = lax.dot_general(
            normed[k][...], rows[k].astype(BF), contract_first, preferred_element_type=F32
        )
        product = product.astype(BF).astype(F32)
        total = product if total is None else total + product
    dkw[...] = total[:, :share]
    dvw[...] = total[:, share:]


def key_tables(chips, past_rows, span_rows, offset):
    me = lax.axis_index("tensor")

    def places(rows):
        index = lax.broadcasted_iota(jnp.int32, (2 * chips * rows, HD), 0)
        place = index // rows
        holder = 2 * ((me // 2) ^ (place % chips)) + ((me % 2) ^ (place // chips))
        return holder * rows + index % rows

    past = places(past_rows)
    span = places(span_rows)
    positions = jnp.concatenate([past, offset + span], axis=0)
    first = jnp.concatenate([jnp.where(past < offset, -1, 1 << 30), span], axis=0)
    lane = lax.broadcasted_iota(jnp.int32, positions.shape, 1)
    inverse_freq = rope_base ** (-2.0 * (lane % (HD // 2)).astype(F32) / HD)
    angles = positions.astype(F32) * inverse_freq
    sine = jnp.sin(angles)
    return jnp.cos(angles), jnp.where(lane < HD // 2, -sine, sine), first


def on_device(
    queries,
    grad_out,
    past_keys,
    past_values,
    span_keys,
    span_values,
    normed,
    key_weight,
    value_weight,
    offsets,
):
    devices = lax.axis_size("tensor")
    replicas = lax.axis_size("dp")
    chips = devices // 2
    past_rows = past_keys.shape[2]
    span_rows = span_keys.shape[2]
    span = queries.shape[2]
    width = past_keys.shape[3]
    heads = width // HD
    copies = devices // heads
    features = normed.shape[3]
    share = width // replicas
    keys = devices * (past_rows + span_rows)
    local_heads = queries.shape[3] // HD

    normed_rows = normed[0, 0]
    kw, vw = key_weight[0], value_weight[0]
    ahead = features * AHEAD // 16

    packed = call(
        functools.partial(pack_body, heads, copies),
        [shape(past_rows + span_rows, 2 * HD, BF)] * heads,
        (past_keys[0, 0], past_values[0, 0], span_keys[0, 0], span_values[0, 0]),
        nbytes=2 * (past_rows + span_rows) * 2 * width * 2,
    )
    per_head = copies // 2
    pieces = [packed[0]] + [swap(packed[j // per_head], "tensor", 2 * j) for j in range(1, chips)]
    pieces = pieces + [swap(piece, "tensor", 1) for piece in pieces]

    normed_from = [normed_rows] + [swap(normed_rows, "dp", k) for k in range(1, replicas)]
    kw_ahead = from_next_section(kw[:ahead])
    vw_ahead = from_next_section(vw[:ahead])

    cos, sin, first = key_tables(chips, past_rows, span_rows, offsets[0, 0])
    part_rows = chips * (past_rows + span_rows)
    query_grad, keep, send = call(
        functools.partial(attend_body, chips, past_rows, span_rows),
        [
            shape(span, local_heads * HD, BF),
            shape(part_rows, 2 * HD, F32),
            shape(part_rows, 2 * HD, BF),
        ],
        (queries[0, 0], grad_out[0, 0], cos, sin, first, *pieces),
        scratch=[
            VMEM((keys, HD), BF),
            VMEM((HD, keys), BF),
            VMEM((keys, HD), BF),
            VMEM((keys, local_heads * span), BF),
            VMEM((keys, local_heads * span), BF),
            VMEM((local_heads * span, HD), BF),
            VMEM((local_heads * span, HD), BF),
        ],
        flops=10 * keys * local_heads * span * HD,
        nbytes=4 * span * local_heads * HD * 2,
    )
    own, *sends = call(
        functools.partial(chip_sum_body, chips, past_rows),
        [shape(past_rows + chips * span_rows, 2 * HD, F32)]
        + [shape(past_rows + chips * span_rows, 2 * HD, BF)] * (chips - 1),
        (keep, swap(send, "tensor", 1)),
        nbytes=part_rows * 2 * HD * 8,
    )
    received = [swap(sends[j - 1], "tensor", 2 * j) for j in range(1, chips)]
    dk_past, dv_past, span_grad, *shares = call(
        functools.partial(group_sum_body, heads, copies, chips, past_rows, span_rows, replicas),
        [
            shape(past_rows, width, F32),
            shape(past_rows, width, F32),
            shape(chips * span_rows, 2 * width, BF),
        ]
        + [shape(chips * span_rows, 2 * share, BF)] * replicas,
        (own, *received),
        scratch=[VMEM((chips * span_rows, 2 * width), row_type(span_rows))],
        nbytes=part_rows * 2 * HD * 8,
    )
    next_grad = from_next_section(span_grad)
    share_from = [shares[-1]] + [swap(shares[k - 1], "dp", k) for k in range(1, replicas)]

    late = call(
        functools.partial(input_grad_body, chips, span_rows),
        shape(span, features - ahead, BF),
        (span_grad, swap(span_grad, "tensor", 1), kw[ahead:], vw[ahead:]),
        scratch=[VMEM((span, 2 * width), row_type(span_rows))],
        flops=4 * span * width * (features - ahead),
        nbytes=(features - ahead) * (4 * width + 2 * span),
    )
    late = from_next_section(late)
    early = call(
        functools.partial(input_grad_body, chips, span_rows),
        shape(span, ahead, BF),
        (next_grad, swap(next_grad, "tensor", 1), kw_ahead, vw_ahead),
        scratch=[VMEM((span, 2 * width), row_type(span_rows))],
        flops=4 * span * width * ahead,
        nbytes=ahead * (4 * width + 2 * span),
    )
    dkw, dvw = call(
        functools.partial(weight_grad_body, chips, span_rows, replicas),
        [shape(features, share, F32)] * 2,
        (*normed_from, *share_from, *[swap(part, "tensor", 1) for part in share_from]),
        scratch=[VMEM((replicas, span, 2 * share), row_type(span_rows))],
        flops=4 * span * features * share * replicas,
        nbytes=features * (2 * span * replicas + 8 * share),
    )
    section_grad = jnp.concatenate([early, late], axis=1)
    return (
        query_grad[None, None],
        dk_past[None, None],
        dv_past[None, None],
        dkw[None],
        dvw[None],
        section_grad[None, None],
    )


def solution(mesh):
    return jax.shard_map(
        on_device,
        mesh=mesh,
        in_specs=(
            P("pipe", "dp", None, "tensor"),
            P("pipe", "dp", None, "tensor"),
            P("pipe", "dp", "tensor", None),
            P("pipe", "dp", "tensor", None),
            P("pipe", "dp", "tensor", None),
            P("pipe", "dp", "tensor", None),
            P("pipe", "dp", None, "tensor"),
            P("pipe", "tensor", None),
            P("pipe", "tensor", None),
            P("pipe", "dp"),
        ),
        out_specs=(
            P("pipe", "dp", None, "tensor"),
            P("pipe", "dp", "tensor", None),
            P("pipe", "dp", "tensor", None),
            P("pipe", "tensor", "dp"),
            P("pipe", "tensor", "dp"),
            P("pipe", "dp", None, "tensor"),
        ),
        check_vma=False,
    )
```

time: 159 us -> 80.3 us (0.51)
  blocking collectives: 46.6 us -> 0 us
  waiting for transfers between devices: 26.5 us -> 44.3 us
  matrix products: 14.5 us -> 0 us
  local copies, waits for them, and re-layouts: 17.4 us -> 3.1 us
  between operations: 15 us -> 1.52 us
  Pallas kernels: 0 us -> 7.73 us
  other arithmetic: 10.7 us -> 3.43 us
  starting transfers between devices: 26.2 us -> 19.7 us
    ppermute x1 -> x21, waiting for transfers between devices: 0.01 us -> 44.3 us  [the longest x4 22.9 us: from_next_section(): return lax.ppermute(block, 'pipe', [(i, i - 1) for i in range(1, size)])]
    all_gather x2 -> x0, blocking collectives: 27.9 us -> none  [the longest x1 14 us: on_device(): key_piece = lax.all_gather(span_key_bf, 'tensor', axis=0, tiled=True)]
    all_to_all x6 -> x0, waiting for transfers between devices: 26.5 us -> none  [the longest x1 8.91 us: on_device(): lax.all_to_all(value_grad[:PAST], 'tensor', split_axis=0, concat_axis=1,...]
    all_to_all x6 -> x0, starting transfers between devices: 24.8 us -> none  [the longest x1 6.33 us: on_device(): lax.all_to_all(spread_heads(span_key_rows, copies), 'tensor', split_axis=...]
    all_to_all x2 -> x0, blocking collectives: 18.7 us -> none  [the longest x1 9.44 us: on_device(): lax.all_to_all(value_grad[PAST:], 'tensor', split_axis=0, concat_axis=1,...]
    ppermute x1 -> x21, starting transfers between devices: 1.41 us -> 19.7 us  [the longest x17 14.6 us: swap(): return lax.ppermute(block, axis, [(i, i ^ distance) for i in range(size)])]
    dot_general x9 -> x0, matrix products: 11.3 us -> none  [the longest x1 2.44 us: attend_backward(): jnp.einsum('thd,kd->htk', grad_rows, value_rows, preferred_element_type=j...]
    pallas_call x0 -> x7, Pallas kernels: none -> 7.73 us  [call(): pl.pallas_call(body, out_shape=out_shape, in_specs=[pl.BlockSpec(memory_s...]
  transfers between devices with their start and end apart: 9 -> 21, of which waited for: 6 -> 11; matrix products, arithmetic and copies ran while one was open for 17% -> 4% of each run, Pallas kernels for 0% -> 2%
where the time goes in v1:
time: 80.3 us; the launch traced here: 79.8 us
  waiting for transfers between devices  44.3 us (55%)
  starting transfers between devices  19.7 us (25%)
  Pallas kernels  7.73 us (10%)
  other arithmetic  3.43 us (4%)
  local copies, waits for them, and re-layouts  3.1 us (4%)
  between operations  1.52 us (2%)
    ppermute x4, waiting for transfers between devices, from_next_section(): return lax.ppermute(block, 'pipe', [(i, i - 1) for i in range(1, size)])  22.9 us
    ppermute x17, waiting for transfers between devices, swap(): return lax.ppermute(block, axis, [(i, i ^ distance) for i in range(size)])  21.4 us
    ppermute x17, starting transfers between devices, swap(): return lax.ppermute(block, axis, [(i, i ^ distance) for i in range(size)])  14.6 us
    pallas_call x7, Pallas kernels, call(): pl.pallas_call(body, out_shape=out_shape, in_specs=[pl.BlockSpec(memory_s...  7.73 us
    ppermute x4, starting transfers between devices, from_next_section(): return lax.ppermute(block, 'pipe', [(i, i - 1) for i in range(1, size)])  5.16 us
    unnamed x18, local copies, waits for them, and re-layouts  2.97 us
  transfers between devices with their start and end apart: 21, of which 11 were waited for; matrix products, arithmetic and copies ran while one was open for 4% of the time, Pallas kernels for 2%

profile of v1, /device:TPU:0, one launch (start us, length us, event | category | flops | bytes accessed | tf_op | source)
XLA Modules:
  0.0 79.8 jit_solution(6092562538590554183)
XLA Ops:
  0.6 0.7 copy-done.1
  1.4 0.8 copy-done.2
  3.6 4.1 %collective-permute-start.1 = (bf16[96,256]{1,0:T(8,128)(2,1)S(1)}, bf16[96,256]{1,0:T(8,128)(2,1)S(1)}, u32[]{:S(2)}, u32[]{:S(2)}) collective-permute-start(bf16[96,256]{1,0:T(8,128)(2,1)S(1)} %get-tuple-element.23), channel_id=1, source_target_pairs={{0,4},{1,5},{2,6},{3,7},{4,0},{5,1},{6,2},{7,3},{8,12},{9,13},{10,... | collective-permute-start | bytes 147464 | tf_op jit(solution)/shard_map/ppermute | solution.py:38
  7.7 1.3 %collective-permute-start.2 = (bf16[96,256]{1,0:T(8,128)(2,1)S(1)}, bf16[96,256]{1,0:T(8,128)(2,1)S(1)}, u32[]{:S(2)}, u32[]{:S(2)}) collective-permute-start(bf16[96,256]{1,0:T(8,128)(2,1)S(1)} %get-tuple-element.23), channel_id=1, source_target_pairs={{0,6},{1,7},{2,4},{3,5},{4,2},{5,3},{6,0},{7,1},{8,14},{9,15},{10,... | collective-permute-start | bytes 147464 | tf_op jit(solution)/shard_map/ppermute | solution.py:38
  10.8 1.6 %negate_select_fusion = (f32[768,128]{1,0:T(8,128)S(1)}, f32[768,128]{1,0:T(8,128)S(1)}) fusion(s32[256,128]{1,0:T(8,128)S(1)} %get-tuple-element.47, s32[512,128]{1,0:T(8,128)S(1)} %get-tuple-element.45, s32[128]{0:T(128)S(1)} %get-tuple-element.62, s32[128]{0:T(128)S(1)} %get-tuple-element.63, pred[128]{0:T(512)(128)(4,1)S(1)} %get-tuple-element.61, ...), kind=kLoop, calls=%fused_computation.5 | loop fusion | flops 786432 | bytes 1180928 | tf_op jit(solution)/shard_map/jit(_where)/select_n | solution.py:230
  12.4 0.8 collective-permute-done.refs_1_
  14.9 3.9 %shard_map.146 = (bf16[256,512]{1,0:T(8,128)(2,1)}, f32[384,256]{1,0:T(8,128)S(1)}, bf16[384,256]{1,0:T(8,128)(2,1)S(1)}) custom-call(bf16[256,512]{1,0:T(8,128)(2,1)S(1)} %bitcast.31, bf16[256,512]{1,0:T(8,128)(2,1)S(1)} %bitcast.32, f32[768,128]{1,0:T(8,128)S(1)} %get-tuple-element.43.cos, f32[768,128]{1,0:T(8,128)S(1)} %get-tuple-element.42.sin, ...), custom_call_target="tpu_custom_call" | custom-call | flops 1006632960 | bytes 1048576 | tf_op jit(solution)/shard_map/pallas_call | solution.py:21
  19.0 1.3 %collective-permute-done.7.received = bf16[384,256]{1,0:T(8,128)(2,1)S(1)} collective-permute-done((bf16[384,256]{1,0:T(8,128)(2,1)S(1)}, bf16[384,256]{1,0:T(8,128)(2,1)S(1)}, u32[]{:S(2)}, u32[]{:S(2)}) %collective-permute-start.7) | collective-permute-done | bytes 196640 | tf_op jit(solution)/shard_map/ppermute | solution.py:38
  20.3 2.9 %collective-permute-start.10 = (bf16[192,256]{1,0:T(8,128)(2,1)S(1)}, bf16[192,256]{1,0:T(8,128)(2,1)S(1)}, u32[]{:S(2)}, u32[]{:S(2)}) collective-permute-start(bf16[192,256]{1,0:T(8,128)(2,1)S(1)} %get-tuple-element.30), channel_id=1, source_target_pairs={{0,6},{1,7},{2,4},{3,5},{4,2},{5,3},{6,0},{7,1},{8,14},{9,15},{10,... | collective-permute-start | bytes 294920 | tf_op jit(solution)/shard_map/ppermute | solution.py:38
  23.2 1.5 %collective-permute-start.9 = (bf16[192,256]{1,0:T(8,128)(2,1)S(1)}, bf16[192,256]{1,0:T(8,128)(2,1)S(1)}, u32[]{:S(2)}, u32[]{:S(2)}) collective-permute-start(bf16[192,256]{1,0:T(8,128)(2,1)S(1)} %get-tuple-element.29), channel_id=1, source_target_pairs={{0,4},{1,5},{2,6},{3,7},{4,0},{5,1},{6,2},{7,3},{8,12},{9,13},{10,... | collective-permute-start | bytes 294920 | tf_op jit(solution)/shard_map/ppermute | solution.py:38
  24.8 1.5 %collective-permute-start.11 = (bf16[256,2048]{1,0:T(8,128)(2,1)S(1)}, bf16[256,2048]{1,0:T(8,128)(2,1)S(1)}, u32[]{:S(2)}, u32[]{:S(2)}) collective-permute-start(bf16[256,2048]{1,0:T(8,128)(2,1)S(1)} %bitcast.25), channel_id=1, source_target_pairs={{0,16},{16,0},{1,17},{17,1},{2,18},{18,2},{3,19},{19,3},{4,20},{20... | collective-permute-start | bytes 3145736 | tf_op jit(solution)/shard_map/ppermute | solution.py:38
  26.3 1.6 %collective-permute-done.10.refs_3_ = bf16[192,256]{1,0:T(8,128)(2,1)S(1)} collective-permute-done((bf16[192,256]{1,0:T(8,128)(2,1)S(1)}, bf16[192,256]{1,0:T(8,128)(2,1)S(1)}, u32[]{:S(2)}, u32[]{:S(2)}) %collective-permute-start.10) | collective-permute-done | bytes 98336 | tf_op jit(solution)/shard_map/ppermute | solution.py:38
  27.9 2.4 %collective-permute-done.8.refs_1_ = bf16[192,256]{1,0:T(8,128)(2,1)S(1)} collective-permute-done((bf16[192,256]{1,0:T(8,128)(2,1)S(1)}, bf16[192,256]{1,0:T(8,128)(2,1)S(1)}, u32[]{:S(2)}, u32[]{:S(2)}) %collective-permute-start.8) | collective-permute-done | bytes 98336 | tf_op jit(solution)/shard_map/ppermute | solution.py:38
  30.3 2.1 %collective-permute-done.9.refs_2_ = bf16[192,256]{1,0:T(8,128)(2,1)S(1)} collective-permute-done((bf16[192,256]{1,0:T(8,128)(2,1)S(1)}, bf16[192,256]{1,0:T(8,128)(2,1)S(1)}, u32[]{:S(2)}, u32[]{:S(2)}) %collective-permute-start.9) | collective-permute-done | bytes 98336 | tf_op jit(solution)/shard_map/ppermute | solution.py:38
  33.3 1.3 %collective-permute-start.17 = (bf16[1024,256]{1,0:T(8,128)(2,1)S(1)}, bf16[1024,256]{1,0:T(8,128)(2,1)S(1)}, u32[]{:S(2)}, u32[]{:S(2)}) collective-permute-start(bf16[1024,256]{1,0:T(8,128)(2,1)S(1)} %get-tuple-element.65), channel_id=1, source_target_pairs={{8,0},{9,1},{10,2},{11,3},{12,4},{13,5},{14,6},{15,7},{24,16},{25,... | collective-permute-start | bytes 1572872 | tf_op jit(solution)/shard_map/ppermute | solution.py:43
  34.6 1.3 %collective-permute-start.18 = (bf16[1024,256]{1,0:T(8,128)(2,1)S(1)}, bf16[1024,256]{1,0:T(8,128)(2,1)S(1)}, u32[]{:S(2)}, u32[]{:S(2)}) collective-permute-start(bf16[1024,256]{1,0:T(8,128)(2,1)S(1)} %get-tuple-element.38), channel_id=1, source_target_pairs={{8,0},{9,1},{10,2},{11,3},{12,4},{13,5},{14,6},{15,7},{24,16},{25,... | collective-permute-start | bytes 1572872 | tf_op jit(solution)/shard_map/ppermute | solution.py:43
  36.4 1.3 %collective-permute-start.20 = (bf16[256,1024]{1,0:T(8,128)(2,1)S(1)}, bf16[256,1024]{1,0:T(8,128)(2,1)S(1)}, u32[]{:S(2)}, u32[]{:S(2)}) collective-permute-start(bf16[256,1024]{1,0:T(8,128)(2,1)S(1)} %shard_map.151), channel_id=1, source_target_pairs={{8,0},{9,1},{10,2},{11,3},{12,4},{13,5},{14,6},{15,7},{24,16},{25,... | collective-permute-start | bytes 1572872 | tf_op jit(solution)/shard_map/ppermute | solution.py:43
  37.7 1.6 %collective-permute-start.12 = (bf16[128,256]{1,0:T(8,128)(2,1)S(1)}, bf16[128,256]{1,0:T(8,128)(2,1)S(1)}, u32[]{:S(2)}, u32[]{:S(2)}) collective-permute-start(bf16[128,256]{1,0:T(8,128)(2,1)S(1)} %get-tuple-element.34), channel_id=1, source_target_pairs={{0,16},{16,0},{1,17},{17,1},{2,18},{18,2},{3,19},{19,3},{4,20},{20... | collective-permute-start | bytes 196616 | tf_op jit(solution)/shard_map/ppermute | solution.py:38
  39.3 11.3 %collective-permute-done.12.refs_3_ = bf16[128,256]{1,0:T(8,128)(2,1)S(1)} collective-permute-done((bf16[128,256]{1,0:T(8,128)(2,1)S(1)}, bf16[128,256]{1,0:T(8,128)(2,1)S(1)}, u32[]{:S(2)}, u32[]{:S(2)}) %collective-permute-start.12) | collective-permute-done | bytes 65568 | tf_op jit(solution)/shard_map/ppermute | solution.py:38
  50.6 1.3 %collective-permute-start.15 = (bf16[128,512]{1,0:T(8,128)(2,1)S(1)}, bf16[128,512]{1,0:T(8,128)(2,1)S(1)}, u32[]{:S(2)}, u32[]{:S(2)}) collective-permute-start(bf16[128,512]{1,0:T(8,128)(2,1)S(1)} %get-tuple-element.37.own), channel_id=1, source_target_pairs={{8,0},{9,1},{10,2},{11,3},{12,4},{13,5},{14,6},{15,7},{24,16},{25,... | collective-permute-start | bytes 393224 | tf_op jit(solution)/shard_map/ppermute | solution.py:43
  51.9 22.9 %collective-permute-done.15.own = bf16[128,512]{1,0:T(8,128)(2,1)S(1)} collective-permute-done((bf16[128,512]{1,0:T(8,128)(2,1)S(1)}, bf16[128,512]{1,0:T(8,128)(2,1)S(1)}, u32[]{:S(2)}, u32[]{:S(2)}) %collective-permute-start.15) | collective-permute-done | bytes 131104 | tf_op jit(solution)/shard_map/ppermute | solution.py:43
  75.4 0.8 collective-permute-done.16.other
  76.6 1.1 %maximum_bitcast_fusion = bf16[1,1,256,2048]{3,2,1,0:T(8,128)(2,1)} fusion(bf16[256,1024]{1,0:T(8,128)(2,1)S(1)} %collective-permute-done.20, bf16[256,1024]{1,0:T(8,128)(2,1)S(1)} %shard_map.150), kind=kLoop, calls=%fused_computation | loop fusion | flops 2097152 | bytes 2097152 | tf_op jit(solution)/shard_map/broadcast_in_dim | solution.py:354
  77.7 2.1 %shard_map.149 = (f32[2048,128]{1,0:T(8,128)}, f32[2048,128]{1,0:T(8,128)}) custom-call(bf16[256,2048]{1,0:T(8,128)(2,1)S(1)} %bitcast.26, bf16[256,2048]{1,0:T(8,128)(2,1)S(1)} %collective-permute-done.11.refs_1_, bf16[128,256]{1,0:T(8,128)(2,1)S(1)} %get-tuple-element.33.refs_2_, bf16[128,256]{1,0:T(8,128)(2,1)S(1)} %collective-permute-done.12.refs_3_, ...), custom_call_target="tpu_custom_call" | custom-call | flops 536870912 | bytes 4194304 | tf_op jit(solution)/shard_map/pallas_call | solution.py:21
  (57 shorter events, 6.8 us)
Async XLA Ops:
  3.6 9.6 %collective-permute-start.1 = (bf16[96,256]{1,0:T(8,128)(2,1)S(1)}, bf16[96,256]{1,0:T(8,128)(2,1)S(1)}, u32[]{:S(2)}, u32[]{:S(2)}) collective-permute-start(bf16[96,256]{1,0:T(8,128)(2,1)S(1)} %get-tuple-element.23), channel_id=1, source_target_pairs={{0,4},{1,5},{2,6},{3,7},{4,0},{5,1},{6,2},{7,3},{8,12},{9,13},{10,... | collective-permute-start | bytes 147464 | tf_op jit(solution)/shard_map/ppermute | solution.py:38
  7.7 6.0 %collective-permute-start.2 = (bf16[96,256]{1,0:T(8,128)(2,1)S(1)}, bf16[96,256]{1,0:T(8,128)(2,1)S(1)}, u32[]{:S(2)}, u32[]{:S(2)}) collective-permute-start(bf16[96,256]{1,0:T(8,128)(2,1)S(1)} %get-tuple-element.23), channel_id=1, source_target_pairs={{0,6},{1,7},{2,4},{3,5},{4,2},{5,3},{6,0},{7,1},{8,14},{9,15},{10,... | collective-permute-start | bytes 147464 | tf_op jit(solution)/shard_map/ppermute | solution.py:38
  9.1 4.1 %collective-permute-start = (bf16[96,256]{1,0:T(8,128)(2,1)S(1)}, bf16[96,256]{1,0:T(8,128)(2,1)S(1)}, u32[]{:S(2)}, u32[]{:S(2)}) collective-permute-start(bf16[96,256]{1,0:T(8,128)(2,1)S(1)} %get-tuple-element.22.refs_0_), channel_id=1, source_target_pairs={{0,2},{1,3},{2,0},{3,1},{4,6},{5,7},{6,4},{7,5},{8,10},{9,11},{10,... | collective-permute-start | bytes 147464 | tf_op jit(solution)/shard_map/ppermute | solution.py:38
  9.3 4.5 %collective-permute-start.3 = (bf16[96,256]{1,0:T(8,128)(2,1)S(1)}, bf16[96,256]{1,0:T(8,128)(2,1)S(1)}, u32[]{:S(2)}, u32[]{:S(2)}) collective-permute-start(bf16[96,256]{1,0:T(8,128)(2,1)S(1)} %get-tuple-element.22.refs_0_), channel_id=1, source_target_pairs={{0,1},{1,0},{2,3},{3,2},{4,5},{5,4},{6,7},{7,6},{8,9},{9,8},{10,11... | collective-permute-start | bytes 147464 | tf_op jit(solution)/shard_map/ppermute | solution.py:38
  13.2 1.2 %collective-permute-start.4 = (bf16[96,256]{1,0:T(8,128)(2,1)S(1)}, bf16[96,256]{1,0:T(8,128)(2,1)S(1)}, u32[]{:S(2)}, u32[]{:S(2)}) collective-permute-start(bf16[96,256]{1,0:T(8,128)(2,1)S(1)} %collective-permute-done.refs_1_), channel_id=1, source_target_pairs={{0,1},{1,0},{2,3},{3,2},{4,5},{5,4},{6,7},{7,6},{8,9},{9,8},{10,11... | collective-permute-start | bytes 147464 | tf_op jit(solution)/shard_map/ppermute | solution.py:38
  13.2 1.4 %collective-permute-start.5 = (bf16[96,256]{1,0:T(8,128)(2,1)S(1)}, bf16[96,256]{1,0:T(8,128)(2,1)S(1)}, u32[]{:S(2)}, u32[]{:S(2)}) collective-permute-start(bf16[96,256]{1,0:T(8,128)(2,1)S(1)} %collective-permute-done.1.refs_2_), channel_id=1, source_target_pairs={{0,1},{1,0},{2,3},{3,2},{4,5},{5,4},{6,7},{7,6},{8,9},{9,8},{10,11... | collective-permute-start | bytes 147464 | tf_op jit(solution)/shard_map/ppermute | solution.py:38
  13.7 1.2 %collective-permute-start.6 = (bf16[96,256]{1,0:T(8,128)(2,1)S(1)}, bf16[96,256]{1,0:T(8,128)(2,1)S(1)}, u32[]{:S(2)}, u32[]{:S(2)}) collective-permute-start(bf16[96,256]{1,0:T(8,128)(2,1)S(1)} %collective-permute-done.2.refs_3_), channel_id=1, source_target_pairs={{0,1},{1,0},{2,3},{3,2},{4,5},{5,4},{6,7},{7,6},{8,9},{9,8},{10,11... | collective-permute-start | bytes 147464 | tf_op jit(solution)/shard_map/ppermute | solution.py:38
  14.9 9.9 %copy-start = (bf16[1,1,256,2048]{3,2,1,0:T(8,128)(2,1)S(1)}, bf16[1,1,256,2048]{3,2,1,0:T(8,128)(2,1)}, u32[]{:S(2)}) copy-start(bf16[1,1,256,2048]{3,2,1,0:T(8,128)(2,1)} %param.16) | copy-start | bytes 3145732
  14.9 18.2 %copy-start.8 = (bf16[1,2048,256]{2,1,0:T(8,128)(2,1)S(1)}, bf16[1,2048,256]{2,1,0:T(8,128)(2,1)}, u32[]{:S(2)}) copy-start(bf16[1,2048,256]{2,1,0:T(8,128)(2,1)} %param.17) | copy-start | bytes 3145732
  18.8 14.3 %copy-start.7 = (bf16[1,2048,256]{2,1,0:T(8,128)(2,1)S(1)}, bf16[1,2048,256]{2,1,0:T(8,128)(2,1)}, u32[]{:S(2)}) copy-start(bf16[1,2048,256]{2,1,0:T(8,128)(2,1)} %param.18) | copy-start | bytes 3145732
  18.8 1.4 %collective-permute-start.7 = (bf16[384,256]{1,0:T(8,128)(2,1)S(1)}, bf16[384,256]{1,0:T(8,128)(2,1)S(1)}, u32[]{:S(2)}, u32[]{:S(2)}) collective-permute-start(bf16[384,256]{1,0:T(8,128)(2,1)S(1)} %get-tuple-element.26), channel_id=1, source_target_pairs={{0,1},{1,0},{2,3},{3,2},{4,5},{5,4},{6,7},{7,6},{8,9},{9,8},{10,11... | collective-permute-start | bytes 589832 | tf_op jit(solution)/shard_map/ppermute | solution.py:38
  20.3 7.5 %collective-permute-start.10 = (bf16[192,256]{1,0:T(8,128)(2,1)S(1)}, bf16[192,256]{1,0:T(8,128)(2,1)S(1)}, u32[]{:S(2)}, u32[]{:S(2)}) collective-permute-start(bf16[192,256]{1,0:T(8,128)(2,1)S(1)} %get-tuple-element.30), channel_id=1, source_target_pairs={{0,6},{1,7},{2,4},{3,5},{4,2},{5,3},{6,0},{7,1},{8,14},{9,15},{10,... | collective-permute-start | bytes 294920 | tf_op jit(solution)/shard_map/ppermute | solution.py:38
  23.2 7.1 %collective-permute-start.8 = (bf16[192,256]{1,0:T(8,128)(2,1)S(1)}, bf16[192,256]{1,0:T(8,128)(2,1)S(1)}, u32[]{:S(2)}, u32[]{:S(2)}) collective-permute-start(bf16[192,256]{1,0:T(8,128)(2,1)S(1)} %get-tuple-element.28), channel_id=1, source_target_pairs={{0,2},{1,3},{2,0},{3,1},{4,6},{5,7},{6,4},{7,5},{8,10},{9,11},{10,... | collective-permute-start | bytes 294920 | tf_op jit(solution)/shard_map/ppermute | solution.py:38
  23.2 9.2 %collective-permute-start.9 = (bf16[192,256]{1,0:T(8,128)(2,1)S(1)}, bf16[192,256]{1,0:T(8,128)(2,1)S(1)}, u32[]{:S(2)}, u32[]{:S(2)}) collective-permute-start(bf16[192,256]{1,0:T(8,128)(2,1)S(1)} %get-tuple-element.29), channel_id=1, source_target_pairs={{0,4},{1,5},{2,6},{3,7},{4,0},{5,1},{6,2},{7,3},{8,12},{9,13},{10,... | collective-permute-start | bytes 294920 | tf_op jit(solution)/shard_map/ppermute | solution.py:38
  24.8 52.9 %collective-permute-start.11 = (bf16[256,2048]{1,0:T(8,128)(2,1)S(1)}, bf16[256,2048]{1,0:T(8,128)(2,1)S(1)}, u32[]{:S(2)}, u32[]{:S(2)}) collective-permute-start(bf16[256,2048]{1,0:T(8,128)(2,1)S(1)} %bitcast.25), channel_id=1, source_target_pairs={{0,16},{16,0},{1,17},{17,1},{2,18},{18,2},{3,19},{19,3},{4,20},{20... | collective-permute-start | bytes 3145736 | tf_op jit(solution)/shard_map/ppermute | solution.py:38
  33.1 2.8 %collective-permute-start.19 = (bf16[128,512]{1,0:T(8,128)(2,1)S(1)}, bf16[128,512]{1,0:T(8,128)(2,1)S(1)}, u32[]{:S(2)}, u32[]{:S(2)}) collective-permute-start(bf16[128,512]{1,0:T(8,128)(2,1)S(1)} %get-tuple-element.37.own), channel_id=1, source_target_pairs={{0,1},{1,0},{2,3},{3,2},{4,5},{5,4},{6,7},{7,6},{8,9},{9,8},{10,11... | collective-permute-start | bytes 393224 | tf_op jit(solution)/shard_map/ppermute | solution.py:38
  33.3 41.5 %collective-permute-start.17 = (bf16[1024,256]{1,0:T(8,128)(2,1)S(1)}, bf16[1024,256]{1,0:T(8,128)(2,1)S(1)}, u32[]{:S(2)}, u32[]{:S(2)}) collective-permute-start(bf16[1024,256]{1,0:T(8,128)(2,1)S(1)} %get-tuple-element.65), channel_id=1, source_target_pairs={{8,0},{9,1},{10,2},{11,3},{12,4},{13,5},{14,6},{15,7},{24,16},{25,... | collective-permute-start | bytes 1572872 | tf_op jit(solution)/shard_map/ppermute | solution.py:43
  34.6 40.7 %collective-permute-start.18 = (bf16[1024,256]{1,0:T(8,128)(2,1)S(1)}, bf16[1024,256]{1,0:T(8,128)(2,1)S(1)}, u32[]{:S(2)}, u32[]{:S(2)}) collective-permute-start(bf16[1024,256]{1,0:T(8,128)(2,1)S(1)} %get-tuple-element.38), channel_id=1, source_target_pairs={{8,0},{9,1},{10,2},{11,3},{12,4},{13,5},{14,6},{15,7},{24,16},{25,... | collective-permute-start | bytes 1572872 | tf_op jit(solution)/shard_map/ppermute | solution.py:43
  36.4 40.2 %collective-permute-start.20 = (bf16[256,1024]{1,0:T(8,128)(2,1)S(1)}, bf16[256,1024]{1,0:T(8,128)(2,1)S(1)}, u32[]{:S(2)}, u32[]{:S(2)}) collective-permute-start(bf16[256,1024]{1,0:T(8,128)(2,1)S(1)} %shard_map.151), channel_id=1, source_target_pairs={{8,0},{9,1},{10,2},{11,3},{12,4},{13,5},{14,6},{15,7},{24,16},{25,... | collective-permute-start | bytes 1572872 | tf_op jit(solution)/shard_map/ppermute | solution.py:43
  37.7 12.9 %collective-permute-start.12 = (bf16[128,256]{1,0:T(8,128)(2,1)S(1)}, bf16[128,256]{1,0:T(8,128)(2,1)S(1)}, u32[]{:S(2)}, u32[]{:S(2)}) collective-permute-start(bf16[128,256]{1,0:T(8,128)(2,1)S(1)} %get-tuple-element.34), channel_id=1, source_target_pairs={{0,16},{16,0},{1,17},{17,1},{2,18},{18,2},{3,19},{19,3},{4,20},{20... | collective-permute-start | bytes 196616 | tf_op jit(solution)/shard_map/ppermute | solution.py:38
  50.6 24.2 %collective-permute-start.15 = (bf16[128,512]{1,0:T(8,128)(2,1)S(1)}, bf16[128,512]{1,0:T(8,128)(2,1)S(1)}, u32[]{:S(2)}, u32[]{:S(2)}) collective-permute-start(bf16[128,512]{1,0:T(8,128)(2,1)S(1)} %get-tuple-element.37.own), channel_id=1, source_target_pairs={{8,0},{9,1},{10,2},{11,3},{12,4},{13,5},{14,6},{15,7},{24,16},{25,... | collective-permute-start | bytes 393224 | tf_op jit(solution)/shard_map/ppermute | solution.py:43
  74.8 1.3 %collective-permute-start.16 = (bf16[128,512]{1,0:T(8,128)(2,1)S(1)}, bf16[128,512]{1,0:T(8,128)(2,1)S(1)}, u32[]{:S(2)}, u32[]{:S(2)}) collective-permute-start(bf16[128,512]{1,0:T(8,128)(2,1)S(1)} %collective-permute-done.15.own), channel_id=1, source_target_pairs={{0,1},{1,0},{2,3},{3,2},{4,5},{5,4},{6,7},{7,6},{8,9},{9,8},{10,11... | collective-permute-start | bytes 393224 | tf_op jit(solution)/shard_map/ppermute | solution.py:38
  74.8 2.9 %collective-permute-start.13 = (bf16[128,256]{1,0:T(8,128)(2,1)S(1)}, bf16[128,256]{1,0:T(8,128)(2,1)S(1)}, u32[]{:S(2)}, u32[]{:S(2)}) collective-permute-start(bf16[128,256]{1,0:T(8,128)(2,1)S(1)} %get-tuple-element.33.refs_2_), channel_id=1, source_target_pairs={{0,1},{1,0},{2,3},{3,2},{4,5},{5,4},{6,7},{7,6},{8,9},{9,8},{10,11... | collective-permute-start | bytes 196616 | tf_op jit(solution)/shard_map/ppermute | solution.py:38
  75.3 2.4 %collective-permute-start.14 = (bf16[128,256]{1,0:T(8,128)(2,1)S(1)}, bf16[128,256]{1,0:T(8,128)(2,1)S(1)}, u32[]{:S(2)}, u32[]{:S(2)}) collective-permute-start(bf16[128,256]{1,0:T(8,128)(2,1)S(1)} %collective-permute-done.12.refs_3_), channel_id=1, source_target_pairs={{0,1},{1,0},{2,3},{3,2},{4,5},{5,4},{6,7},{7,6},{8,9},{9,8},{10,11... | collective-permute-start | bytes 196616 | tf_op jit(solution)/shard_map/ppermute | solution.py:38
  (6 other events, 11.2 us)

commit v2 on v1

--- a/solution.py
+++ b/solution.py
@@ -2,6 +2,7 @@
 
 import jax
 import jax.numpy as jnp
+import numpy as np
 from jax import lax
 from jax.experimental import pallas as pl
 from jax.experimental.pallas import tpu as pltpu
@@ -17,14 +18,14 @@
 AHEAD = 8
 
 
-def call(body, out_shape, args, scratch=(), flops=0, nbytes=0):
+def call(body, out_shape, args, scratch=(), flops=0, nbytes=0, specs=None, limit=40):
     return pl.pallas_call(
         body,
         out_shape=out_shape,
-        in_specs=[pl.BlockSpec(memory_space=VMEM)] * len(args),
+        in_specs=specs or [pl.BlockSpec(memory_space=VMEM)] * len(args),
         out_specs=jax.tree.map(lambda _: pl.BlockSpec(memory_space=VMEM), out_shape),
         scratch_shapes=list(scratch),
-        compiler_params=pltpu.CompilerParams(vmem_limit_bytes=40 * 1024 * 1024),
+        compiler_params=pltpu.CompilerParams(vmem_limit_bytes=limit * 1024 * 1024),
         cost_estimate=pl.CostEstimate(flops=flops, bytes_accessed=nbytes, transcendentals=0),
     )(*args)
 
@@ -40,7 +41,11 @@
 
 def from_next_section(block):
     size = lax.axis_size("pipe")
-    return lax.ppermute(block, "pipe", [(i, i - 1) for i in range(1, size)])
+    return lax.ppermute(block, "pipe", [(i, (i - 1) % size) for i in range(size)])
+
+
+def after(block, *events):
+    return lax.optimization_barrier((block, *events))[0]
 
 
 def head_columns(head):
@@ -52,8 +57,22 @@
     return me // 2, me % 2, me // copies
 
 
-def pack_body(heads, copies, pk, pv, sk, sv, *outs):
+def load_all(sources, targets, arrived):
+    loads = [
+        pltpu.make_async_copy(source, target, arrived.at[i])
+        for i, (source, target) in enumerate(zip(sources, targets))
+    ]
+    for load in loads:
+        load.start()
+    for load in loads:
+        load.wait()
+
+
+def pack_body(heads, copies, *refs):
     z, core, own = my_place(copies)
+    outs, held, arrived = refs[4 : 4 + heads], refs[4 + heads : 8 + heads], refs[-1]
+    load_all(refs[:4], held, arrived)
+    pk, pv, sk, sv = held
     rows = pk.shape[0]
     for apart in range(heads):
         columns = head_columns(own ^ apart)
@@ -61,6 +80,43 @@
         outs[apart][:rows, HD:] = pv[:, columns]
         outs[apart][rows:, :HD] = sk[:, columns]
         outs[apart][rows:, HD:] = sv[:, columns]
+
+
+def ahead_body(kw, vw, weights, arrived):
+    ahead = weights.shape[0] // 2
+    count = arrived.shape[0] // 2
+    rows = ahead // count
+    sources = [array.at[pl.ds(i * rows, rows)] for array in (kw, vw) for i in range(count)]
+    targets = [weights.at[pl.ds(i * rows, rows)] for i in range(2 * count)]
+    load_all(sources, targets, arrived)
+
+
+def table_body(chips, past_rows, span_rows, offset, freq, cos, sin, first):
+    me = lax.axis_index("tensor")
+    z, core = me // 2, me % 2
+    places = 2 * chips
+    start = offset[0, 0]
+    frequencies = freq[...]
+    place = lax.broadcasted_iota(jnp.int32, (places, HD), 0)
+    holder = 2 * (z ^ (place % chips)) + (core ^ (place // chips))
+    row = lax.broadcasted_iota(jnp.int32, (max(past_rows, span_rows), HD), 0)
+    lane = lax.broadcasted_iota(jnp.int32, row.shape, 1)
+
+    def turn(positions):
+        angles = positions.astype(F32) * frequencies
+        return jnp.cos(angles), jnp.sin(angles)
+
+    row_cos, row_sin = turn(row)
+    for low, rows, begin in ((0, past_rows, 0), (places * past_rows, span_rows, start)):
+        place_cos, place_sin = turn(begin + rows * holder)
+        signs = jnp.where(lane[:rows] < HD // 2, -1.0, 1.0)
+        for i in range(places):
+            part = slice(low + i * rows, low + (i + 1) * rows)
+            c, s = place_cos[i : i + 1], place_sin[i : i + 1]
+            cos[part, :] = c * row_cos[:rows] - s * row_sin[:rows]
+            sin[part, :] = (s * row_cos[:rows] + c * row_sin[:rows]) * signs
+            index = rows * (2 * (z ^ (i % chips)) + (core ^ (i // chips))) + row[:rows]
+            first[part, :] = jnp.where(index < start, -1, 1 << 30) if low == 0 else index
 
 
 def attend_body(chips, past_rows, span_rows, q, do, cos, sin, first, *refs):
@@ -116,54 +172,64 @@
         send[half:, columns] = grad[past + quarter :].astype(BF)
 
 
-def chip_sum_body(chips, past_rows, keep, received, *outs):
-    own, sends = outs[0], outs[1:]
+def chip_sum_body(chips, past_rows, keep, received, span_own, span_send, *past):
     half = chips * past_rows
     total = keep[...] + received[...].astype(F32)
-    own[:past_rows, :] = total[:past_rows]
-    own[past_rows:, :] = total[half:]
-    span_part = total[half:].astype(BF)
-    for j in range(1, chips):
-        sends[j - 1][:past_rows, :] = total[j * past_rows : (j + 1) * past_rows].astype(BF)
-        sends[j - 1][past_rows:, :] = span_part
-
-
-def group_sum_body(heads, copies, chips, past_rows, span_rows, peers, *refs):
-    own, received = refs[0], refs[1:chips]
-    dk_past, dv_past, span_grad = refs[chips : chips + 3]
-    sends = refs[chips + 3 : chips + 2 + peers]
-    mine, ordered = refs[chips + 2 + peers :]
+    span_own[...] = total[half:]
+    span_send[...] = total[half:].astype(BF)
+    for j in range(chips):
+        block = total[j * past_rows : (j + 1) * past_rows]
+        past[j][...] = block.astype(past[j].dtype)
+
+
+def sum_span(heads, copies, chips, span_rows, blocks, ordered, span_grad):
     z, core, head = my_place(copies)
-    replica = lax.axis_index("dp")
     per_head = copies // 2
     width = heads * HD
-    share = width // peers
     for apart in range(heads):
-        past_total = None
-        span_total = [None] * chips
+        total = [None] * chips
         for j in range(apart * per_head, (apart + 1) * per_head):
-            block = own if j == 0 else received[j - 1]
-            part = block[:past_rows, :].astype(F32)
-            past_total = part if past_total is None else past_total + part
             for i in range(chips):
-                lower = past_rows + i * span_rows
-                part = block[lower : lower + span_rows, :].astype(F32)
-                span_total[i ^ j] = part if span_total[i ^ j] is None else span_total[i ^ j] + part
-        columns = head_columns(head ^ apart)
-        dk_past[:, columns] = past_total[:, :HD]
-        dv_past[:, columns] = past_total[:, HD:]
+                part = blocks[j][i * span_rows : (i + 1) * span_rows, :].astype(F32)
+                total[i ^ j] = part if total[i ^ j] is None else total[i ^ j] + part
+        key_columns = head_columns(head ^ apart)
         value_columns = pl.ds(pl.multiple_of(width + (head ^ apart) * HD, HD), HD)
         for i in range(chips):
             rows = pl.ds(pl.multiple_of((z ^ i) * span_rows, span_rows), span_rows)
-            rounded = span_total[i].astype(ordered.dtype)
-            ordered[rows, columns] = rounded[:, :HD]
+            rounded = total[i].astype(ordered.dtype)
+            ordered[rows, key_columns] = rounded[:, :HD]
             ordered[rows, value_columns] = rounded[:, HD:]
     span_grad[...] = ordered[...].astype(BF)
+
+
+def span_sum_body(heads, copies, chips, span_rows, peers, *refs):
+    blocks = refs[:chips]
+    span_grad = refs[chips]
+    sends = refs[chips + 1 : chips + peers]
+    mine, ordered = refs[chips + peers :]
+    sum_span(heads, copies, chips, span_rows, blocks, ordered, span_grad)
+    replica = lax.axis_index("dp")
+    width = heads * HD
+    share = width // peers
     for k in range(peers):
         target = mine if k == 0 else sends[k - 1]
         lower = pl.multiple_of((replica ^ k) * share, HD)
         target[:, :share] = span_grad[:, pl.ds(lower, share)]
         target[:, share:] = span_grad[:, pl.ds(pl.multiple_of(width + lower, HD), share)]
+
+
+def past_sum_body(heads, copies, *refs):
+    blocks = refs[:-2]
+    dk_past, dv_past = refs[-2:]
+    z, core, head = my_place(copies)
+    per_head = copies // 2
+    for apart in range(heads):
+        total = blocks[apart * per_head][...].astype(F32)
+        for j in range(apart * per_head + 1, (apart + 1) * per_head):
+            total = total + blocks[j][...].astype(F32)
+        columns = head_columns(head ^ apart)
+        dk_past[:, columns] = total[:, :HD]
+        dv_past[:, columns] = total[:, HD:]
 
 
 def row_type(span_rows):
@@ -180,15 +246,39 @@
         target[pl.ds(lower, span_rows), :] = other[part, :].astype(target.dtype)
 
 
-def input_grad_body(chips, span_rows, own, other, kw, vw, out, rows):
+def late_grad_body(chips, span_rows, own, other, kw, vw, out, rows):
     weave(chips, span_rows, rows, own, other)
     width = kw.shape[1]
     contract_last = (((1,), (1,)), ((), ()))
-    total = lax.dot_general(rows[:, :width].astype(BF), kw[...], contract_last, preferred_element_type=F32)
+    total = lax.dot_general(
+        rows[:, :width].astype(BF), kw[...], contract_last, preferred_element_type=F32
+    )
     total = total + lax.dot_general(
         rows[:, width:].astype(BF), vw[...], contract_last, preferred_element_type=F32
     )
     out[...] = total.astype(BF)
+
+
+def early_grad_body(chips, span_rows, sections, own, other, weights, late, out, rows):
+    weave(chips, span_rows, rows, own, other)
+    ahead, width = weights.shape[0] // 2, weights.shape[1]
+    contract_last = (((1,), (1,)), ((), ()))
+    total = lax.dot_general(
+        rows[:, :width].astype(BF), weights[:ahead], contract_last, preferred_element_type=F32
+    )
+    total = total + lax.dot_general(
+        rows[:, width:].astype(BF), weights[ahead:], contract_last, preferred_element_type=F32
+    )
+    last = lax.axis_index("pipe") == sections - 1
+
+    @pl.when(last)
+    def _():
+        out[...] = jnp.zeros_like(out)
+
+    @pl.when(jnp.logical_not(last))
+    def _():
+        out[:, :ahead] = total.astype(BF)
+        out[:, ahead:] = late[...]
 
 
 def weight_grad_body(chips, span_rows, replicas, *refs):
@@ -208,26 +298,6 @@
         total = product if total is None else total + product
     dkw[...] = total[:, :share]
     dvw[...] = total[:, share:]
-
-
-def key_tables(chips, past_rows, span_rows, offset):
-    me = lax.axis_index("tensor")
-
-    def places(rows):
-        index = lax.broadcasted_iota(jnp.int32, (2 * chips * rows, HD), 0)
-        place = index // rows
-        holder = 2 * ((me // 2) ^ (place % chips)) + ((me % 2) ^ (place // chips))
-        return holder * rows + index % rows
-
-    past = places(past_rows)
-    span = places(span_rows)
-    positions = jnp.concatenate([past, offset + span], axis=0)
-    first = jnp.concatenate([jnp.where(past < offset, -1, 1 << 30), span], axis=0)
-    lane = lax.broadcasted_iota(jnp.int32, positions.shape, 1)
-    inverse_freq = rope_base ** (-2.0 * (lane % (HD // 2)).astype(F32) / HD)
-    angles = positions.astype(F32) * inverse_freq
-    sine = jnp.sin(angles)
-    return jnp.cos(angles), jnp.where(lane < HD // 2, -sine, sine), first
 
 
 def on_device(
@@ -265,16 +335,31 @@
         [shape(past_rows + span_rows, 2 * HD, BF)] * heads,
         (past_keys[0, 0], past_values[0, 0], span_keys[0, 0], span_values[0, 0]),
         nbytes=2 * (past_rows + span_rows) * 2 * width * 2,
+        scratch=[VMEM((past_rows, width), BF)] * 2
+        + [VMEM((span_rows, width), BF)] * 2
+        + [pltpu.SemaphoreType.DMA((4,))],
+        specs=[pl.BlockSpec(memory_space=pltpu.HBM)] * 4,
     )
     per_head = copies // 2
-    pieces = [packed[0]] + [swap(packed[j // per_head], "tensor", 2 * j) for j in range(1, chips)]
+    half_dim = HD // 2
+    freq = np.tile(rope_base ** (-2.0 * np.arange(half_dim) / HD), 2).astype(np.float32)
+    cos, sin, first = call(
+        functools.partial(table_body, chips, past_rows, span_rows),
+        [shape(keys, HD, F32)] * 2 + [shape(keys, HD, jnp.int32)],
+        (offsets, jnp.asarray(freq[None])),
+        nbytes=keys * HD * 12,
+        specs=[pl.BlockSpec(memory_space=pltpu.SMEM), pl.BlockSpec(memory_space=VMEM)],
+    )
+    pieces = [swap(packed[j // per_head], "tensor", 2 * j) for j in range(1, chips)]
+    late_kw, late_vw, cos, *pieces = lax.optimization_barrier(
+        (after(kw, packed[0])[ahead:], after(vw, packed[0])[ahead:], cos, *pieces)
+    )
+    pieces = [packed[0], *pieces]
     pieces = pieces + [swap(piece, "tensor", 1) for piece in pieces]
 
-    normed_from = [normed_rows] + [swap(normed_rows, "dp", k) for k in range(1, replicas)]
-    kw_ahead = from_next_section(kw[:ahead])
-    vw_ahead = from_next_section(vw[:ahead])
-
-    cos, sin, first = key_tables(chips, past_rows, span_rows, offsets[0, 0])
+    weights = from_next_section(jnp.concatenate([kw[:ahead], vw[:ahead]], axis=0))
+    normed_from = [swap(normed_rows, "dp", k) for k in range(1, replicas)]
+
     part_rows = chips * (past_rows + span_rows)
     query_grad, keep, send = call(
         functools.partial(attend_body, chips, past_rows, span_rows),
@@ -296,55 +381,70 @@
         flops=10 * keys * local_heads * span * HD,
         nbytes=4 * span * local_heads * HD * 2,
     )
-    own, *sends = call(
+    span_own, span_send, *past = call(
         functools.partial(chip_sum_body, chips, past_rows),
-        [shape(past_rows + chips * span_rows, 2 * HD, F32)]
-        + [shape(past_rows + chips * span_rows, 2 * HD, BF)] * (chips - 1),
+        [
+            shape(chips * span_rows, 2 * HD, F32),
+            shape(chips * span_rows, 2 * HD, BF),
+            shape(past_rows, 2 * HD, F32),
+        ]
+        + [shape(past_rows, 2 * HD, BF)] * (chips - 1),
         (keep, swap(send, "tensor", 1)),
         nbytes=part_rows * 2 * HD * 8,
     )
-    received = [swap(sends[j - 1], "tensor", 2 * j) for j in range(1, chips)]
-    dk_past, dv_past, span_grad, *shares = call(
-        functools.partial(group_sum_body, heads, copies, chips, past_rows, span_rows, replicas),
-        [
-            shape(past_rows, width, F32),
-            shape(past_rows, width, F32),
-            shape(chips * span_rows, 2 * width, BF),
-        ]
+    received = [swap(span_send, "tensor", 2 * j) for j in range(1, chips)]
+    span_grad, *shares = call(
+        functools.partial(span_sum_body, heads, copies, chips, span_rows, replicas),
+        [shape(chips * span_rows, 2 * width, BF)]
         + [shape(chips * span_rows, 2 * share, BF)] * replicas,
-        (own, *received),
+        (after(span_own, weights), *received),
         scratch=[VMEM((chips * span_rows, 2 * width), row_type(span_rows))],
         nbytes=part_rows * 2 * HD * 8,
     )
+    share_from = [shares[-1]] + [swap(shares[k - 1], "dp", k) for k in range(1, replicas)]
     next_grad = from_next_section(span_grad)
-    share_from = [shares[-1]] + [swap(shares[k - 1], "dp", k) for k in range(1, replicas)]
-
+    past = past[:1] + [swap(after(past[j], next_grad), "tensor", 2 * j) for j in range(1, chips)]
+    dkw, dvw = call(
+        functools.partial(weight_grad_body, chips, span_rows, replicas),
+        [shape(features, share, F32)] * 2,
+        (
+            normed_rows,
+            *normed_from,
+            *share_from,
+            *[swap(part, "tensor", 1) for part in share_from],
+        ),
+        scratch=[VMEM((replicas, span, 2 * share), row_type(span_rows))],
+        flops=4 * span * features * share * replicas,
+        nbytes=features * (2 * span * replicas + 8 * share),
+    )
+    dk_past, dv_past = call(
+        functools.partial(past_sum_body, heads, copies),
+        [shape(past_rows, width, F32)] * 2,
+        past,
+        nbytes=chips * past_rows * 2 * HD * 4,
+    )
     late = call(
-        functools.partial(input_grad_body, chips, span_rows),
+        functools.partial(late_grad_body, chips, span_rows),
         shape(span, features - ahead, BF),
-        (span_grad, swap(span_grad, "tensor", 1), kw[ahead:], vw[ahead:]),
+        (
+            span_grad,
+            swap(span_grad, "tensor", 1),
+            late_kw,
+            late_vw,
+        ),
         scratch=[VMEM((span, 2 * width), row_type(span_rows))],
         flops=4 * span * width * (features - ahead),
         nbytes=(features - ahead) * (4 * width + 2 * span),
     )
-    late = from_next_section(late)
-    early = call(
-        functools.partial(input_grad_body, chips, span_rows),
-        shape(span, ahead, BF),
-        (next_grad, swap(next_grad, "tensor", 1), kw_ahead, vw_ahead),
+    late = from_next_section(after(late, next_grad, *normed_from))
+    section_grad = call(
+        functools.partial(early_grad_body, chips, span_rows, lax.axis_size("pipe")),
+        shape(span, features, BF),
+        (next_grad, swap(next_grad, "tensor", 1), weights, late),
         scratch=[VMEM((span, 2 * width), row_type(span_rows))],
         flops=4 * span * width * ahead,
         nbytes=ahead * (4 * width + 2 * span),
     )
-    dkw, dvw = call(
-        functools.partial(weight_grad_body, chips, span_rows, replicas),
-        [shape(features, share, F32)] * 2,
-        (*normed_from, *share_from, *[swap(part, "tensor", 1) for part in share_from]),
-        scratch=[VMEM((replicas, span, 2 * share), row_type(span_rows))],
-        flops=4 * span * features * share * replicas,
-        nbytes=features * (2 * span * replicas + 8 * share),
-    )
-    section_grad = jnp.concatenate([early, late], axis=1)
     return (
         query_grad[None, None],
         dk_past[None, None],

time: 80.3 us -> 53.2 us (0.66)
  waiting for transfers between devices: 44.3 us -> 19.9 us
  other arithmetic: 3.43 us -> 0.07 us
  local copies, waits for them, and re-layouts: 3.1 us -> 1.41 us
  Pallas kernels: 7.73 us -> 9.33 us
  starting transfers between devices: 19.7 us -> 20.9 us
    ppermute x4 -> x3, waiting for transfers between devices: 22.9 us -> 5.16 us  [from_next_section(): lax.ppermute(block, 'pipe', [(i, (i - 1) % size) for i in range(size)])]
    ppermute x17 -> x20, waiting for transfers between devices: 21.4 us -> 14.7 us  [swap(): return lax.ppermute(block, axis, [(i, i ^ distance) for i in range(size)])]
    unnamed x18 -> x20, local copies, waits for them, and re-layouts: 2.97 us -> 0.06 us
    select_n x2 -> x0, other arithmetic: 2.03 us -> none  [the longest x1 1.56 us: key_tables(): return (jnp.cos(angles), jnp.where(lane < HD // 2, -sine, sine), first)]
    pallas_call x7 -> x9, Pallas kernels: 7.73 us -> 9.33 us  [call(): pl.pallas_call(body, out_shape=out_shape, in_specs=specs or [pl.BlockSpec...]
    slice x1 -> x3, local copies, waits for them, and re-layouts: 0.14 us -> 1.34 us  [the longest x1 1.27 us: on_device(): vw[:ahead]]
    ppermute x17 -> x20, starting transfers between devices: 14.6 us -> 15.7 us  [swap(): return lax.ppermute(block, axis, [(i, i ^ distance) for i in range(size)])]
    broadcast_in_dim x1 -> x0, other arithmetic: 1.06 us -> none  [on_device(): section_grad[None, None]]
  transfers between devices with their start and end apart: 21 -> 23, of which waited for: 11 -> 14; matrix products, arithmetic and copies ran while one was open for 4% -> 0% of each run, Pallas kernels for 2% -> 15%
where the time goes in v2:
time: 53.2 us; the launch traced here: 53.1 us
  starting transfers between devices  20.9 us (39%)
  waiting for transfers between devices  19.9 us (37%)
  Pallas kernels  9.33 us (18%)
  between operations  1.54 us (3%)
  local copies, waits for them, and re-layouts  1.41 us (3%)
    ppermute x20, starting transfers between devices, swap(): return lax.ppermute(block, axis, [(i, i ^ distance) for i in range(size)])  15.7 us
    ppermute x20, waiting for transfers between devices, swap(): return lax.ppermute(block, axis, [(i, i ^ distance) for i in range(size)])  14.7 us
    pallas_call x9, Pallas kernels, call(): pl.pallas_call(body, out_shape=out_shape, in_specs=specs or [pl.BlockSpec...  9.33 us
    ppermute x3, starting transfers between devices, from_next_section(): lax.ppermute(block, 'pipe', [(i, (i - 1) % size) for i in range(size)])  5.19 us
    ppermute x3, waiting for transfers between devices, from_next_section(): lax.ppermute(block, 'pipe', [(i, (i - 1) % size) for i in range(size)])  5.16 us
    slice x1, local copies, waits for them, and re-layouts, on_device(): vw[:ahead]  1.27 us
  transfers between devices with their start and end apart: 23, of which 14 were waited for; matrix products, arithmetic and copies ran while one was open for 0% of the time, Pallas kernels for 15%

profile of v2, /device:TPU:0, one launch (start us, length us, event | category | flops | bytes accessed | tf_op | source)
XLA Modules:
  0.0 53.1 jit_solution(6712232319899970144)
XLA Ops:
  0.6 1.3 %slice_bitcast_fusion = (bf16[1024,256]{1,0:T(8,128)(2,1)S(1)}, bf16[1024,256]{1,0:T(8,128)(2,1)S(1)}) fusion(bf16[1,2048,256]{2,1,0:T(8,128)(2,1)} %param.19, bf16[1,2048,256]{2,1,0:T(8,128)(2,1)} %param.18), kind=kLoop, calls=%fused_computation.1 | loop fusion | bytes 2097152 | tf_op jit(solution)/shard_map/slice | solution.py:360
  2.1 3.0 %collective-permute-start.8 = (bf16[2048,256]{1,0:T(8,128)(2,1)S(1)}, bf16[2048,256]{1,0:T(8,128)(2,1)S(1)}, u32[]{:S(2)}, u32[]{:S(2)}) collective-permute-start(bf16[2048,256]{1,0:T(8,128)(2,1)S(1)} %pad_maximum_fusion), channel_id=1, source_target_pairs={{0,8},{8,0},{1,9},{9,1},{2,10},{10,2},{3,11},{11,3},{4,12},{12,4},... | collective-permute-start | bytes 3145736 | tf_op jit(solution)/shard_map/ppermute | solution.py:44
  5.1 1.5 %collective-permute-start.16 = (bf16[256,2048]{1,0:T(8,128)(2,1)S(1)}, bf16[256,2048]{1,0:T(8,128)(2,1)S(1)}, u32[]{:S(2)}, u32[]{:S(2)}) collective-permute-start(bf16[256,2048]{1,0:T(8,128)(2,1)S(1)} %bitcast.19), channel_id=1, source_target_pairs={{0,16},{16,0},{1,17},{17,1},{2,18},{18,2},{3,19},{19,3},{4,20},{20... | collective-permute-start | bytes 3145736 | tf_op jit(solution)/shard_map/ppermute | solution.py:39
  6.8 1.6 %collective-permute-start = (bf16[96,256]{1,0:T(8,128)(2,1)S(1)}, bf16[96,256]{1,0:T(8,128)(2,1)S(1)}, u32[]{:S(2)}, u32[]{:S(2)}) collective-permute-start(bf16[96,256]{1,0:T(8,128)(2,1)S(1)} %get-tuple-element.40.refs_0_), channel_id=1, source_target_pairs={{0,2},{1,3},{2,0},{3,1},{4,6},{5,7},{6,4},{7,5},{8,10},{9,11},{10,... | collective-permute-start | bytes 147464 | tf_op jit(solution)/shard_map/ppermute | solution.py:39
  8.5 2.6 %collective-permute-start.1 = (bf16[96,256]{1,0:T(8,128)(2,1)S(1)}, bf16[96,256]{1,0:T(8,128)(2,1)S(1)}, u32[]{:S(2)}, u32[]{:S(2)}) collective-permute-start(bf16[96,256]{1,0:T(8,128)(2,1)S(1)} %get-tuple-element.44), channel_id=1, source_target_pairs={{0,4},{1,5},{2,6},{3,7},{4,0},{5,1},{6,2},{7,3},{8,12},{9,13},{10,... | collective-permute-start | bytes 147464 | tf_op jit(solution)/shard_map/ppermute | solution.py:39
  12.4 1.5 %collective-permute-done.1.refs_2_ = bf16[96,256]{1,0:T(8,128)(2,1)S(1)} collective-permute-done((bf16[96,256]{1,0:T(8,128)(2,1)S(1)}, bf16[96,256]{1,0:T(8,128)(2,1)S(1)}, u32[]{:S(2)}, u32[]{:S(2)}) %collective-permute-start.1) | collective-permute-done | bytes 49184 | tf_op jit(solution)/shard_map/ppermute | solution.py:39
  14.0 3.0 %collective-permute-done.2.refs_3_ = bf16[96,256]{1,0:T(8,128)(2,1)S(1)} collective-permute-done((bf16[96,256]{1,0:T(8,128)(2,1)S(1)}, bf16[96,256]{1,0:T(8,128)(2,1)S(1)}, u32[]{:S(2)}, u32[]{:S(2)}) %collective-permute-start.2) | collective-permute-done | bytes 49184 | tf_op jit(solution)/shard_map/ppermute | solution.py:39
  17.5 0.7 %collective-permute-done.4.refs_5_ = bf16[96,256]{1,0:T(8,128)(2,1)S(1)} collective-permute-done((bf16[96,256]{1,0:T(8,128)(2,1)S(1)}, bf16[96,256]{1,0:T(8,128)(2,1)S(1)}, u32[]{:S(2)}, u32[]{:S(2)}) %collective-permute-start.4) | collective-permute-done | bytes 49184 | tf_op jit(solution)/shard_map/ppermute | solution.py:39
  18.7 3.9 %shard_map.156 = (bf16[256,512]{1,0:T(8,128)(2,1)}, f32[384,256]{1,0:T(8,128)S(1)}, bf16[384,256]{1,0:T(8,128)(2,1)S(1)}) custom-call(bf16[256,512]{1,0:T(8,128)(2,1)S(1)} %bitcast.25, bf16[256,512]{1,0:T(8,128)(2,1)S(1)} %bitcast.26, f32[768,128]{1,0:T(8,128)S(1)} %get-tuple-element.45.cos, f32[768,128]{1,0:T(8,128)S(1)} %get-tuple-element.46.sin, ...), custom_call_target="tpu_custom_call" | custom-call | flops 1006632960 | bytes 1048576 | tf_op jit(solution)/shard_map/pallas_call | solution.py:22
  22.8 1.3 %collective-permute-done.7.received = bf16[384,256]{1,0:T(8,128)(2,1)S(1)} collective-permute-done((bf16[384,256]{1,0:T(8,128)(2,1)S(1)}, bf16[384,256]{1,0:T(8,128)(2,1)S(1)}, u32[]{:S(2)}, u32[]{:S(2)}) %collective-permute-start.7) | collective-permute-done | bytes 196640 | tf_op jit(solution)/shard_map/ppermute | solution.py:39
  24.2 1.2 %collective-permute-start.11 = (bf16[128,256]{1,0:T(8,128)(2,1)S(1)}, bf16[128,256]{1,0:T(8,128)(2,1)S(1)}, u32[]{:S(2)}, u32[]{:S(2)}) collective-permute-start(bf16[128,256]{1,0:T(8,128)(2,1)S(1)} %get-tuple-element.58), channel_id=1, source_target_pairs={{0,6},{1,7},{2,4},{3,5},{4,2},{5,3},{6,0},{7,1},{8,14},{9,15},{10,... | collective-permute-start | bytes 196616 | tf_op jit(solution)/shard_map/ppermute | solution.py:39
  25.3 2.3 %collective-permute-start.9 = (bf16[128,256]{1,0:T(8,128)(2,1)S(1)}, bf16[128,256]{1,0:T(8,128)(2,1)S(1)}, u32[]{:S(2)}, u32[]{:S(2)}) collective-permute-start(bf16[128,256]{1,0:T(8,128)(2,1)S(1)} %get-tuple-element.58), channel_id=1, source_target_pairs={{0,2},{1,3},{2,0},{3,1},{4,6},{5,7},{6,4},{7,5},{8,10},{9,11},{10,... | collective-permute-start | bytes 196616 | tf_op jit(solution)/shard_map/ppermute | solution.py:39
  27.6 0.6 %collective-permute-done.8.weights = bf16[2048,256]{1,0:T(8,128)(2,1)S(1)} collective-permute-done((bf16[2048,256]{1,0:T(8,128)(2,1)S(1)}, bf16[2048,256]{1,0:T(8,128)(2,1)S(1)}, u32[]{:S(2)}, u32[]{:S(2)}) %collective-permute-start.8) | collective-permute-done | bytes 1048608 | tf_op jit(solution)/shard_map/ppermute | solution.py:44
  28.2 3.1 %collective-permute-done.10.refs_2_ = bf16[128,256]{1,0:T(8,128)(2,1)S(1)} collective-permute-done((bf16[128,256]{1,0:T(8,128)(2,1)S(1)}, bf16[128,256]{1,0:T(8,128)(2,1)S(1)}, u32[]{:S(2)}, u32[]{:S(2)}) %collective-permute-start.10) | collective-permute-done | bytes 65568 | tf_op jit(solution)/shard_map/ppermute | solution.py:39
  31.3 0.7 %collective-permute-done.9.refs_1_ = bf16[128,256]{1,0:T(8,128)(2,1)S(1)} collective-permute-done((bf16[128,256]{1,0:T(8,128)(2,1)S(1)}, bf16[128,256]{1,0:T(8,128)(2,1)S(1)}, u32[]{:S(2)}, u32[]{:S(2)}) %collective-permute-start.9) | collective-permute-done | bytes 65568 | tf_op jit(solution)/shard_map/ppermute | solution.py:39
  32.2 1.1 %collective-permute-start.12 = (bf16[128,512]{1,0:T(8,128)(2,1)S(1)}, bf16[128,512]{1,0:T(8,128)(2,1)S(1)}, u32[]{:S(2)}, u32[]{:S(2)}) collective-permute-start(bf16[128,512]{1,0:T(8,128)(2,1)S(1)} %get-tuple-element.59.own), channel_id=1, source_target_pairs={{0,8},{8,0},{1,9},{9,1},{2,10},{10,2},{3,11},{11,3},{4,12},{12,4},... | collective-permute-start | bytes 393224 | tf_op jit(solution)/shard_map/ppermute | solution.py:44
  34.0 4.1 %collective-permute-done.12.own = bf16[128,512]{1,0:T(8,128)(2,1)S(1)} collective-permute-done((bf16[128,512]{1,0:T(8,128)(2,1)S(1)}, bf16[128,512]{1,0:T(8,128)(2,1)S(1)}, u32[]{:S(2)}, u32[]{:S(2)}) %collective-permute-start.12) | collective-permute-done | bytes 131104 | tf_op jit(solution)/shard_map/ppermute | solution.py:44
  38.1 1.1 %collective-permute-start.22 = (bf16[256,1024]{1,0:T(8,128)(2,1)S(1)}, bf16[256,1024]{1,0:T(8,128)(2,1)S(1)}, u32[]{:S(2)}, u32[]{:S(2)}) collective-permute-start(bf16[256,1024]{1,0:T(8,128)(2,1)S(1)} %shard_map.161), channel_id=1, source_target_pairs={{0,8},{8,0},{1,9},{9,1},{2,10},{10,2},{3,11},{11,3},{4,12},{12,4},... | collective-permute-start | bytes 1572872 | tf_op jit(solution)/shard_map/ppermute | solution.py:44
  40.2 3.2 %collective-permute-done.17.refs_3_ = bf16[128,256]{1,0:T(8,128)(2,1)S(1)} collective-permute-done((bf16[128,256]{1,0:T(8,128)(2,1)S(1)}, bf16[128,256]{1,0:T(8,128)(2,1)S(1)}, u32[]{:S(2)}, u32[]{:S(2)}) %collective-permute-start.17) | collective-permute-done | bytes 65568 | tf_op jit(solution)/shard_map/ppermute | solution.py:39
  43.4 1.7 %collective-permute-start.15 = (bf16[64,256]{1,0:T(8,128)(2,1)S(1)}, bf16[64,256]{1,0:T(8,128)(2,1)S(1)}, u32[]{:S(2)}, u32[]{:S(2)}) collective-permute-start(bf16[64,256]{1,0:T(8,128)(2,1)S(1)} %get-tuple-element.64), channel_id=1, source_target_pairs={{0,6},{1,7},{2,4},{3,5},{4,2},{5,3},{6,0},{7,1},{8,14},{9,15},{10,... | collective-permute-start | bytes 98312 | tf_op jit(solution)/shard_map/ppermute | solution.py:39
  45.5 2.4 %collective-permute-start.13 = (bf16[64,256]{1,0:T(8,128)(2,1)S(1)}, bf16[64,256]{1,0:T(8,128)(2,1)S(1)}, u32[]{:S(2)}, u32[]{:S(2)}) collective-permute-start(bf16[64,256]{1,0:T(8,128)(2,1)S(1)} %get-tuple-element.60), channel_id=1, source_target_pairs={{0,2},{1,3},{2,0},{3,1},{4,6},{5,7},{6,4},{7,5},{8,10},{9,11},{10,... | collective-permute-start | bytes 98312 | tf_op jit(solution)/shard_map/ppermute | solution.py:39
  47.8 2.1 %shard_map.160 = (f32[2048,128]{1,0:T(8,128)}, f32[2048,128]{1,0:T(8,128)}) custom-call(bf16[256,2048]{1,0:T(8,128)(2,1)S(1)} %bitcast.20, bf16[256,2048]{1,0:T(8,128)(2,1)S(1)} %collective-permute-done.16.refs_1_, bf16[128,256]{1,0:T(8,128)(2,1)S(1)} %get-tuple-element.67.refs_2_, bf16[128,256]{1,0:T(8,128)(2,1)S(1)} %collective-permute-done.17.refs_3_, ...), custom_call_target="tpu_custom_call" | custom-call | flops 536870912 | bytes 4194304 | tf_op jit(solution)/shard_map/pallas_call | solution.py:22
  50.4 0.7 %shard_map.159 = (f32[64,256]{1,0:T(8,128)}, f32[64,256]{1,0:T(8,128)}) custom-call(f32[64,256]{1,0:T(8,128)S(1)} %get-tuple-element.54.refs_0_, bf16[64,256]{1,0:T(8,128)(2,1)S(1)} %collective-permute-done.13.refs_1_, bf16[64,256]{1,0:T(8,128)(2,1)S(1)} %collective-permute-done.14.refs_2_, bf16[64,256]{1,0:T(8,128)(2,1)S(1)} %collective-permute-done.15.refs_3_), custom_call_target="tpu_custom_call" | custom-call | bytes 262144 | tf_op jit(solution)/shard_map/pallas_call | solution.py:22
  51.6 1.5 %shard_map.162 = bf16[256,2048]{1,0:T(8,128)(2,1)} custom-call(bf16[128,512]{1,0:T(8,128)(2,1)S(1)} %collective-permute-done.12.own, bf16[128,512]{1,0:T(8,128)(2,1)S(1)} %collective-permute-done.20.other, bf16[2048,256]{1,0:T(8,128)(2,1)S(1)} %collective-permute-done.8.weights, bf16[256,1024]{1,0:T(8,128)(2,1)S(1)} %collective-permute-done.22.late), custom_call_target="tpu_custom_call" | custom-call | flops 268435456 | bytes 1572864 | tf_op jit(solution)/shard_map/pallas_call | solution.py:22
  (55 shorter events, 5.3 us)
Async XLA Ops:
  2.0 9.3 %copy-start.8 = (bf16[1,2048,256]{2,1,0:T(8,128)(2,1)S(1)}, bf16[1,2048,256]{2,1,0:T(8,128)(2,1)}, u32[]{:S(2)}) copy-start(bf16[1,2048,256]{2,1,0:T(8,128)(2,1)} %param.18) | copy-start | bytes 3145732
  2.1 26.2 %collective-permute-start.8 = (bf16[2048,256]{1,0:T(8,128)(2,1)S(1)}, bf16[2048,256]{1,0:T(8,128)(2,1)S(1)}, u32[]{:S(2)}, u32[]{:S(2)}) collective-permute-start(bf16[2048,256]{1,0:T(8,128)(2,1)S(1)} %pad_maximum_fusion), channel_id=1, source_target_pairs={{0,8},{8,0},{1,9},{9,1},{2,10},{10,2},{3,11},{11,3},{4,12},{12,4},... | collective-permute-start | bytes 3145736 | tf_op jit(solution)/shard_map/ppermute | solution.py:44
  5.1 28.9 %collective-permute-start.16 = (bf16[256,2048]{1,0:T(8,128)(2,1)S(1)}, bf16[256,2048]{1,0:T(8,128)(2,1)S(1)}, u32[]{:S(2)}, u32[]{:S(2)}) collective-permute-start(bf16[256,2048]{1,0:T(8,128)(2,1)S(1)} %bitcast.19), channel_id=1, source_target_pairs={{0,16},{16,0},{1,17},{17,1},{2,18},{18,2},{3,19},{19,3},{4,20},{20... | collective-permute-start | bytes 3145736 | tf_op jit(solution)/shard_map/ppermute | solution.py:39
  6.8 4.5 %collective-permute-start = (bf16[96,256]{1,0:T(8,128)(2,1)S(1)}, bf16[96,256]{1,0:T(8,128)(2,1)S(1)}, u32[]{:S(2)}, u32[]{:S(2)}) collective-permute-start(bf16[96,256]{1,0:T(8,128)(2,1)S(1)} %get-tuple-element.40.refs_0_), channel_id=1, source_target_pairs={{0,2},{1,3},{2,0},{3,1},{4,6},{5,7},{6,4},{7,5},{8,10},{9,11},{10,... | collective-permute-start | bytes 147464 | tf_op jit(solution)/shard_map/ppermute | solution.py:39
  8.5 5.5 %collective-permute-start.1 = (bf16[96,256]{1,0:T(8,128)(2,1)S(1)}, bf16[96,256]{1,0:T(8,128)(2,1)S(1)}, u32[]{:S(2)}, u32[]{:S(2)}) collective-permute-start(bf16[96,256]{1,0:T(8,128)(2,1)S(1)} %get-tuple-element.44), channel_id=1, source_target_pairs={{0,4},{1,5},{2,6},{3,7},{4,0},{5,1},{6,2},{7,3},{8,12},{9,13},{10,... | collective-permute-start | bytes 147464 | tf_op jit(solution)/shard_map/ppermute | solution.py:39
  11.0 5.9 %collective-permute-start.2 = (bf16[96,256]{1,0:T(8,128)(2,1)S(1)}, bf16[96,256]{1,0:T(8,128)(2,1)S(1)}, u32[]{:S(2)}, u32[]{:S(2)}) collective-permute-start(bf16[96,256]{1,0:T(8,128)(2,1)S(1)} %get-tuple-element.44), channel_id=1, source_target_pairs={{0,6},{1,7},{2,4},{3,5},{4,2},{5,3},{6,0},{7,1},{8,14},{9,15},{10,... | collective-permute-start | bytes 147464 | tf_op jit(solution)/shard_map/ppermute | solution.py:39
  11.3 6.2 %collective-permute-start.3 = (bf16[96,256]{1,0:T(8,128)(2,1)S(1)}, bf16[96,256]{1,0:T(8,128)(2,1)S(1)}, u32[]{:S(2)}, u32[]{:S(2)}) collective-permute-start(bf16[96,256]{1,0:T(8,128)(2,1)S(1)} %get-tuple-element.40.refs_0_), channel_id=1, source_target_pairs={{0,1},{1,0},{2,3},{3,2},{4,5},{5,4},{6,7},{7,6},{8,9},{9,8},{10,11... | collective-permute-start | bytes 147464 | tf_op jit(solution)/shard_map/ppermute | solution.py:39
  16.9 1.2 %collective-permute-start.4 = (bf16[96,256]{1,0:T(8,128)(2,1)S(1)}, bf16[96,256]{1,0:T(8,128)(2,1)S(1)}, u32[]{:S(2)}, u32[]{:S(2)}) collective-permute-start(bf16[96,256]{1,0:T(8,128)(2,1)S(1)} %collective-permute-done.refs_1_), channel_id=1, source_target_pairs={{0,1},{1,0},{2,3},{3,2},{4,5},{5,4},{6,7},{7,6},{8,9},{9,8},{10,11... | collective-permute-start | bytes 147464 | tf_op jit(solution)/shard_map/ppermute | solution.py:39
  16.9 1.4 %collective-permute-start.5 = (bf16[96,256]{1,0:T(8,128)(2,1)S(1)}, bf16[96,256]{1,0:T(8,128)(2,1)S(1)}, u32[]{:S(2)}, u32[]{:S(2)}) collective-permute-start(bf16[96,256]{1,0:T(8,128)(2,1)S(1)} %collective-permute-done.1.refs_2_), channel_id=1, source_target_pairs={{0,1},{1,0},{2,3},{3,2},{4,5},{5,4},{6,7},{7,6},{8,9},{9,8},{10,11... | collective-permute-start | bytes 147464 | tf_op jit(solution)/shard_map/ppermute | solution.py:39
  17.4 1.2 %collective-permute-start.6 = (bf16[96,256]{1,0:T(8,128)(2,1)S(1)}, bf16[96,256]{1,0:T(8,128)(2,1)S(1)}, u32[]{:S(2)}, u32[]{:S(2)}) collective-permute-start(bf16[96,256]{1,0:T(8,128)(2,1)S(1)} %collective-permute-done.2.refs_3_), channel_id=1, source_target_pairs={{0,1},{1,0},{2,3},{3,2},{4,5},{5,4},{6,7},{7,6},{8,9},{9,8},{10,11... | collective-permute-start | bytes 147464 | tf_op jit(solution)/shard_map/ppermute | solution.py:39
  22.6 1.4 %collective-permute-start.7 = (bf16[384,256]{1,0:T(8,128)(2,1)S(1)}, bf16[384,256]{1,0:T(8,128)(2,1)S(1)}, u32[]{:S(2)}, u32[]{:S(2)}) collective-permute-start(bf16[384,256]{1,0:T(8,128)(2,1)S(1)} %get-tuple-element.53), channel_id=1, source_target_pairs={{0,1},{1,0},{2,3},{3,2},{4,5},{5,4},{6,7},{7,6},{8,9},{9,8},{10,11... | collective-permute-start | bytes 589832 | tf_op jit(solution)/shard_map/ppermute | solution.py:39
  24.1 7.2 %collective-permute-start.10 = (bf16[128,256]{1,0:T(8,128)(2,1)S(1)}, bf16[128,256]{1,0:T(8,128)(2,1)S(1)}, u32[]{:S(2)}, u32[]{:S(2)}) collective-permute-start(bf16[128,256]{1,0:T(8,128)(2,1)S(1)} %get-tuple-element.58), channel_id=1, source_target_pairs={{0,4},{1,5},{2,6},{3,7},{4,0},{5,1},{6,2},{7,3},{8,12},{9,13},{10,... | collective-permute-start | bytes 196616 | tf_op jit(solution)/shard_map/ppermute | solution.py:39
  24.2 7.2 %collective-permute-start.11 = (bf16[128,256]{1,0:T(8,128)(2,1)S(1)}, bf16[128,256]{1,0:T(8,128)(2,1)S(1)}, u32[]{:S(2)}, u32[]{:S(2)}) collective-permute-start(bf16[128,256]{1,0:T(8,128)(2,1)S(1)} %get-tuple-element.58), channel_id=1, source_target_pairs={{0,6},{1,7},{2,4},{3,5},{4,2},{5,3},{6,0},{7,1},{8,14},{9,15},{10,... | collective-permute-start | bytes 196616 | tf_op jit(solution)/shard_map/ppermute | solution.py:39
  25.3 6.7 %collective-permute-start.9 = (bf16[128,256]{1,0:T(8,128)(2,1)S(1)}, bf16[128,256]{1,0:T(8,128)(2,1)S(1)}, u32[]{:S(2)}, u32[]{:S(2)}) collective-permute-start(bf16[128,256]{1,0:T(8,128)(2,1)S(1)} %get-tuple-element.58), channel_id=1, source_target_pairs={{0,2},{1,3},{2,0},{3,1},{4,6},{5,7},{6,4},{7,5},{8,10},{9,11},{10,... | collective-permute-start | bytes 196616 | tf_op jit(solution)/shard_map/ppermute | solution.py:39
  32.1 1.4 %collective-permute-start.21 = (bf16[128,512]{1,0:T(8,128)(2,1)S(1)}, bf16[128,512]{1,0:T(8,128)(2,1)S(1)}, u32[]{:S(2)}, u32[]{:S(2)}) collective-permute-start(bf16[128,512]{1,0:T(8,128)(2,1)S(1)} %get-tuple-element.59.own), channel_id=1, source_target_pairs={{0,1},{1,0},{2,3},{3,2},{4,5},{5,4},{6,7},{7,6},{8,9},{9,8},{10,11... | collective-permute-start | bytes 393224 | tf_op jit(solution)/shard_map/ppermute | solution.py:39
  32.2 5.9 %collective-permute-start.12 = (bf16[128,512]{1,0:T(8,128)(2,1)S(1)}, bf16[128,512]{1,0:T(8,128)(2,1)S(1)}, u32[]{:S(2)}, u32[]{:S(2)}) collective-permute-start(bf16[128,512]{1,0:T(8,128)(2,1)S(1)} %get-tuple-element.59.own), channel_id=1, source_target_pairs={{0,8},{8,0},{1,9},{9,1},{2,10},{10,2},{3,11},{11,3},{4,12},{12,4},... | collective-permute-start | bytes 393224 | tf_op jit(solution)/shard_map/ppermute | solution.py:44
  38.1 13.5 %collective-permute-start.22 = (bf16[256,1024]{1,0:T(8,128)(2,1)S(1)}, bf16[256,1024]{1,0:T(8,128)(2,1)S(1)}, u32[]{:S(2)}, u32[]{:S(2)}) collective-permute-start(bf16[256,1024]{1,0:T(8,128)(2,1)S(1)} %shard_map.161), channel_id=1, source_target_pairs={{0,8},{8,0},{1,9},{9,1},{2,10},{10,2},{3,11},{11,3},{4,12},{12,4},... | collective-permute-start | bytes 1572872 | tf_op jit(solution)/shard_map/ppermute | solution.py:44
  39.1 4.3 %collective-permute-start.17 = (bf16[128,256]{1,0:T(8,128)(2,1)S(1)}, bf16[128,256]{1,0:T(8,128)(2,1)S(1)}, u32[]{:S(2)}, u32[]{:S(2)}) collective-permute-start(bf16[128,256]{1,0:T(8,128)(2,1)S(1)} %get-tuple-element.68), channel_id=1, source_target_pairs={{0,16},{16,0},{1,17},{17,1},{2,18},{18,2},{3,19},{19,3},{4,20},{20... | collective-permute-start | bytes 196616 | tf_op jit(solution)/shard_map/ppermute | solution.py:39
  39.7 11.4 %collective-permute-start.20 = (bf16[128,512]{1,0:T(8,128)(2,1)S(1)}, bf16[128,512]{1,0:T(8,128)(2,1)S(1)}, u32[]{:S(2)}, u32[]{:S(2)}) collective-permute-start(bf16[128,512]{1,0:T(8,128)(2,1)S(1)} %collective-permute-done.12.own), channel_id=1, source_target_pairs={{0,1},{1,0},{2,3},{3,2},{4,5},{5,4},{6,7},{7,6},{8,9},{9,8},{10,11... | collective-permute-start | bytes 393224 | tf_op jit(solution)/shard_map/ppermute | solution.py:39
  39.7 5.5 %collective-permute-start.18 = (bf16[128,256]{1,0:T(8,128)(2,1)S(1)}, bf16[128,256]{1,0:T(8,128)(2,1)S(1)}, u32[]{:S(2)}, u32[]{:S(2)}) collective-permute-start(bf16[128,256]{1,0:T(8,128)(2,1)S(1)} %get-tuple-element.67.refs_2_), channel_id=1, source_target_pairs={{0,1},{1,0},{2,3},{3,2},{4,5},{5,4},{6,7},{7,6},{8,9},{9,8},{10,11... | collective-permute-start | bytes 196616 | tf_op jit(solution)/shard_map/ppermute | solution.py:39
  43.4 2.0 %collective-permute-start.19 = (bf16[128,256]{1,0:T(8,128)(2,1)S(1)}, bf16[128,256]{1,0:T(8,128)(2,1)S(1)}, u32[]{:S(2)}, u32[]{:S(2)}) collective-permute-start(bf16[128,256]{1,0:T(8,128)(2,1)S(1)} %collective-permute-done.17.refs_3_), channel_id=1, source_target_pairs={{0,1},{1,0},{2,3},{3,2},{4,5},{5,4},{6,7},{7,6},{8,9},{9,8},{10,11... | collective-permute-start | bytes 196616 | tf_op jit(solution)/shard_map/ppermute | solution.py:39
  43.4 6.5 %collective-permute-start.15 = (bf16[64,256]{1,0:T(8,128)(2,1)S(1)}, bf16[64,256]{1,0:T(8,128)(2,1)S(1)}, u32[]{:S(2)}, u32[]{:S(2)}) collective-permute-start(bf16[64,256]{1,0:T(8,128)(2,1)S(1)} %get-tuple-element.64), channel_id=1, source_target_pairs={{0,6},{1,7},{2,4},{3,5},{4,2},{5,3},{6,0},{7,1},{8,14},{9,15},{10,... | collective-permute-start | bytes 98312 | tf_op jit(solution)/shard_map/ppermute | solution.py:39
  45.2 5.3 %collective-permute-start.14 = (bf16[64,256]{1,0:T(8,128)(2,1)S(1)}, bf16[64,256]{1,0:T(8,128)(2,1)S(1)}, u32[]{:S(2)}, u32[]{:S(2)}) collective-permute-start(bf16[64,256]{1,0:T(8,128)(2,1)S(1)} %get-tuple-element.62), channel_id=1, source_target_pairs={{0,4},{1,5},{2,6},{3,7},{4,0},{5,1},{6,2},{7,3},{8,12},{9,13},{10,... | collective-permute-start | bytes 98312 | tf_op jit(solution)/shard_map/ppermute | solution.py:39
  45.5 5.0 %collective-permute-start.13 = (bf16[64,256]{1,0:T(8,128)(2,1)S(1)}, bf16[64,256]{1,0:T(8,128)(2,1)S(1)}, u32[]{:S(2)}, u32[]{:S(2)}) collective-permute-start(bf16[64,256]{1,0:T(8,128)(2,1)S(1)} %get-tuple-element.60), channel_id=1, source_target_pairs={{0,2},{1,3},{2,0},{3,1},{4,6},{5,7},{6,4},{7,5},{8,10},{9,11},{10,... | collective-permute-start | bytes 98312 | tf_op jit(solution)/shard_map/ppermute | solution.py:39
  (9 other events, 46.7 us)

commit v3 on v2

--- a/solution.py
+++ b/solution.py
@@ -15,7 +15,7 @@
 F32 = jnp.float32
 VMEM = pltpu.VMEM
 
-AHEAD = 8
+AHEAD, SHARED = 6, 5
 
 
 def call(body, out_shape, args, scratch=(), flops=0, nbytes=0, specs=None, limit=40):
@@ -146,15 +146,24 @@
     start_key = jnp.concatenate([first[...]] * (span // HD), axis=1)
     visible = start_key <= row
     contract_last = (((1,), (1,)), ((), ()))
+
+    def products(h):
+        columns = slice(h * span, (h + 1) * span)
+        s = lax.dot_general(kr[...], qs[columns, :], contract_last, preferred_element_type=F32)
+        dp = lax.dot_general(v[...], ds[columns, :], contract_last, preferred_element_type=F32)
+        return s, dp
+
+    following = products(0)
     for h in range(heads):
         columns = slice(h * span, (h + 1) * span)
-        s = lax.dot_general(kr[...], qs[columns, :], contract_last, preferred_element_type=F32)
+        s, dp = following
+        if h + 1 < heads:
+            following = products(h + 1)
         s = jnp.where(visible, s * scale, neg_large)
         e = jnp.exp(s - jnp.max(s, axis=0, keepdims=True))
         a = e * (1.0 / jnp.sum(e, axis=0, keepdims=True))
         a_bf = a.astype(BF)
         at[:, columns] = a_bf
-        dp = lax.dot_general(v[...], ds[columns, :], contract_last, preferred_element_type=F32)
         delta = jnp.sum(a_bf.astype(F32) * dp, axis=0, keepdims=True)
         d = (a * (dp - delta)).astype(BF)
         dst[:, columns] = d
@@ -205,14 +214,12 @@
 def span_sum_body(heads, copies, chips, span_rows, peers, *refs):
     blocks = refs[:chips]
     span_grad = refs[chips]
-    sends = refs[chips + 1 : chips + peers]
-    mine, ordered = refs[chips + peers :]
+    sends, ordered = refs[chips + 1 : -1], refs[-1]
     sum_span(heads, copies, chips, span_rows, blocks, ordered, span_grad)
     replica = lax.axis_index("dp")
     width = heads * HD
     share = width // peers
-    for k in range(peers):
-        target = mine if k == 0 else sends[k - 1]
+    for k, target in enumerate(sends, 1):
         lower = pl.multiple_of((replica ^ k) * share, HD)
         target[:, :share] = span_grad[:, pl.ds(lower, share)]
         target[:, share:] = span_grad[:, pl.ds(pl.multiple_of(width + lower, HD), share)]
@@ -259,17 +266,12 @@
     out[...] = total.astype(BF)
 
 
-def early_grad_body(chips, span_rows, sections, own, other, weights, late, out, rows):
-    weave(chips, span_rows, rows, own, other)
-    ahead, width = weights.shape[0] // 2, weights.shape[1]
+def early_grad_body(chips, span_rows, sections, ahead, own, other, weights, late, *refs):
+    more, (out, rows) = refs[:-2], refs[-2:]
+    last = lax.axis_index("pipe") == sections - 1
+    width = weights.shape[1]
+    ready = out.shape[1] - late.shape[1]
     contract_last = (((1,), (1,)), ((), ()))
-    total = lax.dot_general(
-        rows[:, :width].astype(BF), weights[:ahead], contract_last, preferred_element_type=F32
-    )
-    total = total + lax.dot_general(
-        rows[:, width:].astype(BF), weights[ahead:], contract_last, preferred_element_type=F32
-    )
-    last = lax.axis_index("pipe") == sections - 1
 
     @pl.when(last)
     def _():
@@ -277,23 +279,45 @@
 
     @pl.when(jnp.logical_not(last))
     def _():
+        weave(chips, span_rows, rows, own, other)
+        kind = lax.axis_index("dp") if more else 0
+
+        def product(which, block):
+            columns = pl.ds(pl.multiple_of(which * width, HD), width)
+            grad = rows[:, columns].astype(BF)
+            return lax.dot_general(grad, block, contract_last, preferred_element_type=F32)
+
+        total = product(kind, weights[:ahead]) + product(1 - kind, weights[ready:])
         out[:, :ahead] = total.astype(BF)
-        out[:, ahead:] = late[...]
+        if more:
+            total = product(kind, weights[ahead:ready]) + product(1 - kind, more[0][...])
+            out[:, ahead:ready] = total.astype(BF)
+        out[:, ready:] = late[...]
 
 
 def weight_grad_body(chips, span_rows, replicas, *refs):
+    count = replicas - 1
     normed = refs[:replicas]
-    own = refs[replicas : 2 * replicas]
-    other = refs[2 * replicas : 3 * replicas]
-    dkw, dvw, rows = refs[3 * replicas :]
+    span_grad, other_grad = refs[replicas : replicas + 2]
+    own = refs[replicas + 2 : replicas + 2 + count]
+    other = refs[replicas + 2 + count : replicas + 2 + 2 * count]
+    dkw, dvw, mine, rows = refs[replicas + 2 + 2 * count :]
     share = dkw.shape[1]
+    width = span_grad.shape[1] // 2
+    weave(chips, span_rows, mine, span_grad, other_grad)
+    lower = pl.multiple_of(lax.axis_index("dp") * share, HD)
+    grads = [
+        jnp.concatenate(
+            [mine[:, pl.ds(half * width + lower, share)].astype(BF) for half in range(2)], axis=1
+        )
+    ]
+    for k in range(count):
+        weave(chips, span_rows, rows.at[k], own[k], other[k])
+        grads.append(rows[k].astype(BF))
     contract_first = (((0,), (0,)), ((), ()))
     total = None
-    for k in range(replicas):
-        weave(chips, span_rows, rows.at[k], own[k], other[k])
-        product = lax.dot_general(
-            normed[k][...], rows[k].astype(BF), contract_first, preferred_element_type=F32
-        )
+    for block, grad in zip(normed, grads):
+        product = lax.dot_general(block[...], grad, contract_first, preferred_element_type=F32)
         product = product.astype(BF).astype(F32)
         total = product if total is None else total + product
     dkw[...] = total[:, :share]
@@ -328,7 +352,10 @@
 
     normed_rows = normed[0, 0]
     kw, vw = key_weight[0], value_weight[0]
-    ahead = features * AHEAD // 16
+    ahead, shared = features * AHEAD // 16, features * SHARED // 16
+    if replicas != 2:
+        ahead, shared = ahead + shared // 2, 0
+    late_start = ahead + shared
 
     packed = call(
         functools.partial(pack_body, heads, copies),
@@ -352,12 +379,19 @@
     )
     pieces = [swap(packed[j // per_head], "tensor", 2 * j) for j in range(1, chips)]
     late_kw, late_vw, cos, *pieces = lax.optimization_barrier(
-        (after(kw, packed[0])[ahead:], after(vw, packed[0])[ahead:], cos, *pieces)
+        (after(kw, packed[0])[late_start:], after(vw, packed[0])[late_start:], cos, *pieces)
     )
     pieces = [packed[0], *pieces]
     pieces = pieces + [swap(piece, "tensor", 1) for piece in pieces]
 
-    weights = from_next_section(jnp.concatenate([kw[:ahead], vw[:ahead]], axis=0))
+    ready = [kw[:late_start], vw[:ahead]]
+    if shared:
+        first_half = lax.axis_index("dp") == 0
+        ready = [
+            jnp.where(first_half, kw[:late_start], vw[:late_start]),
+            jnp.where(first_half, vw[:ahead], kw[:ahead]),
+        ]
+    weights = from_next_section(jnp.concatenate(ready, axis=0))
     normed_from = [swap(normed_rows, "dp", k) for k in range(1, replicas)]
 
     part_rows = chips * (past_rows + span_rows)
@@ -396,24 +430,30 @@
     span_grad, *shares = call(
         functools.partial(span_sum_body, heads, copies, chips, span_rows, replicas),
         [shape(chips * span_rows, 2 * width, BF)]
-        + [shape(chips * span_rows, 2 * share, BF)] * replicas,
-        (after(span_own, weights), *received),
+        + [shape(chips * span_rows, 2 * share, BF)] * (replicas - 1),
+        (after(span_own, weights, *normed_from), *received),
         scratch=[VMEM((chips * span_rows, 2 * width), row_type(span_rows))],
         nbytes=part_rows * 2 * HD * 8,
     )
-    share_from = [shares[-1]] + [swap(shares[k - 1], "dp", k) for k in range(1, replicas)]
+    share_from = [swap(block, "dp", k + 1) for k, block in enumerate(shares)]
     next_grad = from_next_section(span_grad)
-    past = past[:1] + [swap(after(past[j], next_grad), "tensor", 2 * j) for j in range(1, chips)]
+    past = past[:1] + [swap(after(past[j], span_grad if j <= 2 else next_grad), "tensor", 2 * j) for j in range(1, chips)]
+    other_grad = swap(span_grad, "tensor", 1)
     dkw, dvw = call(
         functools.partial(weight_grad_body, chips, span_rows, replicas),
         [shape(features, share, F32)] * 2,
         (
             normed_rows,
             *normed_from,
+            span_grad,
+            other_grad,
             *share_from,
-            *[swap(part, "tensor", 1) for part in share_from],
+            *[swap(after(part, *normed_from), "tensor", 1) for part in share_from],
         ),
-        scratch=[VMEM((replicas, span, 2 * share), row_type(span_rows))],
+        scratch=[
+            VMEM((span, 2 * width), row_type(span_rows)),
+            VMEM((replicas - 1, span, 2 * share), row_type(span_rows)),
+        ],
         flops=4 * span * features * share * replicas,
         nbytes=features * (2 * span * replicas + 8 * share),
     )
@@ -425,25 +465,26 @@
     )
     late = call(
         functools.partial(late_grad_body, chips, span_rows),
-        shape(span, features - ahead, BF),
+        shape(span, features - late_start, BF),
         (
             span_grad,
-            swap(span_grad, "tensor", 1),
+            other_grad,
             late_kw,
             late_vw,
         ),
         scratch=[VMEM((span, 2 * width), row_type(span_rows))],
-        flops=4 * span * width * (features - ahead),
-        nbytes=(features - ahead) * (4 * width + 2 * span),
-    )
-    late = from_next_section(after(late, next_grad, *normed_from))
+        flops=4 * span * width * (features - late_start),
+        nbytes=(features - late_start) * (4 * width + 2 * span),
+    )
+    more = [swap(after(weights, *share_from)[ahead:late_start], "dp", 1)] if shared else []
+    late = from_next_section(after(late, next_grad, past[1], past[2], *share_from))
     section_grad = call(
-        functools.partial(early_grad_body, chips, span_rows, lax.axis_size("pipe")),
+        functools.partial(early_grad_body, chips, span_rows, lax.axis_size("pipe"), ahead),
         shape(span, features, BF),
-        (next_grad, swap(next_grad, "tensor", 1), weights, late),
+        (next_grad, swap(next_grad, "tensor", 1), weights, late, *more),
         scratch=[VMEM((span, 2 * width), row_type(span_rows))],
-        flops=4 * span * width * ahead,
-        nbytes=ahead * (4 * width + 2 * span),
+        flops=4 * span * width * late_start,
+        nbytes=late_start * (4 * width + 2 * span),
     )
     return (
         query_grad[None, None],

time: 53.2 us -> 50.5 us (0.949)
  waiting for transfers between devices: 19.9 us -> 14.6 us
  starting transfers between devices: 20.9 us -> 23.1 us
  other arithmetic: 0.07 us -> 1.67 us
  local copies, waits for them, and re-layouts: 1.41 us -> 0.52 us
    ppermute x3, waiting for transfers between devices: 5.16 us -> 0.76 us  [from_next_section(): lax.ppermute(block, 'pipe', [(i, (i - 1) % size) for i in range(size)])]
    ppermute x20, starting transfers between devices: 15.7 us -> 18.3 us  [swap(): return lax.ppermute(block, axis, [(i, i ^ distance) for i in range(size)])]
    select_n x0 -> x2, other arithmetic: none -> 1.59 us  [the longest x1 1.55 us: on_device(): jnp.where(first_half, kw[:late_start], vw[:late_start])]
    slice x3, local copies, waits for them, and re-layouts: 1.34 us -> 0.07 us  [the longest x1 0.02 us: on_device(): after(vw, packed[0])[late_start:]]
    ppermute x20, waiting for transfers between devices: 14.7 us -> 13.9 us  [swap(): return lax.ppermute(block, axis, [(i, i ^ distance) for i in range(size)])]
  transfers between devices with their start and end apart: 23 -> 23, of which waited for: 14 -> 13; matrix products, arithmetic and copies ran while one was open for 0% -> 0% of each run, Pallas kernels for 15% -> 15%
where the time goes in v3:
time: 50.5 us; the launch traced here: 50.3 us
  starting transfers between devices  23.1 us (46%)
  waiting for transfers between devices  14.6 us (29%)
  Pallas kernels  8.94 us (18%)
  other arithmetic  1.67 us (3%)
  between operations  1.48 us (3%)
  local copies, waits for them, and re-layouts  0.52 us (1%)
    ppermute x20, starting transfers between devices, swap(): return lax.ppermute(block, axis, [(i, i ^ distance) for i in range(size)])  18.3 us
    ppermute x20, waiting for transfers between devices, swap(): return lax.ppermute(block, axis, [(i, i ^ distance) for i in range(size)])  13.9 us
    pallas_call x9, Pallas kernels, call(): pl.pallas_call(body, out_shape=out_shape, in_specs=specs or [pl.BlockSpec...  8.94 us
    ppermute x3, starting transfers between devices, from_next_section(): lax.ppermute(block, 'pipe', [(i, (i - 1) % size) for i in range(size)])  4.76 us
    select_n x1, other arithmetic, on_device(): jnp.where(first_half, kw[:late_start], vw[:late_start])  1.55 us
  transfers between devices with their start and end apart: 23, of which 13 were waited for; matrix products, arithmetic and copies ran while one was open for 0% of the time, Pallas kernels for 15%

profile of v3, /device:TPU:0, one launch (start us, length us, event | category | flops | bytes accessed | tf_op | source)
XLA Modules:
  0.0 50.3 jit_solution(10797093026834745298)
XLA Ops:
  0.7 1.6 %select_bitcast_fusion = bf16[1408,256]{1,0:T(8,128)(2,1)S(1)} fusion(bf16[1,2048,256]{2,1,0:T(8,128)(2,1)} %param.19, bf16[1,2048,256]{2,1,0:T(8,128)(2,1)} %param.18, pred[]{:T(512)S(6)} %eq.3), kind=kLoop, calls=%fused_computation.1 | loop fusion | flops 360448 | bytes 2162689 | tf_op jit(solution)/shard_map/jit(_where)/select_n | solution.py:391
  2.8 3.0 %collective-permute-start.8 = (bf16[2176,256]{1,0:T(8,128)(2,1)S(1)}, bf16[2176,256]{1,0:T(8,128)(2,1)S(1)}, u32[]{:S(2)}, u32[]{:S(2)}) collective-permute-start(bf16[2176,256]{1,0:T(8,128)(2,1)S(1)} %pad_maximum_fusion), channel_id=1, source_target_pairs={{0,8},{8,0},{1,9},{9,1},{2,10},{10,2},{3,11},{11,3},{4,12},{12,4},... | collective-permute-start | bytes 3342344 | tf_op jit(solution)/shard_map/ppermute | solution.py:44
  5.8 1.5 %collective-permute-start.9 = (bf16[256,2048]{1,0:T(8,128)(2,1)S(1)}, bf16[256,2048]{1,0:T(8,128)(2,1)S(1)}, u32[]{:S(2)}, u32[]{:S(2)}) collective-permute-start(bf16[256,2048]{1,0:T(8,128)(2,1)S(1)} %bitcast.19), channel_id=1, source_target_pairs={{0,16},{16,0},{1,17},{17,1},{2,18},{18,2},{3,19},{19,3},{4,20},{20... | collective-permute-start | bytes 3145736 | tf_op jit(solution)/shard_map/ppermute | solution.py:39
  7.6 1.6 %collective-permute-start = (bf16[96,256]{1,0:T(8,128)(2,1)S(1)}, bf16[96,256]{1,0:T(8,128)(2,1)S(1)}, u32[]{:S(2)}, u32[]{:S(2)}) collective-permute-start(bf16[96,256]{1,0:T(8,128)(2,1)S(1)} %get-tuple-element.41.refs_0_), channel_id=1, source_target_pairs={{0,2},{1,3},{2,0},{3,1},{4,6},{5,7},{6,4},{7,5},{8,10},{9,11},{10,... | collective-permute-start | bytes 147464 | tf_op jit(solution)/shard_map/ppermute | solution.py:39
  9.2 2.6 %collective-permute-start.1 = (bf16[96,256]{1,0:T(8,128)(2,1)S(1)}, bf16[96,256]{1,0:T(8,128)(2,1)S(1)}, u32[]{:S(2)}, u32[]{:S(2)}) collective-permute-start(bf16[96,256]{1,0:T(8,128)(2,1)S(1)} %get-tuple-element.45), channel_id=1, source_target_pairs={{0,4},{1,5},{2,6},{3,7},{4,0},{5,1},{6,2},{7,3},{8,12},{9,13},{10,... | collective-permute-start | bytes 147464 | tf_op jit(solution)/shard_map/ppermute | solution.py:39
  13.1 1.7 %collective-permute-done.1.refs_2_ = bf16[96,256]{1,0:T(8,128)(2,1)S(1)} collective-permute-done((bf16[96,256]{1,0:T(8,128)(2,1)S(1)}, bf16[96,256]{1,0:T(8,128)(2,1)S(1)}, u32[]{:S(2)}, u32[]{:S(2)}) %collective-permute-start.1) | collective-permute-done | bytes 49184 | tf_op jit(solution)/shard_map/ppermute | solution.py:39
  14.7 3.0 %collective-permute-done.2.refs_3_ = bf16[96,256]{1,0:T(8,128)(2,1)S(1)} collective-permute-done((bf16[96,256]{1,0:T(8,128)(2,1)S(1)}, bf16[96,256]{1,0:T(8,128)(2,1)S(1)}, u32[]{:S(2)}, u32[]{:S(2)}) %collective-permute-start.2) | collective-permute-done | bytes 49184 | tf_op jit(solution)/shard_map/ppermute | solution.py:39
  18.2 0.7 %collective-permute-done.4.refs_5_ = bf16[96,256]{1,0:T(8,128)(2,1)S(1)} collective-permute-done((bf16[96,256]{1,0:T(8,128)(2,1)S(1)}, bf16[96,256]{1,0:T(8,128)(2,1)S(1)}, u32[]{:S(2)}, u32[]{:S(2)}) %collective-permute-start.4) | collective-permute-done | bytes 49184 | tf_op jit(solution)/shard_map/ppermute | solution.py:39
  19.5 3.5 %shard_map.156 = (bf16[256,512]{1,0:T(8,128)(2,1)}, f32[384,256]{1,0:T(8,128)S(1)}, bf16[384,256]{1,0:T(8,128)(2,1)S(1)}) custom-call(bf16[256,512]{1,0:T(8,128)(2,1)S(1)} %bitcast.25, bf16[256,512]{1,0:T(8,128)(2,1)S(1)} %bitcast.26, f32[768,128]{1,0:T(8,128)S(1)} %get-tuple-element.46.cos, f32[768,128]{1,0:T(8,128)S(1)} %get-tuple-element.47.sin, ...), custom_call_target="tpu_custom_call" | custom-call | flops 1006632960 | bytes 1048576 | tf_op jit(solution)/shard_map/pallas_call | solution.py:22
  23.2 1.3 %collective-permute-done.7.received = bf16[384,256]{1,0:T(8,128)(2,1)S(1)} collective-permute-done((bf16[384,256]{1,0:T(8,128)(2,1)S(1)}, bf16[384,256]{1,0:T(8,128)(2,1)S(1)}, u32[]{:S(2)}, u32[]{:S(2)}) %collective-permute-start.7) | collective-permute-done | bytes 196640 | tf_op jit(solution)/shard_map/ppermute | solution.py:39
  24.6 1.2 %collective-permute-start.11 = (bf16[128,256]{1,0:T(8,128)(2,1)S(1)}, bf16[128,256]{1,0:T(8,128)(2,1)S(1)}, u32[]{:S(2)}, u32[]{:S(2)}) collective-permute-start(bf16[128,256]{1,0:T(8,128)(2,1)S(1)} %get-tuple-element.59), channel_id=1, source_target_pairs={{0,4},{1,5},{2,6},{3,7},{4,0},{5,1},{6,2},{7,3},{8,12},{9,13},{10,... | collective-permute-start | bytes 196616 | tf_op jit(solution)/shard_map/ppermute | solution.py:39
  25.7 3.2 %collective-permute-start.12 = (bf16[128,256]{1,0:T(8,128)(2,1)S(1)}, bf16[128,256]{1,0:T(8,128)(2,1)S(1)}, u32[]{:S(2)}, u32[]{:S(2)}) collective-permute-start(bf16[128,256]{1,0:T(8,128)(2,1)S(1)} %get-tuple-element.59), channel_id=1, source_target_pairs={{0,6},{1,7},{2,4},{3,5},{4,2},{5,3},{6,0},{7,1},{8,14},{9,15},{10,... | collective-permute-start | bytes 196616 | tf_op jit(solution)/shard_map/ppermute | solution.py:39
  28.9 1.5 %collective-permute-done.9.refs_1_ = bf16[256,2048]{1,0:T(8,128)(2,1)S(1)} collective-permute-done((bf16[256,2048]{1,0:T(8,128)(2,1)S(1)}, bf16[256,2048]{1,0:T(8,128)(2,1)S(1)}, u32[]{:S(2)}, u32[]{:S(2)}) %collective-permute-start.9) | collective-permute-done | bytes 1048608 | tf_op jit(solution)/shard_map/ppermute | solution.py:39
  30.5 2.7 %collective-permute-done.11.refs_2_ = bf16[128,256]{1,0:T(8,128)(2,1)S(1)} collective-permute-done((bf16[128,256]{1,0:T(8,128)(2,1)S(1)}, bf16[128,256]{1,0:T(8,128)(2,1)S(1)}, u32[]{:S(2)}, u32[]{:S(2)}) %collective-permute-start.11) | collective-permute-done | bytes 65568 | tf_op jit(solution)/shard_map/ppermute | solution.py:39
  33.3 1.0 %collective-permute-start.15 = (bf16[128,512]{1,0:T(8,128)(2,1)S(1)}, bf16[128,512]{1,0:T(8,128)(2,1)S(1)}, u32[]{:S(2)}, u32[]{:S(2)}) collective-permute-start(bf16[128,512]{1,0:T(8,128)(2,1)S(1)} %get-tuple-element.60.refs_2_.own), channel_id=1, source_target_pairs={{0,8},{8,0},{1,9},{9,1},{2,10},{10,2},{3,11},{11,3},{4,12},{12,4},... | collective-permute-start | bytes 393224 | tf_op jit(solution)/shard_map/ppermute | solution.py:44
  34.9 1.6 %collective-permute-start.14 = (bf16[64,256]{1,0:T(8,128)(2,1)S(1)}, bf16[64,256]{1,0:T(8,128)(2,1)S(1)}, u32[]{:S(2)}, u32[]{:S(2)}) collective-permute-start(bf16[64,256]{1,0:T(8,128)(2,1)S(1)} %get-tuple-element.63), channel_id=1, source_target_pairs={{0,4},{1,5},{2,6},{3,7},{4,0},{5,1},{6,2},{7,3},{8,12},{9,13},{10,... | collective-permute-start | bytes 98312 | tf_op jit(solution)/shard_map/ppermute | solution.py:39
  36.5 1.6 %collective-permute-start.13 = (bf16[64,256]{1,0:T(8,128)(2,1)S(1)}, bf16[64,256]{1,0:T(8,128)(2,1)S(1)}, u32[]{:S(2)}, u32[]{:S(2)}) collective-permute-start(bf16[64,256]{1,0:T(8,128)(2,1)S(1)} %get-tuple-element.61), channel_id=1, source_target_pairs={{0,2},{1,3},{2,0},{3,1},{4,6},{5,7},{6,4},{7,5},{8,10},{9,11},{10,... | collective-permute-start | bytes 98312 | tf_op jit(solution)/shard_map/ppermute | solution.py:39
  39.7 0.7 %collective-permute-done.13.refs_1_ = bf16[64,256]{1,0:T(8,128)(2,1)S(1)} collective-permute-done((bf16[64,256]{1,0:T(8,128)(2,1)S(1)}, bf16[64,256]{1,0:T(8,128)(2,1)S(1)}, u32[]{:S(2)}, u32[]{:S(2)}) %collective-permute-start.13) | collective-permute-done | bytes 32800 | tf_op jit(solution)/shard_map/ppermute | solution.py:39
  40.4 0.7 %collective-permute-start.21 = (bf16[256,640]{1,0:T(8,128)(2,1)S(1)}, bf16[256,640]{1,0:T(8,128)(2,1)S(1)}, u32[]{:S(2)}, u32[]{:S(2)}) collective-permute-start(bf16[256,640]{1,0:T(8,128)(2,1)S(1)} %shard_map.161), channel_id=1, source_target_pairs={{0,8},{8,0},{1,9},{9,1},{2,10},{10,2},{3,11},{11,3},{4,12},{12,4},... | collective-permute-start | bytes 983048 | tf_op jit(solution)/shard_map/ppermute | solution.py:44
  41.6 2.4 %collective-permute-start.16 = (bf16[64,256]{1,0:T(8,128)(2,1)S(1)}, bf16[64,256]{1,0:T(8,128)(2,1)S(1)}, u32[]{:S(2)}, u32[]{:S(2)}) collective-permute-start(bf16[64,256]{1,0:T(8,128)(2,1)S(1)} %get-tuple-element.65), channel_id=1, source_target_pairs={{0,6},{1,7},{2,4},{3,5},{4,2},{5,3},{6,0},{7,1},{8,14},{9,15},{10,... | collective-permute-start | bytes 98312 | tf_op jit(solution)/shard_map/ppermute | solution.py:39
  44.0 2.2 %shard_map.160 = (f32[2048,128]{1,0:T(8,128)}, f32[2048,128]{1,0:T(8,128)}) custom-call(bf16[256,2048]{1,0:T(8,128)(2,1)S(1)} %bitcast.20, bf16[256,2048]{1,0:T(8,128)(2,1)S(1)} %collective-permute-done.9.refs_1_, bf16[128,512]{1,0:T(8,128)(2,1)S(1)} %get-tuple-element.60.refs_2_.own, bf16[128,512]{1,0:T(8,128)(2,1)S(1)} %collective-permute-done.17.refs_3_.other, ...), custom_call_target="tpu_custom_call" | custom-call | flops 536870912 | bytes 4194304 | tf_op jit(solution)/shard_map/pallas_call | solution.py:22
  46.2 1.1 %collective-permute-done.16.refs_3_ = bf16[64,256]{1,0:T(8,128)(2,1)S(1)} collective-permute-done((bf16[64,256]{1,0:T(8,128)(2,1)S(1)}, bf16[64,256]{1,0:T(8,128)(2,1)S(1)}, u32[]{:S(2)}, u32[]{:S(2)}) %collective-permute-start.16) | collective-permute-done | bytes 32800 | tf_op jit(solution)/shard_map/ppermute | solution.py:39
  48.0 0.8 %collective-permute-done.21.late = bf16[256,640]{1,0:T(8,128)(2,1)S(1)} collective-permute-done((bf16[256,640]{1,0:T(8,128)(2,1)S(1)}, bf16[256,640]{1,0:T(8,128)(2,1)S(1)}, u32[]{:S(2)}, u32[]{:S(2)}) %collective-permute-start.21) | collective-permute-done | bytes 327712 | tf_op jit(solution)/shard_map/ppermute | solution.py:44
  48.8 1.6 %shard_map.162 = bf16[256,2048]{1,0:T(8,128)(2,1)} custom-call(bf16[128,512]{1,0:T(8,128)(2,1)S(1)} %collective-permute-done.15.own, bf16[128,512]{1,0:T(8,128)(2,1)S(1)} %collective-permute-done.20.other, bf16[2176,256]{1,0:T(8,128)(2,1)S(1)} %collective-permute-done.8.weights, bf16[256,640]{1,0:T(8,128)(2,1)S(1)} %collective-permute-done.21.late, ...), custom_call_target="tpu_custom_call" | custom-call | flops 369098752 | bytes 2162688 | tf_op jit(solution)/shard_map/pallas_call | solution.py:22
  (57 shorter events, 6.1 us)
Async XLA Ops:
  2.8 16.6 %copy-start.5 = (bf16[1,1,256,512]{3,2,1,0:T(8,128)(2,1)S(1)}, bf16[1,1,256,512]{3,2,1,0:T(8,128)(2,1)}, u32[]{:S(2)}) copy-start(bf16[1,1,256,512]{3,2,1,0:T(8,128)(2,1)} %param.11) | copy-start | bytes 786436
  2.8 27.6 %collective-permute-start.8 = (bf16[2176,256]{1,0:T(8,128)(2,1)S(1)}, bf16[2176,256]{1,0:T(8,128)(2,1)S(1)}, u32[]{:S(2)}, u32[]{:S(2)}) collective-permute-start(bf16[2176,256]{1,0:T(8,128)(2,1)S(1)} %pad_maximum_fusion), channel_id=1, source_target_pairs={{0,8},{8,0},{1,9},{9,1},{2,10},{10,2},{3,11},{11,3},{4,12},{12,4},... | collective-permute-start | bytes 3342344 | tf_op jit(solution)/shard_map/ppermute | solution.py:44
  5.8 24.6 %collective-permute-start.9 = (bf16[256,2048]{1,0:T(8,128)(2,1)S(1)}, bf16[256,2048]{1,0:T(8,128)(2,1)S(1)}, u32[]{:S(2)}, u32[]{:S(2)}) collective-permute-start(bf16[256,2048]{1,0:T(8,128)(2,1)S(1)} %bitcast.19), channel_id=1, source_target_pairs={{0,16},{16,0},{1,17},{17,1},{2,18},{18,2},{3,19},{19,3},{4,20},{20... | collective-permute-start | bytes 3145736 | tf_op jit(solution)/shard_map/ppermute | solution.py:39
  7.6 4.5 %collective-permute-start = (bf16[96,256]{1,0:T(8,128)(2,1)S(1)}, bf16[96,256]{1,0:T(8,128)(2,1)S(1)}, u32[]{:S(2)}, u32[]{:S(2)}) collective-permute-start(bf16[96,256]{1,0:T(8,128)(2,1)S(1)} %get-tuple-element.41.refs_0_), channel_id=1, source_target_pairs={{0,2},{1,3},{2,0},{3,1},{4,6},{5,7},{6,4},{7,5},{8,10},{9,11},{10,... | collective-permute-start | bytes 147464 | tf_op jit(solution)/shard_map/ppermute | solution.py:39
  9.2 5.5 %collective-permute-start.1 = (bf16[96,256]{1,0:T(8,128)(2,1)S(1)}, bf16[96,256]{1,0:T(8,128)(2,1)S(1)}, u32[]{:S(2)}, u32[]{:S(2)}) collective-permute-start(bf16[96,256]{1,0:T(8,128)(2,1)S(1)} %get-tuple-element.45), channel_id=1, source_target_pairs={{0,4},{1,5},{2,6},{3,7},{4,0},{5,1},{6,2},{7,3},{8,12},{9,13},{10,... | collective-permute-start | bytes 147464 | tf_op jit(solution)/shard_map/ppermute | solution.py:39
  11.8 5.9 %collective-permute-start.2 = (bf16[96,256]{1,0:T(8,128)(2,1)S(1)}, bf16[96,256]{1,0:T(8,128)(2,1)S(1)}, u32[]{:S(2)}, u32[]{:S(2)}) collective-permute-start(bf16[96,256]{1,0:T(8,128)(2,1)S(1)} %get-tuple-element.45), channel_id=1, source_target_pairs={{0,6},{1,7},{2,4},{3,5},{4,2},{5,3},{6,0},{7,1},{8,14},{9,15},{10,... | collective-permute-start | bytes 147464 | tf_op jit(solution)/shard_map/ppermute | solution.py:39
  12.0 6.2 %collective-permute-start.3 = (bf16[96,256]{1,0:T(8,128)(2,1)S(1)}, bf16[96,256]{1,0:T(8,128)(2,1)S(1)}, u32[]{:S(2)}, u32[]{:S(2)}) collective-permute-start(bf16[96,256]{1,0:T(8,128)(2,1)S(1)} %get-tuple-element.41.refs_0_), channel_id=1, source_target_pairs={{0,1},{1,0},{2,3},{3,2},{4,5},{5,4},{6,7},{7,6},{8,9},{9,8},{10,11... | collective-permute-start | bytes 147464 | tf_op jit(solution)/shard_map/ppermute | solution.py:39
  17.7 1.2 %collective-permute-start.4 = (bf16[96,256]{1,0:T(8,128)(2,1)S(1)}, bf16[96,256]{1,0:T(8,128)(2,1)S(1)}, u32[]{:S(2)}, u32[]{:S(2)}) collective-permute-start(bf16[96,256]{1,0:T(8,128)(2,1)S(1)} %collective-permute-done.refs_1_), channel_id=1, source_target_pairs={{0,1},{1,0},{2,3},{3,2},{4,5},{5,4},{6,7},{7,6},{8,9},{9,8},{10,11... | collective-permute-start | bytes 147464 | tf_op jit(solution)/shard_map/ppermute | solution.py:39
  17.7 1.4 %collective-permute-start.5 = (bf16[96,256]{1,0:T(8,128)(2,1)S(1)}, bf16[96,256]{1,0:T(8,128)(2,1)S(1)}, u32[]{:S(2)}, u32[]{:S(2)}) collective-permute-start(bf16[96,256]{1,0:T(8,128)(2,1)S(1)} %collective-permute-done.1.refs_2_), channel_id=1, source_target_pairs={{0,1},{1,0},{2,3},{3,2},{4,5},{5,4},{6,7},{7,6},{8,9},{9,8},{10,11... | collective-permute-start | bytes 147464 | tf_op jit(solution)/shard_map/ppermute | solution.py:39
  18.2 1.2 %collective-permute-start.6 = (bf16[96,256]{1,0:T(8,128)(2,1)S(1)}, bf16[96,256]{1,0:T(8,128)(2,1)S(1)}, u32[]{:S(2)}, u32[]{:S(2)}) collective-permute-start(bf16[96,256]{1,0:T(8,128)(2,1)S(1)} %collective-permute-done.2.refs_3_), channel_id=1, source_target_pairs={{0,1},{1,0},{2,3},{3,2},{4,5},{5,4},{6,7},{7,6},{8,9},{9,8},{10,11... | collective-permute-start | bytes 147464 | tf_op jit(solution)/shard_map/ppermute | solution.py:39
  23.0 1.4 %collective-permute-start.7 = (bf16[384,256]{1,0:T(8,128)(2,1)S(1)}, bf16[384,256]{1,0:T(8,128)(2,1)S(1)}, u32[]{:S(2)}, u32[]{:S(2)}) collective-permute-start(bf16[384,256]{1,0:T(8,128)(2,1)S(1)} %get-tuple-element.54), channel_id=1, source_target_pairs={{0,1},{1,0},{2,3},{3,2},{4,5},{5,4},{6,7},{7,6},{8,9},{9,8},{10,11... | collective-permute-start | bytes 589832 | tf_op jit(solution)/shard_map/ppermute | solution.py:39
  24.5 6.0 %collective-permute-start.10 = (bf16[128,256]{1,0:T(8,128)(2,1)S(1)}, bf16[128,256]{1,0:T(8,128)(2,1)S(1)}, u32[]{:S(2)}, u32[]{:S(2)}) collective-permute-start(bf16[128,256]{1,0:T(8,128)(2,1)S(1)} %get-tuple-element.59), channel_id=1, source_target_pairs={{0,2},{1,3},{2,0},{3,1},{4,6},{5,7},{6,4},{7,5},{8,10},{9,11},{10,... | collective-permute-start | bytes 196616 | tf_op jit(solution)/shard_map/ppermute | solution.py:39
  24.6 8.6 %collective-permute-start.11 = (bf16[128,256]{1,0:T(8,128)(2,1)S(1)}, bf16[128,256]{1,0:T(8,128)(2,1)S(1)}, u32[]{:S(2)}, u32[]{:S(2)}) collective-permute-start(bf16[128,256]{1,0:T(8,128)(2,1)S(1)} %get-tuple-element.59), channel_id=1, source_target_pairs={{0,4},{1,5},{2,6},{3,7},{4,0},{5,1},{6,2},{7,3},{8,12},{9,13},{10,... | collective-permute-start | bytes 196616 | tf_op jit(solution)/shard_map/ppermute | solution.py:39
  25.7 7.5 %collective-permute-start.12 = (bf16[128,256]{1,0:T(8,128)(2,1)S(1)}, bf16[128,256]{1,0:T(8,128)(2,1)S(1)}, u32[]{:S(2)}, u32[]{:S(2)}) collective-permute-start(bf16[128,256]{1,0:T(8,128)(2,1)S(1)} %get-tuple-element.59), channel_id=1, source_target_pairs={{0,6},{1,7},{2,4},{3,5},{4,2},{5,3},{6,0},{7,1},{8,14},{9,15},{10,... | collective-permute-start | bytes 196616 | tf_op jit(solution)/shard_map/ppermute | solution.py:39
  33.3 6.0 %collective-permute-start.17 = (bf16[128,512]{1,0:T(8,128)(2,1)S(1)}, bf16[128,512]{1,0:T(8,128)(2,1)S(1)}, u32[]{:S(2)}, u32[]{:S(2)}) collective-permute-start(bf16[128,512]{1,0:T(8,128)(2,1)S(1)} %get-tuple-element.60.refs_2_.own), channel_id=1, source_target_pairs={{0,1},{1,0},{2,3},{3,2},{4,5},{5,4},{6,7},{7,6},{8,9},{9,8},{10,11... | collective-permute-start | bytes 393224 | tf_op jit(solution)/shard_map/ppermute | solution.py:39
  33.3 7.1 %collective-permute-start.15 = (bf16[128,512]{1,0:T(8,128)(2,1)S(1)}, bf16[128,512]{1,0:T(8,128)(2,1)S(1)}, u32[]{:S(2)}, u32[]{:S(2)}) collective-permute-start(bf16[128,512]{1,0:T(8,128)(2,1)S(1)} %get-tuple-element.60.refs_2_.own), channel_id=1, source_target_pairs={{0,8},{8,0},{1,9},{9,1},{2,10},{10,2},{3,11},{11,3},{4,12},{12,4},... | collective-permute-start | bytes 393224 | tf_op jit(solution)/shard_map/ppermute | solution.py:44
  34.4 4.3 %collective-permute-start.18 = (bf16[128,256]{1,0:T(8,128)(2,1)S(1)}, bf16[128,256]{1,0:T(8,128)(2,1)S(1)}, u32[]{:S(2)}, u32[]{:S(2)}) collective-permute-start(bf16[128,256]{1,0:T(8,128)(2,1)S(1)} %get-tuple-element.68), channel_id=1, source_target_pairs={{0,16},{16,0},{1,17},{17,1},{2,18},{18,2},{3,19},{19,3},{4,20},{20... | collective-permute-start | bytes 196616 | tf_op jit(solution)/shard_map/ppermute | solution.py:39
  34.9 4.8 %collective-permute-start.14 = (bf16[64,256]{1,0:T(8,128)(2,1)S(1)}, bf16[64,256]{1,0:T(8,128)(2,1)S(1)}, u32[]{:S(2)}, u32[]{:S(2)}) collective-permute-start(bf16[64,256]{1,0:T(8,128)(2,1)S(1)} %get-tuple-element.63), channel_id=1, source_target_pairs={{0,4},{1,5},{2,6},{3,7},{4,0},{5,1},{6,2},{7,3},{8,12},{9,13},{10,... | collective-permute-start | bytes 98312 | tf_op jit(solution)/shard_map/ppermute | solution.py:39
  36.5 3.9 %collective-permute-start.13 = (bf16[64,256]{1,0:T(8,128)(2,1)S(1)}, bf16[64,256]{1,0:T(8,128)(2,1)S(1)}, u32[]{:S(2)}, u32[]{:S(2)}) collective-permute-start(bf16[64,256]{1,0:T(8,128)(2,1)S(1)} %get-tuple-element.61), channel_id=1, source_target_pairs={{0,2},{1,3},{2,0},{3,1},{4,6},{5,7},{6,4},{7,5},{8,10},{9,11},{10,... | collective-permute-start | bytes 98312 | tf_op jit(solution)/shard_map/ppermute | solution.py:39
  38.7 9.3 %collective-permute-start.22 = (bf16[640,256]{1,0:T(8,128)(2,1)S(1)}, bf16[640,256]{1,0:T(8,128)(2,1)S(1)}, u32[]{:S(2)}, u32[]{:S(2)}) collective-permute-start(bf16[640,256]{1,0:T(8,128)(2,1)S(1)} %slice.31), channel_id=1, source_target_pairs={{0,16},{16,0},{1,17},{17,1},{2,18},{18,2},{3,19},{19,3},{4,20},{20... | collective-permute-start | bytes 983048 | tf_op jit(solution)/shard_map/ppermute | solution.py:39
  40.4 8.4 %collective-permute-start.21 = (bf16[256,640]{1,0:T(8,128)(2,1)S(1)}, bf16[256,640]{1,0:T(8,128)(2,1)S(1)}, u32[]{:S(2)}, u32[]{:S(2)}) collective-permute-start(bf16[256,640]{1,0:T(8,128)(2,1)S(1)} %shard_map.161), channel_id=1, source_target_pairs={{0,8},{8,0},{1,9},{9,1},{2,10},{10,2},{3,11},{11,3},{4,12},{12,4},... | collective-permute-start | bytes 983048 | tf_op jit(solution)/shard_map/ppermute | solution.py:44
  41.1 6.9 %collective-permute-start.20 = (bf16[128,512]{1,0:T(8,128)(2,1)S(1)}, bf16[128,512]{1,0:T(8,128)(2,1)S(1)}, u32[]{:S(2)}, u32[]{:S(2)}) collective-permute-start(bf16[128,512]{1,0:T(8,128)(2,1)S(1)} %collective-permute-done.15.own), channel_id=1, source_target_pairs={{0,1},{1,0},{2,3},{3,2},{4,5},{5,4},{6,7},{7,6},{8,9},{9,8},{10,11... | collective-permute-start | bytes 393224 | tf_op jit(solution)/shard_map/ppermute | solution.py:39
  41.1 2.9 %collective-permute-start.19 = (bf16[128,256]{1,0:T(8,128)(2,1)S(1)}, bf16[128,256]{1,0:T(8,128)(2,1)S(1)}, u32[]{:S(2)}, u32[]{:S(2)}) collective-permute-start(bf16[128,256]{1,0:T(8,128)(2,1)S(1)} %collective-permute-done.18.refs_4_), channel_id=1, source_target_pairs={{0,1},{1,0},{2,3},{3,2},{4,5},{5,4},{6,7},{7,6},{8,9},{9,8},{10,11... | collective-permute-start | bytes 196616 | tf_op jit(solution)/shard_map/ppermute | solution.py:39
  41.6 5.7 %collective-permute-start.16 = (bf16[64,256]{1,0:T(8,128)(2,1)S(1)}, bf16[64,256]{1,0:T(8,128)(2,1)S(1)}, u32[]{:S(2)}, u32[]{:S(2)}) collective-permute-start(bf16[64,256]{1,0:T(8,128)(2,1)S(1)} %get-tuple-element.65), channel_id=1, source_target_pairs={{0,6},{1,7},{2,4},{3,5},{4,2},{5,3},{6,0},{7,1},{8,14},{9,15},{10,... | collective-permute-start | bytes 98312 | tf_op jit(solution)/shard_map/ppermute | solution.py:39
  (9 other events, 52.1 us)

commit v4 on v3

--- a/solution.py
+++ b/solution.py
@@ -18,12 +18,12 @@
 AHEAD, SHARED = 6, 5
 
 
-def call(body, out_shape, args, scratch=(), flops=0, nbytes=0, specs=None, limit=40):
+def call(body, out_shape, args, scratch=(), flops=0, nbytes=0, specs=None, limit=40, out_space=VMEM):
     return pl.pallas_call(
         body,
         out_shape=out_shape,
         in_specs=specs or [pl.BlockSpec(memory_space=VMEM)] * len(args),
-        out_specs=jax.tree.map(lambda _: pl.BlockSpec(memory_space=VMEM), out_shape),
+        out_specs=jax.tree.map(lambda _: pl.BlockSpec(memory_space=out_space), out_shape),
         scratch_shapes=list(scratch),
         compiler_params=pltpu.CompilerParams(vmem_limit_bytes=limit * 1024 * 1024),
         cost_estimate=pl.CostEstimate(flops=flops, bytes_accessed=nbytes, transcendentals=0),
@@ -144,7 +144,7 @@
         ds[h * span : (h + 1) * span, :] = do[:, h * HD : (h + 1) * HD]
     row = lax.broadcasted_iota(jnp.int32, (keys, span), 1)
     start_key = jnp.concatenate([first[...]] * (span // HD), axis=1)
-    visible = start_key <= row
+    bias = jnp.where(start_key <= row, 0.0, neg_large)
     contract_last = (((1,), (1,)), ((), ()))
 
     def products(h):
@@ -159,7 +159,7 @@
         s, dp = following
         if h + 1 < heads:
             following = products(h + 1)
-        s = jnp.where(visible, s * scale, neg_large)
+        s = s * scale + bias
         e = jnp.exp(s - jnp.max(s, axis=0, keepdims=True))
         a = e * (1.0 / jnp.sum(e, axis=0, keepdims=True))
         a_bf = a.astype(BF)
@@ -267,18 +267,28 @@
 
 
 def early_grad_body(chips, span_rows, sections, ahead, own, other, weights, late, *refs):
-    more, (out, rows) = refs[:-2], refs[-2:]
+    more, (out, rows, held, held_more, moved) = refs[:-5], refs[-5:]
     last = lax.axis_index("pipe") == sections - 1
     width = weights.shape[1]
-    ready = out.shape[1] - late.shape[1]
+    features = held.shape[1]
+    ready = features - late.shape[1]
     contract_last = (((1,), (1,)), ((), ()))
+
+    def move(source, low, high, which):
+        columns = pl.ds(low, high - low)
+        return pltpu.make_async_copy(source, out.at[:, columns], moved.at[which])
 
     @pl.when(last)
     def _():
-        out[...] = jnp.zeros_like(out)
+        held[...] = jnp.zeros_like(held)
+        whole = move(held, 0, features, 0)
+        whole.start()
+        whole.wait()
 
     @pl.when(jnp.logical_not(last))
     def _():
+        moves = [move(late, ready, features, 0)]
+        moves[0].start()
         weave(chips, span_rows, rows, own, other)
         kind = lax.axis_index("dp") if more else 0
 
@@ -288,11 +298,16 @@
             return lax.dot_general(grad, block, contract_last, preferred_element_type=F32)
 
         total = product(kind, weights[:ahead]) + product(1 - kind, weights[ready:])
-        out[:, :ahead] = total.astype(BF)
+        held[:, :ahead] = total.astype(BF)
+        moves.append(move(held.at[:, pl.ds(0, ahead)], 0, ahead, 1))
+        moves[1].start()
         if more:
             total = product(kind, weights[ahead:ready]) + product(1 - kind, more[0][...])
-            out[:, ahead:ready] = total.astype(BF)
-        out[:, ready:] = late[...]
+            held_more[...] = total.astype(BF)
+            moves.append(move(held_more, ahead, ready, 2))
+            moves[2].start()
+        for each in moves:
+            each.wait()
 
 
 def weight_grad_body(chips, span_rows, replicas, *refs):
@@ -354,7 +369,7 @@
     kw, vw = key_weight[0], value_weight[0]
     ahead, shared = features * AHEAD // 16, features * SHARED // 16
     if replicas != 2:
-        ahead, shared = ahead + shared // 2, 0
+        ahead, shared = (ahead + shared // 2) // HD * HD, 0
     late_start = ahead + shared
 
     packed = call(
@@ -378,10 +393,16 @@
         specs=[pl.BlockSpec(memory_space=pltpu.SMEM), pl.BlockSpec(memory_space=VMEM)],
     )
     pieces = [swap(packed[j // per_head], "tensor", 2 * j) for j in range(1, chips)]
-    late_kw, late_vw, cos, *pieces = lax.optimization_barrier(
-        (after(kw, packed[0])[late_start:], after(vw, packed[0])[late_start:], cos, *pieces)
-    )
-    pieces = [packed[0], *pieces]
+    late_kw, late_vw, cos, *near = lax.optimization_barrier(
+        (
+            after(kw, packed[0])[late_start:],
+            after(vw, packed[0])[late_start:],
+            cos,
+            packed[0],
+            *pieces[:-1],
+        )
+    )
+    pieces = [*near, pieces[-1]]
     pieces = pieces + [swap(piece, "tensor", 1) for piece in pieces]
 
     ready = [kw[:late_start], vw[:ahead]]
@@ -482,7 +503,13 @@
         functools.partial(early_grad_body, chips, span_rows, lax.axis_size("pipe"), ahead),
         shape(span, features, BF),
         (next_grad, swap(next_grad, "tensor", 1), weights, late, *more),
-        scratch=[VMEM((span, 2 * width), row_type(span_rows))],
+        scratch=[
+            VMEM((span, 2 * width), row_type(span_rows)),
+            VMEM((span, features), BF),
+            VMEM((span, shared or HD), BF),
+            pltpu.SemaphoreType.DMA((3,)),
+        ],
+        out_space=pl.ANY,
         flops=4 * span * width * late_start,
         nbytes=late_start * (4 * width + 2 * span),
     )

time: 50.5 us -> 50.2 us (level)
  starting transfers between devices: 23.1 us -> 24.1 us
  waiting for transfers between devices: 14.6 us -> 13.6 us
    ppermute x20, starting transfers between devices: 18.3 us -> 19.4 us  [swap(): return lax.ppermute(block, axis, [(i, i ^ distance) for i in range(size)])]
    ppermute x20, waiting for transfers between devices: 13.9 us -> 12.8 us  [swap(): return lax.ppermute(block, axis, [(i, i ^ distance) for i in range(size)])]
  transfers between devices with their start and end apart: 23 -> 23, of which waited for: 13 -> 12; matrix products, arithmetic and copies ran while one was open for 0% -> 0% of each run, Pallas kernels for 15% -> 15%
where the time goes in v4:
time: 50.2 us; the launch traced here: 50.1 us
  starting transfers between devices  24.1 us (48%)
  waiting for transfers between devices  13.6 us (27%)
  Pallas kernels  8.73 us (17%)
  other arithmetic  1.67 us (3%)
  between operations  1.49 us (3%)
  local copies, waits for them, and re-layouts  0.52 us (1%)
    ppermute x20, starting transfers between devices, swap(): return lax.ppermute(block, axis, [(i, i ^ distance) for i in range(size)])  19.4 us
    ppermute x20, waiting for transfers between devices, swap(): return lax.ppermute(block, axis, [(i, i ^ distance) for i in range(size)])  12.8 us
    pallas_call x9, Pallas kernels, call(): pl.pallas_call(body, out_shape=out_shape, in_specs=specs or [pl.BlockSpec...  8.73 us
    ppermute x3, starting transfers between devices, from_next_section(): lax.ppermute(block, 'pipe', [(i, (i - 1) % size) for i in range(size)])  4.64 us
    select_n x1, other arithmetic, on_device(): jnp.where(first_half, kw[:late_start], vw[:late_start])  1.55 us
  transfers between devices with their start and end apart: 23, of which 12 were waited for; matrix products, arithmetic and copies ran while one was open for 0% of the time, Pallas kernels for 15%

profile of v4, /device:TPU:0, one launch (start us, length us, event | category | flops | bytes accessed | tf_op | source)
XLA Modules:
  0.0 50.1 jit_solution(11657511948701757401)
XLA Ops:
  0.7 1.6 %select_bitcast_fusion = bf16[1408,256]{1,0:T(8,128)(2,1)S(1)} fusion(bf16[1,2048,256]{2,1,0:T(8,128)(2,1)} %param.19, bf16[1,2048,256]{2,1,0:T(8,128)(2,1)} %param.18, pred[]{:T(512)S(6)} %eq.3), kind=kLoop, calls=%fused_computation.1 | loop fusion | flops 360448 | bytes 2162689 | tf_op jit(solution)/shard_map/jit(_where)/select_n | solution.py:412
  2.8 3.0 %collective-permute-start.8 = (bf16[2176,256]{1,0:T(8,128)(2,1)S(1)}, bf16[2176,256]{1,0:T(8,128)(2,1)S(1)}, u32[]{:S(2)}, u32[]{:S(2)}) collective-permute-start(bf16[2176,256]{1,0:T(8,128)(2,1)S(1)} %pad_maximum_fusion), channel_id=1, source_target_pairs={{0,8},{8,0},{1,9},{9,1},{2,10},{10,2},{3,11},{11,3},{4,12},{12,4},... | collective-permute-start | bytes 3342344 | tf_op jit(solution)/shard_map/ppermute | solution.py:44
  5.8 1.5 %collective-permute-start.9 = (bf16[256,2048]{1,0:T(8,128)(2,1)S(1)}, bf16[256,2048]{1,0:T(8,128)(2,1)S(1)}, u32[]{:S(2)}, u32[]{:S(2)}) collective-permute-start(bf16[256,2048]{1,0:T(8,128)(2,1)S(1)} %bitcast.19), channel_id=1, source_target_pairs={{0,16},{16,0},{1,17},{17,1},{2,18},{18,2},{3,19},{19,3},{4,20},{20... | collective-permute-start | bytes 3145736 | tf_op jit(solution)/shard_map/ppermute | solution.py:39
  7.6 1.6 %collective-permute-start = (bf16[96,256]{1,0:T(8,128)(2,1)S(1)}, bf16[96,256]{1,0:T(8,128)(2,1)S(1)}, u32[]{:S(2)}, u32[]{:S(2)}) collective-permute-start(bf16[96,256]{1,0:T(8,128)(2,1)S(1)} %get-tuple-element.49.refs_0_), channel_id=1, source_target_pairs={{0,2},{1,3},{2,0},{3,1},{4,6},{5,7},{6,4},{7,5},{8,10},{9,11},{10,... | collective-permute-start | bytes 147464 | tf_op jit(solution)/shard_map/ppermute | solution.py:39
  9.2 2.6 %collective-permute-start.1 = (bf16[96,256]{1,0:T(8,128)(2,1)S(1)}, bf16[96,256]{1,0:T(8,128)(2,1)S(1)}, u32[]{:S(2)}, u32[]{:S(2)}) collective-permute-start(bf16[96,256]{1,0:T(8,128)(2,1)S(1)} %get-tuple-element.45), channel_id=1, source_target_pairs={{0,4},{1,5},{2,6},{3,7},{4,0},{5,1},{6,2},{7,3},{8,12},{9,13},{10,... | collective-permute-start | bytes 147464 | tf_op jit(solution)/shard_map/ppermute | solution.py:39
  13.1 1.7 %collective-permute-done.1.refs_2_ = bf16[96,256]{1,0:T(8,128)(2,1)S(1)} collective-permute-done((bf16[96,256]{1,0:T(8,128)(2,1)S(1)}, bf16[96,256]{1,0:T(8,128)(2,1)S(1)}, u32[]{:S(2)}, u32[]{:S(2)}) %collective-permute-start.1) | collective-permute-done | bytes 49184 | tf_op jit(solution)/shard_map/ppermute | solution.py:39
  15.2 2.5 %collective-permute-done.2.refs_3_ = bf16[96,256]{1,0:T(8,128)(2,1)S(1)} collective-permute-done((bf16[96,256]{1,0:T(8,128)(2,1)S(1)}, bf16[96,256]{1,0:T(8,128)(2,1)S(1)}, u32[]{:S(2)}, u32[]{:S(2)}) %collective-permute-start.2) | collective-permute-done | bytes 49184 | tf_op jit(solution)/shard_map/ppermute | solution.py:39
  18.2 0.7 %collective-permute-done.5.refs_6_ = bf16[96,256]{1,0:T(8,128)(2,1)S(1)} collective-permute-done((bf16[96,256]{1,0:T(8,128)(2,1)S(1)}, bf16[96,256]{1,0:T(8,128)(2,1)S(1)}, u32[]{:S(2)}, u32[]{:S(2)}) %collective-permute-start.5) | collective-permute-done | bytes 49184 | tf_op jit(solution)/shard_map/ppermute | solution.py:39
  19.1 3.5 %shard_map.156 = (bf16[256,512]{1,0:T(8,128)(2,1)}, f32[384,256]{1,0:T(8,128)S(1)}, bf16[384,256]{1,0:T(8,128)(2,1)S(1)}) custom-call(bf16[256,512]{1,0:T(8,128)(2,1)S(1)} %bitcast.25, bf16[256,512]{1,0:T(8,128)(2,1)S(1)} %bitcast.26, f32[768,128]{1,0:T(8,128)S(1)} %get-tuple-element.46.cos, f32[768,128]{1,0:T(8,128)S(1)} %get-tuple-element.47.sin, ...), custom_call_target="tpu_custom_call" | custom-call | flops 1006632960 | bytes 1048576 | tf_op jit(solution)/shard_map/pallas_call | solution.py:22
  23.0 1.1 %collective-permute-done.7.received = bf16[384,256]{1,0:T(8,128)(2,1)S(1)} collective-permute-done((bf16[384,256]{1,0:T(8,128)(2,1)S(1)}, bf16[384,256]{1,0:T(8,128)(2,1)S(1)}, u32[]{:S(2)}, u32[]{:S(2)}) %collective-permute-start.7) | collective-permute-done | bytes 196640 | tf_op jit(solution)/shard_map/ppermute | solution.py:39
  24.2 1.2 %collective-permute-start.11 = (bf16[128,256]{1,0:T(8,128)(2,1)S(1)}, bf16[128,256]{1,0:T(8,128)(2,1)S(1)}, u32[]{:S(2)}, u32[]{:S(2)}) collective-permute-start(bf16[128,256]{1,0:T(8,128)(2,1)S(1)} %get-tuple-element.59), channel_id=1, source_target_pairs={{0,4},{1,5},{2,6},{3,7},{4,0},{5,1},{6,2},{7,3},{8,12},{9,13},{10,... | collective-permute-start | bytes 196616 | tf_op jit(solution)/shard_map/ppermute | solution.py:39
  25.4 3.2 %collective-permute-start.12 = (bf16[128,256]{1,0:T(8,128)(2,1)S(1)}, bf16[128,256]{1,0:T(8,128)(2,1)S(1)}, u32[]{:S(2)}, u32[]{:S(2)}) collective-permute-start(bf16[128,256]{1,0:T(8,128)(2,1)S(1)} %get-tuple-element.59), channel_id=1, source_target_pairs={{0,6},{1,7},{2,4},{3,5},{4,2},{5,3},{6,0},{7,1},{8,14},{9,15},{10,... | collective-permute-start | bytes 196616 | tf_op jit(solution)/shard_map/ppermute | solution.py:39
  28.6 1.9 %collective-permute-done.9.refs_1_ = bf16[256,2048]{1,0:T(8,128)(2,1)S(1)} collective-permute-done((bf16[256,2048]{1,0:T(8,128)(2,1)S(1)}, bf16[256,2048]{1,0:T(8,128)(2,1)S(1)}, u32[]{:S(2)}, u32[]{:S(2)}) %collective-permute-start.9) | collective-permute-done | bytes 1048608 | tf_op jit(solution)/shard_map/ppermute | solution.py:39
  30.5 2.4 %collective-permute-done.11.refs_2_ = bf16[128,256]{1,0:T(8,128)(2,1)S(1)} collective-permute-done((bf16[128,256]{1,0:T(8,128)(2,1)S(1)}, bf16[128,256]{1,0:T(8,128)(2,1)S(1)}, u32[]{:S(2)}, u32[]{:S(2)}) %collective-permute-start.11) | collective-permute-done | bytes 65568 | tf_op jit(solution)/shard_map/ppermute | solution.py:39
  33.0 1.0 %collective-permute-start.15 = (bf16[128,512]{1,0:T(8,128)(2,1)S(1)}, bf16[128,512]{1,0:T(8,128)(2,1)S(1)}, u32[]{:S(2)}, u32[]{:S(2)}) collective-permute-start(bf16[128,512]{1,0:T(8,128)(2,1)S(1)} %get-tuple-element.60.refs_2_.own), channel_id=1, source_target_pairs={{0,8},{8,0},{1,9},{9,1},{2,10},{10,2},{3,11},{11,3},{4,12},{12,4},... | collective-permute-start | bytes 393224 | tf_op jit(solution)/shard_map/ppermute | solution.py:44
  34.6 1.9 %collective-permute-start.14 = (bf16[64,256]{1,0:T(8,128)(2,1)S(1)}, bf16[64,256]{1,0:T(8,128)(2,1)S(1)}, u32[]{:S(2)}, u32[]{:S(2)}) collective-permute-start(bf16[64,256]{1,0:T(8,128)(2,1)S(1)} %get-tuple-element.63), channel_id=1, source_target_pairs={{0,4},{1,5},{2,6},{3,7},{4,0},{5,1},{6,2},{7,3},{8,12},{9,13},{10,... | collective-permute-start | bytes 98312 | tf_op jit(solution)/shard_map/ppermute | solution.py:39
  36.5 1.6 %collective-permute-start.13 = (bf16[64,256]{1,0:T(8,128)(2,1)S(1)}, bf16[64,256]{1,0:T(8,128)(2,1)S(1)}, u32[]{:S(2)}, u32[]{:S(2)}) collective-permute-start(bf16[64,256]{1,0:T(8,128)(2,1)S(1)} %get-tuple-element.61), channel_id=1, source_target_pairs={{0,2},{1,3},{2,0},{3,1},{4,6},{5,7},{6,4},{7,5},{8,10},{9,11},{10,... | collective-permute-start | bytes 98312 | tf_op jit(solution)/shard_map/ppermute | solution.py:39
  39.5 0.9 %collective-permute-done.13.refs_1_ = bf16[64,256]{1,0:T(8,128)(2,1)S(1)} collective-permute-done((bf16[64,256]{1,0:T(8,128)(2,1)S(1)}, bf16[64,256]{1,0:T(8,128)(2,1)S(1)}, u32[]{:S(2)}, u32[]{:S(2)}) %collective-permute-start.13) | collective-permute-done | bytes 32800 | tf_op jit(solution)/shard_map/ppermute | solution.py:39
  41.5 2.5 %collective-permute-start.16 = (bf16[64,256]{1,0:T(8,128)(2,1)S(1)}, bf16[64,256]{1,0:T(8,128)(2,1)S(1)}, u32[]{:S(2)}, u32[]{:S(2)}) collective-permute-start(bf16[64,256]{1,0:T(8,128)(2,1)S(1)} %get-tuple-element.65), channel_id=1, source_target_pairs={{0,6},{1,7},{2,4},{3,5},{4,2},{5,3},{6,0},{7,1},{8,14},{9,15},{10,... | collective-permute-start | bytes 98312 | tf_op jit(solution)/shard_map/ppermute | solution.py:39
  44.0 2.2 %shard_map.160 = (f32[2048,128]{1,0:T(8,128)}, f32[2048,128]{1,0:T(8,128)}) custom-call(bf16[256,2048]{1,0:T(8,128)(2,1)S(1)} %bitcast.20, bf16[256,2048]{1,0:T(8,128)(2,1)S(1)} %collective-permute-done.9.refs_1_, bf16[128,512]{1,0:T(8,128)(2,1)S(1)} %get-tuple-element.60.refs_2_.own, bf16[128,512]{1,0:T(8,128)(2,1)S(1)} %collective-permute-done.17.refs_3_.other, ...), custom_call_target="tpu_custom_call" | custom-call | flops 536870912 | bytes 4194304 | tf_op jit(solution)/shard_map/pallas_call | solution.py:22
  46.1 1.1 %collective-permute-done.16.refs_3_ = bf16[64,256]{1,0:T(8,128)(2,1)S(1)} collective-permute-done((bf16[64,256]{1,0:T(8,128)(2,1)S(1)}, bf16[64,256]{1,0:T(8,128)(2,1)S(1)}, u32[]{:S(2)}, u32[]{:S(2)}) %collective-permute-start.16) | collective-permute-done | bytes 32800 | tf_op jit(solution)/shard_map/ppermute | solution.py:39
  47.2 0.7 %shard_map.159 = (f32[64,256]{1,0:T(8,128)}, f32[64,256]{1,0:T(8,128)}) custom-call(f32[64,256]{1,0:T(8,128)S(1)} %get-tuple-element.55.refs_0_, bf16[64,256]{1,0:T(8,128)(2,1)S(1)} %collective-permute-done.13.refs_1_, bf16[64,256]{1,0:T(8,128)(2,1)S(1)} %collective-permute-done.14.refs_2_, bf16[64,256]{1,0:T(8,128)(2,1)S(1)} %collective-permute-done.16.refs_3_), custom_call_target="tpu_custom_call" | custom-call | bytes 262144 | tf_op jit(solution)/shard_map/pallas_call | solution.py:22
  47.9 0.8 %collective-permute-done.21.late = bf16[256,640]{1,0:T(8,128)(2,1)S(1)} collective-permute-done((bf16[256,640]{1,0:T(8,128)(2,1)S(1)}, bf16[256,640]{1,0:T(8,128)(2,1)S(1)}, u32[]{:S(2)}, u32[]{:S(2)}) %collective-permute-start.21) | collective-permute-done | bytes 327712 | tf_op jit(solution)/shard_map/ppermute | solution.py:44
  48.7 1.4 %shard_map.162 = bf16[256,2048]{1,0:T(8,128)(2,1)} custom-call(bf16[128,512]{1,0:T(8,128)(2,1)S(1)} %collective-permute-done.15.own, bf16[128,512]{1,0:T(8,128)(2,1)S(1)} %collective-permute-done.20.other, bf16[2176,256]{1,0:T(8,128)(2,1)S(1)} %collective-permute-done.8.weights, bf16[256,640]{1,0:T(8,128)(2,1)S(1)} %collective-permute-done.21.late, ...), custom_call_target="tpu_custom_call" | custom-call | flops 369098752 | bytes 2162688 | tf_op jit(solution)/shard_map/pallas_call | solution.py:22
  (57 shorter events, 6.2 us)
Async XLA Ops:
  2.8 16.3 %copy-start.5 = (bf16[1,1,256,512]{3,2,1,0:T(8,128)(2,1)S(1)}, bf16[1,1,256,512]{3,2,1,0:T(8,128)(2,1)}, u32[]{:S(2)}) copy-start(bf16[1,1,256,512]{3,2,1,0:T(8,128)(2,1)} %param.11) | copy-start | bytes 786436
  2.8 27.6 %collective-permute-start.8 = (bf16[2176,256]{1,0:T(8,128)(2,1)S(1)}, bf16[2176,256]{1,0:T(8,128)(2,1)S(1)}, u32[]{:S(2)}, u32[]{:S(2)}) collective-permute-start(bf16[2176,256]{1,0:T(8,128)(2,1)S(1)} %pad_maximum_fusion), channel_id=1, source_target_pairs={{0,8},{8,0},{1,9},{9,1},{2,10},{10,2},{3,11},{11,3},{4,12},{12,4},... | collective-permute-start | bytes 3342344 | tf_op jit(solution)/shard_map/ppermute | solution.py:44
  5.8 24.6 %collective-permute-start.9 = (bf16[256,2048]{1,0:T(8,128)(2,1)S(1)}, bf16[256,2048]{1,0:T(8,128)(2,1)S(1)}, u32[]{:S(2)}, u32[]{:S(2)}) collective-permute-start(bf16[256,2048]{1,0:T(8,128)(2,1)S(1)} %bitcast.19), channel_id=1, source_target_pairs={{0,16},{16,0},{1,17},{17,1},{2,18},{18,2},{3,19},{19,3},{4,20},{20... | collective-permute-start | bytes 3145736 | tf_op jit(solution)/shard_map/ppermute | solution.py:39
  7.6 5.5 %collective-permute-start = (bf16[96,256]{1,0:T(8,128)(2,1)S(1)}, bf16[96,256]{1,0:T(8,128)(2,1)S(1)}, u32[]{:S(2)}, u32[]{:S(2)}) collective-permute-start(bf16[96,256]{1,0:T(8,128)(2,1)S(1)} %get-tuple-element.49.refs_0_), channel_id=1, source_target_pairs={{0,2},{1,3},{2,0},{3,1},{4,6},{5,7},{6,4},{7,5},{8,10},{9,11},{10,... | collective-permute-start | bytes 147464 | tf_op jit(solution)/shard_map/ppermute | solution.py:39
  9.2 5.5 %collective-permute-start.1 = (bf16[96,256]{1,0:T(8,128)(2,1)S(1)}, bf16[96,256]{1,0:T(8,128)(2,1)S(1)}, u32[]{:S(2)}, u32[]{:S(2)}) collective-permute-start(bf16[96,256]{1,0:T(8,128)(2,1)S(1)} %get-tuple-element.45), channel_id=1, source_target_pairs={{0,4},{1,5},{2,6},{3,7},{4,0},{5,1},{6,2},{7,3},{8,12},{9,13},{10,... | collective-permute-start | bytes 147464 | tf_op jit(solution)/shard_map/ppermute | solution.py:39
  11.8 5.9 %collective-permute-start.2 = (bf16[96,256]{1,0:T(8,128)(2,1)S(1)}, bf16[96,256]{1,0:T(8,128)(2,1)S(1)}, u32[]{:S(2)}, u32[]{:S(2)}) collective-permute-start(bf16[96,256]{1,0:T(8,128)(2,1)S(1)} %get-tuple-element.45), channel_id=1, source_target_pairs={{0,6},{1,7},{2,4},{3,5},{4,2},{5,3},{6,0},{7,1},{8,14},{9,15},{10,... | collective-permute-start | bytes 147464 | tf_op jit(solution)/shard_map/ppermute | solution.py:39
  14.7 3.0 %collective-permute-start.3 = (bf16[96,256]{1,0:T(8,128)(2,1)S(1)}, bf16[96,256]{1,0:T(8,128)(2,1)S(1)}, u32[]{:S(2)}, u32[]{:S(2)}) collective-permute-start(bf16[96,256]{1,0:T(8,128)(2,1)S(1)} %get-tuple-element.49.refs_0_), channel_id=1, source_target_pairs={{0,1},{1,0},{2,3},{3,2},{4,5},{5,4},{6,7},{7,6},{8,9},{9,8},{10,11... | collective-permute-start | bytes 147464 | tf_op jit(solution)/shard_map/ppermute | solution.py:39
  14.7 3.5 %collective-permute-start.4 = (bf16[96,256]{1,0:T(8,128)(2,1)S(1)}, bf16[96,256]{1,0:T(8,128)(2,1)S(1)}, u32[]{:S(2)}, u32[]{:S(2)}) collective-permute-start(bf16[96,256]{1,0:T(8,128)(2,1)S(1)} %collective-permute-done.refs_1_), channel_id=1, source_target_pairs={{0,1},{1,0},{2,3},{3,2},{4,5},{5,4},{6,7},{7,6},{8,9},{9,8},{10,11... | collective-permute-start | bytes 147464 | tf_op jit(solution)/shard_map/ppermute | solution.py:39
  17.7 1.2 %collective-permute-start.5 = (bf16[96,256]{1,0:T(8,128)(2,1)S(1)}, bf16[96,256]{1,0:T(8,128)(2,1)S(1)}, u32[]{:S(2)}, u32[]{:S(2)}) collective-permute-start(bf16[96,256]{1,0:T(8,128)(2,1)S(1)} %collective-permute-done.1.refs_2_), channel_id=1, source_target_pairs={{0,1},{1,0},{2,3},{3,2},{4,5},{5,4},{6,7},{7,6},{8,9},{9,8},{10,11... | collective-permute-start | bytes 147464 | tf_op jit(solution)/shard_map/ppermute | solution.py:39
  17.7 1.4 %collective-permute-start.6 = (bf16[96,256]{1,0:T(8,128)(2,1)S(1)}, bf16[96,256]{1,0:T(8,128)(2,1)S(1)}, u32[]{:S(2)}, u32[]{:S(2)}) collective-permute-start(bf16[96,256]{1,0:T(8,128)(2,1)S(1)} %collective-permute-done.2.refs_3_), channel_id=1, source_target_pairs={{0,1},{1,0},{2,3},{3,2},{4,5},{5,4},{6,7},{7,6},{8,9},{9,8},{10,11... | collective-permute-start | bytes 147464 | tf_op jit(solution)/shard_map/ppermute | solution.py:39
  22.6 1.4 %collective-permute-start.7 = (bf16[384,256]{1,0:T(8,128)(2,1)S(1)}, bf16[384,256]{1,0:T(8,128)(2,1)S(1)}, u32[]{:S(2)}, u32[]{:S(2)}) collective-permute-start(bf16[384,256]{1,0:T(8,128)(2,1)S(1)} %get-tuple-element.54), channel_id=1, source_target_pairs={{0,1},{1,0},{2,3},{3,2},{4,5},{5,4},{6,7},{7,6},{8,9},{9,8},{10,11... | collective-permute-start | bytes 589832 | tf_op jit(solution)/shard_map/ppermute | solution.py:39
  24.1 6.4 %collective-permute-start.10 = (bf16[128,256]{1,0:T(8,128)(2,1)S(1)}, bf16[128,256]{1,0:T(8,128)(2,1)S(1)}, u32[]{:S(2)}, u32[]{:S(2)}) collective-permute-start(bf16[128,256]{1,0:T(8,128)(2,1)S(1)} %get-tuple-element.59), channel_id=1, source_target_pairs={{0,2},{1,3},{2,0},{3,1},{4,6},{5,7},{6,4},{7,5},{8,10},{9,11},{10,... | collective-permute-start | bytes 196616 | tf_op jit(solution)/shard_map/ppermute | solution.py:39
  24.2 8.7 %collective-permute-start.11 = (bf16[128,256]{1,0:T(8,128)(2,1)S(1)}, bf16[128,256]{1,0:T(8,128)(2,1)S(1)}, u32[]{:S(2)}, u32[]{:S(2)}) collective-permute-start(bf16[128,256]{1,0:T(8,128)(2,1)S(1)} %get-tuple-element.59), channel_id=1, source_target_pairs={{0,4},{1,5},{2,6},{3,7},{4,0},{5,1},{6,2},{7,3},{8,12},{9,13},{10,... | collective-permute-start | bytes 196616 | tf_op jit(solution)/shard_map/ppermute | solution.py:39
  25.4 7.5 %collective-permute-start.12 = (bf16[128,256]{1,0:T(8,128)(2,1)S(1)}, bf16[128,256]{1,0:T(8,128)(2,1)S(1)}, u32[]{:S(2)}, u32[]{:S(2)}) collective-permute-start(bf16[128,256]{1,0:T(8,128)(2,1)S(1)} %get-tuple-element.59), channel_id=1, source_target_pairs={{0,6},{1,7},{2,4},{3,5},{4,2},{5,3},{6,0},{7,1},{8,14},{9,15},{10,... | collective-permute-start | bytes 196616 | tf_op jit(solution)/shard_map/ppermute | solution.py:39
  32.9 6.0 %collective-permute-start.17 = (bf16[128,512]{1,0:T(8,128)(2,1)S(1)}, bf16[128,512]{1,0:T(8,128)(2,1)S(1)}, u32[]{:S(2)}, u32[]{:S(2)}) collective-permute-start(bf16[128,512]{1,0:T(8,128)(2,1)S(1)} %get-tuple-element.60.refs_2_.own), channel_id=1, source_target_pairs={{0,1},{1,0},{2,3},{3,2},{4,5},{5,4},{6,7},{7,6},{8,9},{9,8},{10,11... | collective-permute-start | bytes 393224 | tf_op jit(solution)/shard_map/ppermute | solution.py:39
  33.0 7.4 %collective-permute-start.15 = (bf16[128,512]{1,0:T(8,128)(2,1)S(1)}, bf16[128,512]{1,0:T(8,128)(2,1)S(1)}, u32[]{:S(2)}, u32[]{:S(2)}) collective-permute-start(bf16[128,512]{1,0:T(8,128)(2,1)S(1)} %get-tuple-element.60.refs_2_.own), channel_id=1, source_target_pairs={{0,8},{8,0},{1,9},{9,1},{2,10},{10,2},{3,11},{11,3},{4,12},{12,4},... | collective-permute-start | bytes 393224 | tf_op jit(solution)/shard_map/ppermute | solution.py:44
  34.1 4.3 %collective-permute-start.18 = (bf16[128,256]{1,0:T(8,128)(2,1)S(1)}, bf16[128,256]{1,0:T(8,128)(2,1)S(1)}, u32[]{:S(2)}, u32[]{:S(2)}) collective-permute-start(bf16[128,256]{1,0:T(8,128)(2,1)S(1)} %get-tuple-element.68), channel_id=1, source_target_pairs={{0,16},{16,0},{1,17},{17,1},{2,18},{18,2},{3,19},{19,3},{4,20},{20... | collective-permute-start | bytes 196616 | tf_op jit(solution)/shard_map/ppermute | solution.py:39
  34.6 4.9 %collective-permute-start.14 = (bf16[64,256]{1,0:T(8,128)(2,1)S(1)}, bf16[64,256]{1,0:T(8,128)(2,1)S(1)}, u32[]{:S(2)}, u32[]{:S(2)}) collective-permute-start(bf16[64,256]{1,0:T(8,128)(2,1)S(1)} %get-tuple-element.63), channel_id=1, source_target_pairs={{0,4},{1,5},{2,6},{3,7},{4,0},{5,1},{6,2},{7,3},{8,12},{9,13},{10,... | collective-permute-start | bytes 98312 | tf_op jit(solution)/shard_map/ppermute | solution.py:39
  36.5 3.9 %collective-permute-start.13 = (bf16[64,256]{1,0:T(8,128)(2,1)S(1)}, bf16[64,256]{1,0:T(8,128)(2,1)S(1)}, u32[]{:S(2)}, u32[]{:S(2)}) collective-permute-start(bf16[64,256]{1,0:T(8,128)(2,1)S(1)} %get-tuple-element.61), channel_id=1, source_target_pairs={{0,2},{1,3},{2,0},{3,1},{4,6},{5,7},{6,4},{7,5},{8,10},{9,11},{10,... | collective-permute-start | bytes 98312 | tf_op jit(solution)/shard_map/ppermute | solution.py:39
  38.4 9.5 %collective-permute-start.22 = (bf16[640,256]{1,0:T(8,128)(2,1)S(1)}, bf16[640,256]{1,0:T(8,128)(2,1)S(1)}, u32[]{:S(2)}, u32[]{:S(2)}) collective-permute-start(bf16[640,256]{1,0:T(8,128)(2,1)S(1)} %slice.31), channel_id=1, source_target_pairs={{0,16},{16,0},{1,17},{17,1},{2,18},{18,2},{3,19},{19,3},{4,20},{20... | collective-permute-start | bytes 983048 | tf_op jit(solution)/shard_map/ppermute | solution.py:39
  40.4 8.3 %collective-permute-start.21 = (bf16[256,640]{1,0:T(8,128)(2,1)S(1)}, bf16[256,640]{1,0:T(8,128)(2,1)S(1)}, u32[]{:S(2)}, u32[]{:S(2)}) collective-permute-start(bf16[256,640]{1,0:T(8,128)(2,1)S(1)} %shard_map.161), channel_id=1, source_target_pairs={{0,8},{8,0},{1,9},{9,1},{2,10},{10,2},{3,11},{11,3},{4,12},{12,4},... | collective-permute-start | bytes 983048 | tf_op jit(solution)/shard_map/ppermute | solution.py:44
  41.0 6.9 %collective-permute-start.20 = (bf16[128,512]{1,0:T(8,128)(2,1)S(1)}, bf16[128,512]{1,0:T(8,128)(2,1)S(1)}, u32[]{:S(2)}, u32[]{:S(2)}) collective-permute-start(bf16[128,512]{1,0:T(8,128)(2,1)S(1)} %collective-permute-done.15.own), channel_id=1, source_target_pairs={{0,1},{1,0},{2,3},{3,2},{4,5},{5,4},{6,7},{7,6},{8,9},{9,8},{10,11... | collective-permute-start | bytes 393224 | tf_op jit(solution)/shard_map/ppermute | solution.py:39
  41.0 3.0 %collective-permute-start.19 = (bf16[128,256]{1,0:T(8,128)(2,1)S(1)}, bf16[128,256]{1,0:T(8,128)(2,1)S(1)}, u32[]{:S(2)}, u32[]{:S(2)}) collective-permute-start(bf16[128,256]{1,0:T(8,128)(2,1)S(1)} %collective-permute-done.18.refs_4_), channel_id=1, source_target_pairs={{0,1},{1,0},{2,3},{3,2},{4,5},{5,4},{6,7},{7,6},{8,9},{9,8},{10,11... | collective-permute-start | bytes 196616 | tf_op jit(solution)/shard_map/ppermute | solution.py:39
  41.5 5.7 %collective-permute-start.16 = (bf16[64,256]{1,0:T(8,128)(2,1)S(1)}, bf16[64,256]{1,0:T(8,128)(2,1)S(1)}, u32[]{:S(2)}, u32[]{:S(2)}) collective-permute-start(bf16[64,256]{1,0:T(8,128)(2,1)S(1)} %get-tuple-element.65), channel_id=1, source_target_pairs={{0,6},{1,7},{2,4},{3,5},{4,2},{5,3},{6,0},{7,1},{8,14},{9,15},{10,... | collective-permute-start | bytes 98312 | tf_op jit(solution)/shard_map/ppermute | solution.py:39
  (9 other events, 51.8 us)

commit v5 on v4

--- a/solution.py
+++ b/solution.py
@@ -11,6 +11,7 @@
 HD = 128
 rope_base = 500000.0
 neg_large = -1e30
+log2_e = 1.4426950408889634
 BF = jnp.bfloat16
 F32 = jnp.float32
 VMEM = pltpu.VMEM
@@ -144,7 +145,7 @@
         ds[h * span : (h + 1) * span, :] = do[:, h * HD : (h + 1) * HD]
     row = lax.broadcasted_iota(jnp.int32, (keys, span), 1)
     start_key = jnp.concatenate([first[...]] * (span // HD), axis=1)
-    bias = jnp.where(start_key <= row, 0.0, neg_large)
+    visible = start_key <= row
     contract_last = (((1,), (1,)), ((), ()))
 
     def products(h):
@@ -159,8 +160,8 @@
         s, dp = following
         if h + 1 < heads:
             following = products(h + 1)
-        s = s * scale + bias
-        e = jnp.exp(s - jnp.max(s, axis=0, keepdims=True))
+        s = jnp.where(visible, s * (scale * log2_e), neg_large)
+        e = jnp.exp2(s - jnp.max(s, axis=0, keepdims=True))
         a = e * (1.0 / jnp.sum(e, axis=0, keepdims=True))
         a_bf = a.astype(BF)
         at[:, columns] = a_bf
@@ -168,7 +169,7 @@
         d = (a * (dp - delta)).astype(BF)
         dst[:, columns] = d
         dqt = jnp.dot(krt[...], d, preferred_element_type=F32) * scale
-        dq[:, h * HD : (h + 1) * HD] = dqt.T.astype(BF)
+        dq[:, h * HD : (h + 1) * HD] = dqt.astype(BF).T
     dk = jnp.dot(dst[...], qs[...], preferred_element_type=F32) * scale
     dk = dk * cos[...] - pltpu.roll(dk, HD // 2, 1) * sin[...]
     dv = jnp.dot(at[...], ds[...], preferred_element_type=F32)

time: 50.2 us -> 50.3 us (level)
  transfers between devices with their start and end apart: 23 -> 23, of which waited for: 12 -> 12; matrix products, arithmetic and copies ran while one was open for 0% -> 0% of each run, Pallas kernels for 15% -> 14%
where the time goes in v5:
time: 50.3 us; the launch traced here: 50.2 us
  starting transfers between devices  24.1 us (48%)
  waiting for transfers between devices  13.7 us (27%)
  Pallas kernels  8.71 us (17%)
  other arithmetic  1.67 us (3%)
  between operations  1.49 us (3%)
  local copies, waits for them, and re-layouts  0.52 us (1%)
    ppermute x20, starting transfers between devices, swap(): return lax.ppermute(block, axis, [(i, i ^ distance) for i in range(size)])  19.4 us
    ppermute x20, waiting for transfers between devices, swap(): return lax.ppermute(block, axis, [(i, i ^ distance) for i in range(size)])  12.8 us
    pallas_call x9, Pallas kernels, call(): pl.pallas_call(body, out_shape=out_shape, in_specs=specs or [pl.BlockSpec...  8.71 us
    ppermute x3, starting transfers between devices, from_next_section(): lax.ppermute(block, 'pipe', [(i, (i - 1) % size) for i in range(size)])  4.63 us
    select_n x1, other arithmetic, on_device(): jnp.where(first_half, kw[:late_start], vw[:late_start])  1.55 us
  transfers between devices with their start and end apart: 23, of which 12 were waited for; matrix products, arithmetic and copies ran while one was open for 0% of the time, Pallas kernels for 14%

profile of v5, /device:TPU:0, one launch (start us, length us, event | category | flops | bytes accessed | tf_op | source)
XLA Modules:
  0.0 50.2 jit_solution(10625609127340755058)
XLA Ops:
  0.7 1.6 %select_bitcast_fusion = bf16[1408,256]{1,0:T(8,128)(2,1)S(1)} fusion(bf16[1,2048,256]{2,1,0:T(8,128)(2,1)} %param.19, bf16[1,2048,256]{2,1,0:T(8,128)(2,1)} %param.18, pred[]{:T(512)S(6)} %eq.3), kind=kLoop, calls=%fused_computation.1 | loop fusion | flops 360448 | bytes 2162689 | tf_op jit(solution)/shard_map/jit(_where)/select_n | solution.py:413
  2.8 3.0 %collective-permute-start.8 = (bf16[2176,256]{1,0:T(8,128)(2,1)S(1)}, bf16[2176,256]{1,0:T(8,128)(2,1)S(1)}, u32[]{:S(2)}, u32[]{:S(2)}) collective-permute-start(bf16[2176,256]{1,0:T(8,128)(2,1)S(1)} %pad_maximum_fusion), channel_id=1, source_target_pairs={{0,8},{8,0},{1,9},{9,1},{2,10},{10,2},{3,11},{11,3},{4,12},{12,4},... | collective-permute-start | bytes 3342344 | tf_op jit(solution)/shard_map/ppermute | solution.py:45
  5.8 1.5 %collective-permute-start.9 = (bf16[256,2048]{1,0:T(8,128)(2,1)S(1)}, bf16[256,2048]{1,0:T(8,128)(2,1)S(1)}, u32[]{:S(2)}, u32[]{:S(2)}) collective-permute-start(bf16[256,2048]{1,0:T(8,128)(2,1)S(1)} %bitcast.19), channel_id=1, source_target_pairs={{0,16},{16,0},{1,17},{17,1},{2,18},{18,2},{3,19},{19,3},{4,20},{20... | collective-permute-start | bytes 3145736 | tf_op jit(solution)/shard_map/ppermute | solution.py:40
  7.6 1.6 %collective-permute-start = (bf16[96,256]{1,0:T(8,128)(2,1)S(1)}, bf16[96,256]{1,0:T(8,128)(2,1)S(1)}, u32[]{:S(2)}, u32[]{:S(2)}) collective-permute-start(bf16[96,256]{1,0:T(8,128)(2,1)S(1)} %get-tuple-element.49.refs_0_), channel_id=1, source_target_pairs={{0,2},{1,3},{2,0},{3,1},{4,6},{5,7},{6,4},{7,5},{8,10},{9,11},{10,... | collective-permute-start | bytes 147464 | tf_op jit(solution)/shard_map/ppermute | solution.py:40
  9.2 2.6 %collective-permute-start.1 = (bf16[96,256]{1,0:T(8,128)(2,1)S(1)}, bf16[96,256]{1,0:T(8,128)(2,1)S(1)}, u32[]{:S(2)}, u32[]{:S(2)}) collective-permute-start(bf16[96,256]{1,0:T(8,128)(2,1)S(1)} %get-tuple-element.45), channel_id=1, source_target_pairs={{0,4},{1,5},{2,6},{3,7},{4,0},{5,1},{6,2},{7,3},{8,12},{9,13},{10,... | collective-permute-start | bytes 147464 | tf_op jit(solution)/shard_map/ppermute | solution.py:40
  13.1 1.7 %collective-permute-done.1.refs_2_ = bf16[96,256]{1,0:T(8,128)(2,1)S(1)} collective-permute-done((bf16[96,256]{1,0:T(8,128)(2,1)S(1)}, bf16[96,256]{1,0:T(8,128)(2,1)S(1)}, u32[]{:S(2)}, u32[]{:S(2)}) %collective-permute-start.1) | collective-permute-done | bytes 49184 | tf_op jit(solution)/shard_map/ppermute | solution.py:40
  15.2 2.5 %collective-permute-done.2.refs_3_ = bf16[96,256]{1,0:T(8,128)(2,1)S(1)} collective-permute-done((bf16[96,256]{1,0:T(8,128)(2,1)S(1)}, bf16[96,256]{1,0:T(8,128)(2,1)S(1)}, u32[]{:S(2)}, u32[]{:S(2)}) %collective-permute-start.2) | collective-permute-done | bytes 49184 | tf_op jit(solution)/shard_map/ppermute | solution.py:40
  18.2 0.7 %collective-permute-done.5.refs_6_ = bf16[96,256]{1,0:T(8,128)(2,1)S(1)} collective-permute-done((bf16[96,256]{1,0:T(8,128)(2,1)S(1)}, bf16[96,256]{1,0:T(8,128)(2,1)S(1)}, u32[]{:S(2)}, u32[]{:S(2)}) %collective-permute-start.5) | collective-permute-done | bytes 49184 | tf_op jit(solution)/shard_map/ppermute | solution.py:40
  19.1 3.5 %shard_map.156 = (bf16[256,512]{1,0:T(8,128)(2,1)}, f32[384,256]{1,0:T(8,128)S(1)}, bf16[384,256]{1,0:T(8,128)(2,1)S(1)}) custom-call(bf16[256,512]{1,0:T(8,128)(2,1)S(1)} %bitcast.25, bf16[256,512]{1,0:T(8,128)(2,1)S(1)} %bitcast.26, f32[768,128]{1,0:T(8,128)S(1)} %get-tuple-element.46.cos, f32[768,128]{1,0:T(8,128)S(1)} %get-tuple-element.47.sin, ...), custom_call_target="tpu_custom_call" | custom-call | flops 1006632960 | bytes 1048576 | tf_op jit(solution)/shard_map/pallas_call | solution.py:23
  23.0 1.1 %collective-permute-done.7.received = bf16[384,256]{1,0:T(8,128)(2,1)S(1)} collective-permute-done((bf16[384,256]{1,0:T(8,128)(2,1)S(1)}, bf16[384,256]{1,0:T(8,128)(2,1)S(1)}, u32[]{:S(2)}, u32[]{:S(2)}) %collective-permute-start.7) | collective-permute-done | bytes 196640 | tf_op jit(solution)/shard_map/ppermute | solution.py:40
  24.2 1.2 %collective-permute-start.11 = (bf16[128,256]{1,0:T(8,128)(2,1)S(1)}, bf16[128,256]{1,0:T(8,128)(2,1)S(1)}, u32[]{:S(2)}, u32[]{:S(2)}) collective-permute-start(bf16[128,256]{1,0:T(8,128)(2,1)S(1)} %get-tuple-element.59), channel_id=1, source_target_pairs={{0,4},{1,5},{2,6},{3,7},{4,0},{5,1},{6,2},{7,3},{8,12},{9,13},{10,... | collective-permute-start | bytes 196616 | tf_op jit(solution)/shard_map/ppermute | solution.py:40
  25.3 3.2 %collective-permute-start.12 = (bf16[128,256]{1,0:T(8,128)(2,1)S(1)}, bf16[128,256]{1,0:T(8,128)(2,1)S(1)}, u32[]{:S(2)}, u32[]{:S(2)}) collective-permute-start(bf16[128,256]{1,0:T(8,128)(2,1)S(1)} %get-tuple-element.59), channel_id=1, source_target_pairs={{0,6},{1,7},{2,4},{3,5},{4,2},{5,3},{6,0},{7,1},{8,14},{9,15},{10,... | collective-permute-start | bytes 196616 | tf_op jit(solution)/shard_map/ppermute | solution.py:40
  28.5 1.9 %collective-permute-done.9.refs_1_ = bf16[256,2048]{1,0:T(8,128)(2,1)S(1)} collective-permute-done((bf16[256,2048]{1,0:T(8,128)(2,1)S(1)}, bf16[256,2048]{1,0:T(8,128)(2,1)S(1)}, u32[]{:S(2)}, u32[]{:S(2)}) %collective-permute-start.9) | collective-permute-done | bytes 1048608 | tf_op jit(solution)/shard_map/ppermute | solution.py:40
  30.5 2.4 %collective-permute-done.11.refs_2_ = bf16[128,256]{1,0:T(8,128)(2,1)S(1)} collective-permute-done((bf16[128,256]{1,0:T(8,128)(2,1)S(1)}, bf16[128,256]{1,0:T(8,128)(2,1)S(1)}, u32[]{:S(2)}, u32[]{:S(2)}) %collective-permute-start.11) | collective-permute-done | bytes 65568 | tf_op jit(solution)/shard_map/ppermute | solution.py:40
  33.0 1.0 %collective-permute-start.15 = (bf16[128,512]{1,0:T(8,128)(2,1)S(1)}, bf16[128,512]{1,0:T(8,128)(2,1)S(1)}, u32[]{:S(2)}, u32[]{:S(2)}) collective-permute-start(bf16[128,512]{1,0:T(8,128)(2,1)S(1)} %get-tuple-element.60.refs_2_.own), channel_id=1, source_target_pairs={{0,8},{8,0},{1,9},{9,1},{2,10},{10,2},{3,11},{11,3},{4,12},{12,4},... | collective-permute-start | bytes 393224 | tf_op jit(solution)/shard_map/ppermute | solution.py:45
  34.6 1.9 %collective-permute-start.14 = (bf16[64,256]{1,0:T(8,128)(2,1)S(1)}, bf16[64,256]{1,0:T(8,128)(2,1)S(1)}, u32[]{:S(2)}, u32[]{:S(2)}) collective-permute-start(bf16[64,256]{1,0:T(8,128)(2,1)S(1)} %get-tuple-element.63), channel_id=1, source_target_pairs={{0,4},{1,5},{2,6},{3,7},{4,0},{5,1},{6,2},{7,3},{8,12},{9,13},{10,... | collective-permute-start | bytes 98312 | tf_op jit(solution)/shard_map/ppermute | solution.py:40
  36.5 1.6 %collective-permute-start.13 = (bf16[64,256]{1,0:T(8,128)(2,1)S(1)}, bf16[64,256]{1,0:T(8,128)(2,1)S(1)}, u32[]{:S(2)}, u32[]{:S(2)}) collective-permute-start(bf16[64,256]{1,0:T(8,128)(2,1)S(1)} %get-tuple-element.61), channel_id=1, source_target_pairs={{0,2},{1,3},{2,0},{3,1},{4,6},{5,7},{6,4},{7,5},{8,10},{9,11},{10,... | collective-permute-start | bytes 98312 | tf_op jit(solution)/shard_map/ppermute | solution.py:40
  39.5 0.9 %collective-permute-done.13.refs_1_ = bf16[64,256]{1,0:T(8,128)(2,1)S(1)} collective-permute-done((bf16[64,256]{1,0:T(8,128)(2,1)S(1)}, bf16[64,256]{1,0:T(8,128)(2,1)S(1)}, u32[]{:S(2)}, u32[]{:S(2)}) %collective-permute-start.13) | collective-permute-done | bytes 32800 | tf_op jit(solution)/shard_map/ppermute | solution.py:40
  41.5 2.5 %collective-permute-start.16 = (bf16[64,256]{1,0:T(8,128)(2,1)S(1)}, bf16[64,256]{1,0:T(8,128)(2,1)S(1)}, u32[]{:S(2)}, u32[]{:S(2)}) collective-permute-start(bf16[64,256]{1,0:T(8,128)(2,1)S(1)} %get-tuple-element.65), channel_id=1, source_target_pairs={{0,6},{1,7},{2,4},{3,5},{4,2},{5,3},{6,0},{7,1},{8,14},{9,15},{10,... | collective-permute-start | bytes 98312 | tf_op jit(solution)/shard_map/ppermute | solution.py:40
  44.0 2.2 %shard_map.160 = (f32[2048,128]{1,0:T(8,128)}, f32[2048,128]{1,0:T(8,128)}) custom-call(bf16[256,2048]{1,0:T(8,128)(2,1)S(1)} %bitcast.20, bf16[256,2048]{1,0:T(8,128)(2,1)S(1)} %collective-permute-done.9.refs_1_, bf16[128,512]{1,0:T(8,128)(2,1)S(1)} %get-tuple-element.60.refs_2_.own, bf16[128,512]{1,0:T(8,128)(2,1)S(1)} %collective-permute-done.17.refs_3_.other, ...), custom_call_target="tpu_custom_call" | custom-call | flops 536870912 | bytes 4194304 | tf_op jit(solution)/shard_map/pallas_call | solution.py:23
  46.1 1.1 %collective-permute-done.16.refs_3_ = bf16[64,256]{1,0:T(8,128)(2,1)S(1)} collective-permute-done((bf16[64,256]{1,0:T(8,128)(2,1)S(1)}, bf16[64,256]{1,0:T(8,128)(2,1)S(1)}, u32[]{:S(2)}, u32[]{:S(2)}) %collective-permute-start.16) | collective-permute-done | bytes 32800 | tf_op jit(solution)/shard_map/ppermute | solution.py:40
  47.2 0.7 %shard_map.159 = (f32[64,256]{1,0:T(8,128)}, f32[64,256]{1,0:T(8,128)}) custom-call(f32[64,256]{1,0:T(8,128)S(1)} %get-tuple-element.55.refs_0_, bf16[64,256]{1,0:T(8,128)(2,1)S(1)} %collective-permute-done.13.refs_1_, bf16[64,256]{1,0:T(8,128)(2,1)S(1)} %collective-permute-done.14.refs_2_, bf16[64,256]{1,0:T(8,128)(2,1)S(1)} %collective-permute-done.16.refs_3_), custom_call_target="tpu_custom_call" | custom-call | bytes 262144 | tf_op jit(solution)/shard_map/pallas_call | solution.py:23
  47.9 0.9 %collective-permute-done.21.late = bf16[256,640]{1,0:T(8,128)(2,1)S(1)} collective-permute-done((bf16[256,640]{1,0:T(8,128)(2,1)S(1)}, bf16[256,640]{1,0:T(8,128)(2,1)S(1)}, u32[]{:S(2)}, u32[]{:S(2)}) %collective-permute-start.21) | collective-permute-done | bytes 327712 | tf_op jit(solution)/shard_map/ppermute | solution.py:45
  48.8 1.4 %shard_map.162 = bf16[256,2048]{1,0:T(8,128)(2,1)} custom-call(bf16[128,512]{1,0:T(8,128)(2,1)S(1)} %collective-permute-done.15.own, bf16[128,512]{1,0:T(8,128)(2,1)S(1)} %collective-permute-done.20.other, bf16[2176,256]{1,0:T(8,128)(2,1)S(1)} %collective-permute-done.8.weights, bf16[256,640]{1,0:T(8,128)(2,1)S(1)} %collective-permute-done.21.late, ...), custom_call_target="tpu_custom_call" | custom-call | flops 369098752 | bytes 2162688 | tf_op jit(solution)/shard_map/pallas_call | solution.py:23
  (57 shorter events, 6.1 us)
Async XLA Ops:
  2.8 16.3 %copy-start.5 = (bf16[1,1,256,512]{3,2,1,0:T(8,128)(2,1)S(1)}, bf16[1,1,256,512]{3,2,1,0:T(8,128)(2,1)}, u32[]{:S(2)}) copy-start(bf16[1,1,256,512]{3,2,1,0:T(8,128)(2,1)} %param.11) | copy-start | bytes 786436
  2.8 27.6 %collective-permute-start.8 = (bf16[2176,256]{1,0:T(8,128)(2,1)S(1)}, bf16[2176,256]{1,0:T(8,128)(2,1)S(1)}, u32[]{:S(2)}, u32[]{:S(2)}) collective-permute-start(bf16[2176,256]{1,0:T(8,128)(2,1)S(1)} %pad_maximum_fusion), channel_id=1, source_target_pairs={{0,8},{8,0},{1,9},{9,1},{2,10},{10,2},{3,11},{11,3},{4,12},{12,4},... | collective-permute-start | bytes 3342344 | tf_op jit(solution)/shard_map/ppermute | solution.py:45
  5.8 24.6 %collective-permute-start.9 = (bf16[256,2048]{1,0:T(8,128)(2,1)S(1)}, bf16[256,2048]{1,0:T(8,128)(2,1)S(1)}, u32[]{:S(2)}, u32[]{:S(2)}) collective-permute-start(bf16[256,2048]{1,0:T(8,128)(2,1)S(1)} %bitcast.19), channel_id=1, source_target_pairs={{0,16},{16,0},{1,17},{17,1},{2,18},{18,2},{3,19},{19,3},{4,20},{20... | collective-permute-start | bytes 3145736 | tf_op jit(solution)/shard_map/ppermute | solution.py:40
  7.6 5.5 %collective-permute-start = (bf16[96,256]{1,0:T(8,128)(2,1)S(1)}, bf16[96,256]{1,0:T(8,128)(2,1)S(1)}, u32[]{:S(2)}, u32[]{:S(2)}) collective-permute-start(bf16[96,256]{1,0:T(8,128)(2,1)S(1)} %get-tuple-element.49.refs_0_), channel_id=1, source_target_pairs={{0,2},{1,3},{2,0},{3,1},{4,6},{5,7},{6,4},{7,5},{8,10},{9,11},{10,... | collective-permute-start | bytes 147464 | tf_op jit(solution)/shard_map/ppermute | solution.py:40
  9.2 5.5 %collective-permute-start.1 = (bf16[96,256]{1,0:T(8,128)(2,1)S(1)}, bf16[96,256]{1,0:T(8,128)(2,1)S(1)}, u32[]{:S(2)}, u32[]{:S(2)}) collective-permute-start(bf16[96,256]{1,0:T(8,128)(2,1)S(1)} %get-tuple-element.45), channel_id=1, source_target_pairs={{0,4},{1,5},{2,6},{3,7},{4,0},{5,1},{6,2},{7,3},{8,12},{9,13},{10,... | collective-permute-start | bytes 147464 | tf_op jit(solution)/shard_map/ppermute | solution.py:40
  11.8 5.9 %collective-permute-start.2 = (bf16[96,256]{1,0:T(8,128)(2,1)S(1)}, bf16[96,256]{1,0:T(8,128)(2,1)S(1)}, u32[]{:S(2)}, u32[]{:S(2)}) collective-permute-start(bf16[96,256]{1,0:T(8,128)(2,1)S(1)} %get-tuple-element.45), channel_id=1, source_target_pairs={{0,6},{1,7},{2,4},{3,5},{4,2},{5,3},{6,0},{7,1},{8,14},{9,15},{10,... | collective-permute-start | bytes 147464 | tf_op jit(solution)/shard_map/ppermute | solution.py:40
  14.7 3.0 %collective-permute-start.3 = (bf16[96,256]{1,0:T(8,128)(2,1)S(1)}, bf16[96,256]{1,0:T(8,128)(2,1)S(1)}, u32[]{:S(2)}, u32[]{:S(2)}) collective-permute-start(bf16[96,256]{1,0:T(8,128)(2,1)S(1)} %get-tuple-element.49.refs_0_), channel_id=1, source_target_pairs={{0,1},{1,0},{2,3},{3,2},{4,5},{5,4},{6,7},{7,6},{8,9},{9,8},{10,11... | collective-permute-start | bytes 147464 | tf_op jit(solution)/shard_map/ppermute | solution.py:40
  14.7 3.5 %collective-permute-start.4 = (bf16[96,256]{1,0:T(8,128)(2,1)S(1)}, bf16[96,256]{1,0:T(8,128)(2,1)S(1)}, u32[]{:S(2)}, u32[]{:S(2)}) collective-permute-start(bf16[96,256]{1,0:T(8,128)(2,1)S(1)} %collective-permute-done.refs_1_), channel_id=1, source_target_pairs={{0,1},{1,0},{2,3},{3,2},{4,5},{5,4},{6,7},{7,6},{8,9},{9,8},{10,11... | collective-permute-start | bytes 147464 | tf_op jit(solution)/shard_map/ppermute | solution.py:40
  17.7 1.2 %collective-permute-start.5 = (bf16[96,256]{1,0:T(8,128)(2,1)S(1)}, bf16[96,256]{1,0:T(8,128)(2,1)S(1)}, u32[]{:S(2)}, u32[]{:S(2)}) collective-permute-start(bf16[96,256]{1,0:T(8,128)(2,1)S(1)} %collective-permute-done.1.refs_2_), channel_id=1, source_target_pairs={{0,1},{1,0},{2,3},{3,2},{4,5},{5,4},{6,7},{7,6},{8,9},{9,8},{10,11... | collective-permute-start | bytes 147464 | tf_op jit(solution)/shard_map/ppermute | solution.py:40
  17.7 1.4 %collective-permute-start.6 = (bf16[96,256]{1,0:T(8,128)(2,1)S(1)}, bf16[96,256]{1,0:T(8,128)(2,1)S(1)}, u32[]{:S(2)}, u32[]{:S(2)}) collective-permute-start(bf16[96,256]{1,0:T(8,128)(2,1)S(1)} %collective-permute-done.2.refs_3_), channel_id=1, source_target_pairs={{0,1},{1,0},{2,3},{3,2},{4,5},{5,4},{6,7},{7,6},{8,9},{9,8},{10,11... | collective-permute-start | bytes 147464 | tf_op jit(solution)/shard_map/ppermute | solution.py:40
  22.6 1.4 %collective-permute-start.7 = (bf16[384,256]{1,0:T(8,128)(2,1)S(1)}, bf16[384,256]{1,0:T(8,128)(2,1)S(1)}, u32[]{:S(2)}, u32[]{:S(2)}) collective-permute-start(bf16[384,256]{1,0:T(8,128)(2,1)S(1)} %get-tuple-element.54), channel_id=1, source_target_pairs={{0,1},{1,0},{2,3},{3,2},{4,5},{5,4},{6,7},{7,6},{8,9},{9,8},{10,11... | collective-permute-start | bytes 589832 | tf_op jit(solution)/shard_map/ppermute | solution.py:40
  24.1 6.4 %collective-permute-start.10 = (bf16[128,256]{1,0:T(8,128)(2,1)S(1)}, bf16[128,256]{1,0:T(8,128)(2,1)S(1)}, u32[]{:S(2)}, u32[]{:S(2)}) collective-permute-start(bf16[128,256]{1,0:T(8,128)(2,1)S(1)} %get-tuple-element.59), channel_id=1, source_target_pairs={{0,2},{1,3},{2,0},{3,1},{4,6},{5,7},{6,4},{7,5},{8,10},{9,11},{10,... | collective-permute-start | bytes 196616 | tf_op jit(solution)/shard_map/ppermute | solution.py:40
  24.2 8.7 %collective-permute-start.11 = (bf16[128,256]{1,0:T(8,128)(2,1)S(1)}, bf16[128,256]{1,0:T(8,128)(2,1)S(1)}, u32[]{:S(2)}, u32[]{:S(2)}) collective-permute-start(bf16[128,256]{1,0:T(8,128)(2,1)S(1)} %get-tuple-element.59), channel_id=1, source_target_pairs={{0,4},{1,5},{2,6},{3,7},{4,0},{5,1},{6,2},{7,3},{8,12},{9,13},{10,... | collective-permute-start | bytes 196616 | tf_op jit(solution)/shard_map/ppermute | solution.py:40
  25.3 7.5 %collective-permute-start.12 = (bf16[128,256]{1,0:T(8,128)(2,1)S(1)}, bf16[128,256]{1,0:T(8,128)(2,1)S(1)}, u32[]{:S(2)}, u32[]{:S(2)}) collective-permute-start(bf16[128,256]{1,0:T(8,128)(2,1)S(1)} %get-tuple-element.59), channel_id=1, source_target_pairs={{0,6},{1,7},{2,4},{3,5},{4,2},{5,3},{6,0},{7,1},{8,14},{9,15},{10,... | collective-permute-start | bytes 196616 | tf_op jit(solution)/shard_map/ppermute | solution.py:40
  32.9 6.0 %collective-permute-start.17 = (bf16[128,512]{1,0:T(8,128)(2,1)S(1)}, bf16[128,512]{1,0:T(8,128)(2,1)S(1)}, u32[]{:S(2)}, u32[]{:S(2)}) collective-permute-start(bf16[128,512]{1,0:T(8,128)(2,1)S(1)} %get-tuple-element.60.refs_2_.own), channel_id=1, source_target_pairs={{0,1},{1,0},{2,3},{3,2},{4,5},{5,4},{6,7},{7,6},{8,9},{9,8},{10,11... | collective-permute-start | bytes 393224 | tf_op jit(solution)/shard_map/ppermute | solution.py:40
  33.0 7.4 %collective-permute-start.15 = (bf16[128,512]{1,0:T(8,128)(2,1)S(1)}, bf16[128,512]{1,0:T(8,128)(2,1)S(1)}, u32[]{:S(2)}, u32[]{:S(2)}) collective-permute-start(bf16[128,512]{1,0:T(8,128)(2,1)S(1)} %get-tuple-element.60.refs_2_.own), channel_id=1, source_target_pairs={{0,8},{8,0},{1,9},{9,1},{2,10},{10,2},{3,11},{11,3},{4,12},{12,4},... | collective-permute-start | bytes 393224 | tf_op jit(solution)/shard_map/ppermute | solution.py:45
  34.1 4.3 %collective-permute-start.18 = (bf16[128,256]{1,0:T(8,128)(2,1)S(1)}, bf16[128,256]{1,0:T(8,128)(2,1)S(1)}, u32[]{:S(2)}, u32[]{:S(2)}) collective-permute-start(bf16[128,256]{1,0:T(8,128)(2,1)S(1)} %get-tuple-element.68), channel_id=1, source_target_pairs={{0,16},{16,0},{1,17},{17,1},{2,18},{18,2},{3,19},{19,3},{4,20},{20... | collective-permute-start | bytes 196616 | tf_op jit(solution)/shard_map/ppermute | solution.py:40
  34.6 4.9 %collective-permute-start.14 = (bf16[64,256]{1,0:T(8,128)(2,1)S(1)}, bf16[64,256]{1,0:T(8,128)(2,1)S(1)}, u32[]{:S(2)}, u32[]{:S(2)}) collective-permute-start(bf16[64,256]{1,0:T(8,128)(2,1)S(1)} %get-tuple-element.63), channel_id=1, source_target_pairs={{0,4},{1,5},{2,6},{3,7},{4,0},{5,1},{6,2},{7,3},{8,12},{9,13},{10,... | collective-permute-start | bytes 98312 | tf_op jit(solution)/shard_map/ppermute | solution.py:40
  36.5 3.9 %collective-permute-start.13 = (bf16[64,256]{1,0:T(8,128)(2,1)S(1)}, bf16[64,256]{1,0:T(8,128)(2,1)S(1)}, u32[]{:S(2)}, u32[]{:S(2)}) collective-permute-start(bf16[64,256]{1,0:T(8,128)(2,1)S(1)} %get-tuple-element.61), channel_id=1, source_target_pairs={{0,2},{1,3},{2,0},{3,1},{4,6},{5,7},{6,4},{7,5},{8,10},{9,11},{10,... | collective-permute-start | bytes 98312 | tf_op jit(solution)/shard_map/ppermute | solution.py:40
  38.3 9.5 %collective-permute-start.22 = (bf16[640,256]{1,0:T(8,128)(2,1)S(1)}, bf16[640,256]{1,0:T(8,128)(2,1)S(1)}, u32[]{:S(2)}, u32[]{:S(2)}) collective-permute-start(bf16[640,256]{1,0:T(8,128)(2,1)S(1)} %slice.31), channel_id=1, source_target_pairs={{0,16},{16,0},{1,17},{17,1},{2,18},{18,2},{3,19},{19,3},{4,20},{20... | collective-permute-start | bytes 983048 | tf_op jit(solution)/shard_map/ppermute | solution.py:40
  40.4 8.4 %collective-permute-start.21 = (bf16[256,640]{1,0:T(8,128)(2,1)S(1)}, bf16[256,640]{1,0:T(8,128)(2,1)S(1)}, u32[]{:S(2)}, u32[]{:S(2)}) collective-permute-start(bf16[256,640]{1,0:T(8,128)(2,1)S(1)} %shard_map.161), channel_id=1, source_target_pairs={{0,8},{8,0},{1,9},{9,1},{2,10},{10,2},{3,11},{11,3},{4,12},{12,4},... | collective-permute-start | bytes 983048 | tf_op jit(solution)/shard_map/ppermute | solution.py:45
  41.0 6.9 %collective-permute-start.20 = (bf16[128,512]{1,0:T(8,128)(2,1)S(1)}, bf16[128,512]{1,0:T(8,128)(2,1)S(1)}, u32[]{:S(2)}, u32[]{:S(2)}) collective-permute-start(bf16[128,512]{1,0:T(8,128)(2,1)S(1)} %collective-permute-done.15.own), channel_id=1, source_target_pairs={{0,1},{1,0},{2,3},{3,2},{4,5},{5,4},{6,7},{7,6},{8,9},{9,8},{10,11... | collective-permute-start | bytes 393224 | tf_op jit(solution)/shard_map/ppermute | solution.py:40
  41.0 3.0 %collective-permute-start.19 = (bf16[128,256]{1,0:T(8,128)(2,1)S(1)}, bf16[128,256]{1,0:T(8,128)(2,1)S(1)}, u32[]{:S(2)}, u32[]{:S(2)}) collective-permute-start(bf16[128,256]{1,0:T(8,128)(2,1)S(1)} %collective-permute-done.18.refs_4_), channel_id=1, source_target_pairs={{0,1},{1,0},{2,3},{3,2},{4,5},{5,4},{6,7},{7,6},{8,9},{9,8},{10,11... | collective-permute-start | bytes 196616 | tf_op jit(solution)/shard_map/ppermute | solution.py:40
  41.5 5.7 %collective-permute-start.16 = (bf16[64,256]{1,0:T(8,128)(2,1)S(1)}, bf16[64,256]{1,0:T(8,128)(2,1)S(1)}, u32[]{:S(2)}, u32[]{:S(2)}) collective-permute-start(bf16[64,256]{1,0:T(8,128)(2,1)S(1)} %get-tuple-element.65), channel_id=1, source_target_pairs={{0,6},{1,7},{2,4},{3,5},{4,2},{5,3},{6,0},{7,1},{8,14},{9,15},{10,... | collective-permute-start | bytes 98312 | tf_op jit(solution)/shard_map/ppermute | solution.py:40
  (9 other events, 51.8 us)
